TPU v7x, 32 devices: a whole 2x2x4 slice. The times are simulated.
32 devices in a mesh: dp: 4 (over y, x), fsdp: 8 (over z, core).
Axes of the slice: x: 2, y: 2, z: 4, core: 2. Of those that a mesh axis runs over, the one named last changes fastest.
Arguments:
- features: bfloat16 [4096, 640], P(('dp', 'fsdp')), may hold values from -6 to 6
- heights: int32 [32, 4], P(('dp', 'fsdp')), may hold values from 0 to 32, as said below
- widths: int32 [32, 4], P(('dp', 'fsdp')), may hold values from 0 to 32, as said below
- timesteps: int32 [32, 4], P(('dp', 'fsdp')), may hold values from 0 to 999
- norm_gain: float32 [640], replicated, may hold values from 0.1 to 1.9
- norm_shift: float32 [640], replicated, may hold values from -3 to 3
- conv_weight: bfloat16 [768, 5760], P('fsdp'), may hold values from -0.078125 to 0.078125
- time_weight: bfloat16 [768, 320], P('fsdp'), may hold values from -0.3125 to 0.3125
- cotangent: bfloat16 [4096, 768], P(('dp', 'fsdp')), may hold values from -6 to 6
Outputs:
- block_out: bfloat16 [4096, 768], P(('dp', 'fsdp'))
- grad_features: bfloat16 [4096, 640], P(('dp', 'fsdp'))
- grad_conv: float32 [768, 5760], P('fsdp')
- grad_time: float32 [768, 320], P('fsdp')
- grad_gain: float32 [640], replicated
- grad_shift: float32 [640], replicated
Inputs may be any that keep to these rules, and one draw needn't show every extreme that they name: In each block the live pixels heights * widths sum to at most 128, and in some block to exactly 128; every block has one or more images, slot after slot; an empty slot has height and width 0; sides are powers of two. `widths`: as for heights; a live image has width 2 or more.
All inputs are finite; a program needn't handle non-finite values.
Results may differ from a plain program's by a relative error of at most 0.0045.
Values may be sent and summed in bfloat16 or wider, within the bound.
No kernel may reach another device: no remote copies, remote signals or barrier semaphores. Data moves between devices by JAX's collectives and lax.ppermute only.
A program may use at most 128 MiB of HBM per device.

v0:
```python
import math

import jax
import jax.numpy as jnp
from jax import lax
from jax.sharding import PartitionSpec as P

CO = 768
GROUPS = 32


highest = lax.Precision.HIGHEST


def layout(heights_row, widths_row, rows):
    images = heights_row.shape[0]
    area = heights_row * widths_row
    ends = jnp.cumsum(area)
    starts = ends - area
    position = jnp.arange(rows, dtype=jnp.int32)
    image = jnp.sum((position[:, None] >= ends[None, :]).astype(jnp.int32), axis=1)
    live = position < ends[images - 1]
    member = (image[:, None] == jnp.arange(images, dtype=jnp.int32)[None, :]) & live[:, None]
    first = jnp.sum(jnp.where(member, starts[None, :], 0), axis=1)
    height = jnp.sum(jnp.where(member, heights_row[None, :], 0), axis=1)
    width = jnp.sum(jnp.where(member, widths_row[None, :], 0), axis=1)
    offset = position - first
    width_safe = jnp.maximum(width, 1)
    row_index = offset // width_safe
    column = offset - row_index * width_safe
    targets = []
    for shift_row in (-1, 0, 1):
        for shift_col in (-1, 0, 1):
            near_row = row_index + shift_row
            near_col = column + shift_col
            valid = (
                live & (near_row >= 0) & (near_row < height) & (near_col >= 0) & (near_col < width)
            )
            targets.append(jnp.where(valid, first + near_row * width + near_col, rows))
    neighbours = jnp.stack(targets, axis=1)
    return (neighbours, live, member.astype(jnp.float32))


def timestep_features(times_row, feature_count):
    half = feature_count // 2
    rates = jnp.exp(-math.log(10000.0) * jnp.arange(half, dtype=jnp.float32) / half)
    angles = times_row.astype(jnp.float32)[:, None] * rates[None, :]
    return jnp.concatenate([jnp.sin(angles), jnp.cos(angles)], axis=1).astype(jnp.bfloat16)


def group_mean(values, member, counts):
    sums = jnp.dot(member.T, values, precision=highest)
    images, channels = sums.shape
    grouped = jnp.sum(sums.reshape(images, GROUPS, channels // GROUPS), axis=2) / counts[:, None]
    spread = jnp.repeat(grouped, channels // GROUPS, axis=1)
    return jnp.dot(member, spread, precision=highest)


def shards(
    features, heights, widths, timesteps, norm_gain, norm_shift, conv_weight, time_weight, cotangent
):
    rows, channels = features.shape
    replicas = lax.axis_size("dp")
    holders = lax.axis_size("fsdp")
    scale = 1.0 / math.sqrt(replicas * holders * rows)
    feature_count = time_weight.shape[1]
    heights_row = heights[0]
    widths_row = widths[0]
    neighbours, live, member = layout(heights_row, widths_row, rows)
    counts = jnp.maximum((heights_row * widths_row).astype(jnp.float32) * (channels // GROUPS), 1.0)
    values = features.astype(jnp.float32)
    mean = group_mean(values, member, counts)
    centered = values - mean
    variance = group_mean(centered * centered, member, counts)
    inverse_std = lax.rsqrt(variance + 1e-05) * live[:, None].astype(jnp.float32)
    normed = centered * inverse_std
    shifted = normed * norm_gain[None, :] + norm_shift[None, :]
    activated = (shifted * jax.nn.sigmoid(shifted)).astype(jnp.bfloat16)
    padded = jnp.concatenate([activated, jnp.zeros((1, channels), jnp.bfloat16)], axis=0)
    patches = padded[neighbours].reshape(rows, 9 * channels)
    cotan_live = jnp.where(live[:, None], cotangent, jnp.zeros_like(cotangent))
    cotan_padded = jnp.concatenate([cotan_live, jnp.zeros((1, CO), jnp.bfloat16)], axis=0)
    embed = timestep_features(timesteps[0], feature_count)
    conv_full, time_full = (
        lax.all_gather(conv_weight, "fsdp", axis=0, tiled=True),
        lax.all_gather(time_weight, "fsdp", axis=0, tiled=True),
    )
    bias_image = lax.dot_general(
        embed, time_full, (((1,), (1,)), ((), ())), preferred_element_type=jnp.float32
    )
    before = lax.dot_general(
        patches, conv_full, (((1,), (1,)), ((), ())), preferred_element_type=jnp.float32
    )
    before = before + jnp.dot(member, bias_image, precision=highest)
    block_out = jnp.where(live[:, None], before, 0.0).astype(jnp.bfloat16)
    reversed_taps = neighbours[:, ::-1]
    cotan_taps = cotan_padded[reversed_taps].reshape(rows, 9 * CO)
    tap_weight = conv_full.reshape(CO, 9, channels).transpose(1, 0, 2).reshape(9 * CO, channels)
    grad_act = jnp.dot(cotan_taps, tap_weight, preferred_element_type=jnp.float32)
    sigmoid_value = jax.nn.sigmoid(shifted)
    grad_shifted = grad_act * sigmoid_value * (1.0 + shifted * (1.0 - sigmoid_value))
    gain_term = jnp.sum(grad_shifted * normed, axis=0) * scale
    shift_term = jnp.sum(grad_shifted, axis=0) * scale
    grad_normed = grad_shifted * norm_gain[None, :]
    mean_grad = group_mean(grad_normed, member, counts)
    mean_cross = group_mean(grad_normed * normed, member, counts)
    grad_features = (inverse_std * (grad_normed - mean_grad - normed * mean_cross)).astype(
        jnp.bfloat16
    )
    per_image = jnp.dot(member.T, cotan_live.astype(jnp.float32), precision=highest)
    conv_part = lax.dot_general(
        cotan_live, patches, (((0,), (0,)), ((), ())), preferred_element_type=jnp.float32
    )
    time_part = lax.dot_general(
        per_image, embed.astype(jnp.float32), (((0,), (0,)), ((), ())), precision=highest
    )
    full_term = jnp.concatenate([conv_part, time_part], axis=1) * scale
    reduced = lax.psum_scatter(full_term, "fsdp", scatter_dimension=0, tiled=True)
    joined = lax.psum(reduced, "dp")
    grad_conv = joined[:, : 9 * channels]
    grad_time = joined[:, 9 * channels :]
    grad_gain, grad_shift = lax.psum((gain_term, shift_term), ("dp", "fsdp"))
    return (block_out, grad_features, grad_conv, grad_time, grad_gain, grad_shift)


def solution(mesh):
    placed = (
        P(("dp", "fsdp"), None),
        P(("dp", "fsdp"), None),
        P(("dp", "fsdp"), None),
        P(("dp", "fsdp"), None),
        P(),
        P(),
        P("fsdp", None),
        P("fsdp", None),
        P(("dp", "fsdp"), None),
    )
    return jax.shard_map(
        shards,
        mesh=mesh,
        in_specs=placed,
        out_specs=(
            P(("dp", "fsdp"), None),
            P(("dp", "fsdp"), None),
            P("fsdp", None),
            P("fsdp", None),
            P(),
            P(),
        ),
        check_vma=False,
    )
```

profile of v0, /device:TPU:0, one launch (start us, length us, event | category | flops | bytes accessed | tf_op | source)
XLA Modules:
  0.0 379.3 jit_solution(7207101345524111477)
XLA Ops:
  7.2 0.7 all-gather.2.cloned.1.call-update
  8.0 0.7 mul.425
  8.6 0.2 reduce-window.4
  8.8 0.6 slice.10
  9.4 0.6 iota_compare_fusion.3
  10.2 0.8 select_reduce_fusion.2
  10.9 0.8 constant_dynamic-update-slice_fusion.8
  11.7 0.1 constant_dynamic-update-slice_fusion.7
  11.8 0.1 constant_dynamic-update-slice_fusion.6
  12.0 0.8 constant_dynamic-update-slice_fusion.5
  12.8 0.1 constant_dynamic-update-slice_fusion.4
  12.9 0.1 constant_dynamic-update-slice_fusion.3
  13.0 0.8 constant_dynamic-update-slice_fusion.2
  13.8 0.1 constant_dynamic-update-slice_fusion.1
  14.0 0.1 constant_dynamic-update-slice_fusion
  14.2 1.1 fusion.48
  15.5 0.2 reshape.1036
  15.8 0.2 reshape.1028
  16.1 0.7 multiply_maximum_fusion
  17.1 1.3 convolution_subtract_fusion.1
  18.3 0.2 fusion.27
  19.1 0.7 fusion.45
  19.8 1.3 multiply_convert_fusion
  21.1 4.5 %gather_fusion = bf16[1152,640]{1,0:T(8,128)(2,1)S(1)} fusion(bf16[129,640]{1,0:T(8,128)(2,1)S(1)} %concatenate.32, s32[2048]{0:T(1024)S(1)} %get-tuple-element.44), kind=kCustom, calls=%fused_computation | custom fusion | bytes 2953728 | tf_op jit(solution)/shard_map/gather | solution.py:80
  25.6 1.7 reshape.1020
  27.6 0.1 fusion.51
  27.8 0.9 fusion.41
  28.6 2.5 fusion.50
  31.1 7.3 %maximum_multiply_fusion = f32[768,6080]{1,0:T(8,128)} fusion(f32[768,320]{1,0:T(8,128)S(1)} %fusion.41, f32[768,5760]{1,0:T(8,128)S(1)} %fusion.50), kind=kLoop, calls=%fused_computation.2 | loop fusion | flops 9338880 | bytes 37355520 | tf_op jit(solution)/shard_map/mul | solution.py:117
  38.5 4.6 %gather_fusion.1 = bf16[1152,768]{1,0:T(8,128)(2,1)S(1)} fusion(bf16[129,768]{1,0:T(8,128)(2,1)S(1)} %concatenate.34, s32[2048]{0:T(1024)S(1)} %get-tuple-element.43), kind=kCustom, calls=%fused_computation.1 | custom fusion | bytes 3543552 | tf_op jit(solution)/shard_map/gather | solution.py:97
  43.1 2.4 reshape.1035
  45.6 21.4 %all_gather.7 = bf16[768,320]{1,0:T(8,128)(2,1)S(1)} all-gather(bf16[96,320]{1,0:T(8,128)(2,1)S(1)} %copy-done.3), channel_id=1, replica_groups=mesh['dp'=4,'fsdp'=8] {'fsdp'}, dimensions={0}, use_global_device_ids=true | all-gather | bytes 552960 | tf_op jit(solution)/shard_map/all_gather | solution.py:86
  67.0 0.3 fusion.42
  67.3 35.6 %all-gather.2.cloned.1.call-done = bf16[768,5760]{1,0:T(8,128)(2,1)} async-done(((bf16[96,5760]{1,0:T(8,128)(2,1)}), bf16[768,5760]{1,0:T(8,128)(2,1)}) %all-gather.2.cloned.1.call-update) | async-done | bytes 8847376 | tf_op jit(solution)/shard_map/all_gather | solution.py:85
  102.9 12.1 %copy.31 = bf16[768,5760]{0,1:T(8,128)(2,1)} copy(bf16[768,5760]{1,0:T(8,128)(2,1)} %all-gather.2.cloned.1.call-done) | data formatting | bytes 17694720 | tf_op jit(solution)/shard_map/all_gather | solution.py:85
  115.0 13.4 %copy.32 = bf16[768,9,640]{2,0,1:T(8,128)(2,1)} copy(bf16[768,9,640]{0,2,1:T(8,128)(2,1)} %bitcast.252) | data formatting | bytes 17694720 | tf_op jit(solution)/shard_map/reshape | solution.py:98
  128.4 6.7 %fusion.46 = (f32[640]{0:T(1024)S(1)}, f32[640]{0:T(1024)S(1)}, f32[128,640]{1,0:T(8,128)S(1)}) fusion(f32[128,640]{1,0:T(8,128)S(1)} %copy-done, f32[640]{0:T(1024)S(1)} %copy-done.5, f32[640]{0:T(1024)S(1)} %copy-done.4, bf16[768,9,640]{2,0,1:T(8,128)(2,1)} %copy.32, bf16[128,9,768]{2,1,0:T(8,128)(2,1)} %reshape.1035), kind=kOutput, calls=%fused_computation.108 | convolution fusion | flops 1133525760 | bytes 11282432 | tf_op jit(solution)/shard_map/dot_general | solution.py:99
  135.0 156.7 %reduce-scatter.2.cloned.1.call-done = f32[96,6080]{1,0:T(8,128)} async-done(((f32[768,6080]{1,0:T(8,128)}), f32[96,6080]{1,0:T(8,128)}) %reduce-scatter.2.cloned.1.call-update) | async-done | bytes 2334736 | tf_op jit(solution)/shard_map/reduce_scatter | solution.py:118
  291.8 0.2 fusion.30
  292.3 0.3 fusion.25
  293.3 38.2 %all-reduce.2 = (f32[640]{0:T(1024)}, f32[640]{0:T(1024)}) all-reduce(f32[640]{0:T(1024)S(1)} %broadcast_multiply_fusion.1, f32[640]{0:T(1024)S(1)} %broadcast_multiply_fusion), channel_id=1, replica_groups=mesh['dp'=4,'fsdp'=8] {'dp','fsdp'}, use_global_device_ids=true, to_apply=%region_12.13 | all-reduce | flops 1280 | bytes 10240 | tf_op jit(solution)/shard_map/psum | solution.py:122
  331.5 6.1 %fusion.49 = f32[128,768]{1,0:T(8,128)S(1)} fusion(bf16[128,5760]{1,0:T(8,128)(2,1)S(1)} %reshape.1020, bf16[768,5760]{1,0:T(8,128)(2,1)} %all-gather.2.cloned.1.call-done), kind=kOutput, calls=%fused_computation.110 | convolution fusion | flops 1132462080 | bytes 10715136 | tf_op jit(solution)/shard_map/dot_general | solution.py:91
  337.6 1.1 fusion.13
  338.7 0.4 convolution_multiply_fusion
  339.1 1.1 fusion.24
  340.1 28.0 %all-reduce.5.cloned.1.call-done = f32[96,6080]{1,0:T(8,128)} async-done(((f32[96,6080]{1,0:T(8,128)}), f32[96,6080]{1,0:T(8,128)}) %all-reduce.5.cloned.1.call-update) | async-done | bytes 2334736 | tf_op jit(solution)/shard_map/psum | solution.py:119
  368.1 1.6 slice.18
  369.7 3.1 slice.17
  (55 shorter events, 2.7 us)
Async XLA Ops:
  7.2 12.6 %copy-start.4 = (f32[640]{0:T(1024)S(1)}, f32[640]{0:T(1024)}, u32[]{:S(2)}) copy-start(f32[640]{0:T(1024)} %param.13) | copy-start | bytes 7684
  7.2 12.6 %copy-start.5 = (f32[640]{0:T(1024)S(1)}, f32[640]{0:T(1024)}, u32[]{:S(2)}) copy-start(f32[640]{0:T(1024)} %param.14) | copy-start | bytes 7684
  7.2 95.7 %all-gather.2.cloned.1.call-start = ((), (), s32[]{:S(2)}) async-start(), calls=%async_computation.1 | async-start | bytes 9953280 | tf_op jit(solution)/shard_map/all_gather | solution.py:85
  7.9 283.9 %reduce-scatter.2.cloned.1.call-start = ((), (), s32[]{:S(2)}) async-start(), calls=%async_computation.2 | async-start | bytes 21233664 | tf_op jit(solution)/shard_map/reduce_scatter | solution.py:118
  21.1 6.3 %copy-start.6 = (s32[1,4]{1,0:T(1,128)S(1)}, s32[1,4]{1,0:T(1,128)}, u32[]{:S(2)}) copy-start(s32[1,4]{1,0:T(1,128)} %param.12) | copy-start | bytes 52
  21.1 6.4 %copy-start.2 = (bf16[128,768]{1,0:T(8,128)(2,1)S(1)}, bf16[128,768]{1,0:T(8,128)(2,1)}, u32[]{:S(2)}) copy-start(bf16[128,768]{1,0:T(8,128)(2,1)} %param.17) | copy-start | bytes 589828
  38.5 329.6 %all-reduce.5.cloned.1.call-start = ((), (), s32[]{:S(2)}) async-start(), calls=%async_computation.3 | async-start | bytes 4718592 | tf_op jit(solution)/shard_map/psum | solution.py:119
  43.1 2.5 copy-start.3
  115.0 13.4 %copy-start = (f32[128,640]{1,0:T(8,128)S(1)}, f32[128,640]{1,0:T(8,128)}, u32[]{:S(2)}) copy-start(f32[128,640]{1,0:T(8,128)} %get-tuple-element.36) | copy-start | bytes 983044
  331.5 7.6 %copy-start.1 = (f32[128,640]{1,0:T(8,128)S(1)}, f32[128,640]{1,0:T(8,128)}, u32[]{:S(2)}) copy-start(f32[128,640]{1,0:T(8,128)} %get-tuple-element.41) | copy-start | bytes 983044
Sparse Core Ops, SparseCore 0:
  9.7 93.2 all-gather.1
  105.3 186.4 reduce-scatter.1
  294.9 73.1 all-reduce.4
where the time goes:
time: 380 us; the launch traced here: 379 us
  waiting for transfers between devices  221 us (58%)
  blocking collectives  59.7 us (16%)
  local copies, waits for them, and re-layouts  46 us (12%)
  matrix products  23.4 us (6%)
  other arithmetic  15 us (4%)
  between operations  14.1 us (4%)
    reduce_scatter x1, waiting for transfers between devices, shards(): lax.psum_scatter(full_term, 'fsdp', scatter_dimension=0, tiled=True)  157 us
    psum x1, blocking collectives, shards(): grad_gain, grad_shift = lax.psum((gain_term, shift_term), ('dp', 'fsdp'))  38.2 us
    all_gather x1, waiting for transfers between devices, shards(): lax.all_gather(conv_weight, 'fsdp', axis=0, tiled=True)  35.6 us
    psum x1, waiting for transfers between devices, shards(): joined = lax.psum(reduced, 'dp')  28 us
    all_gather x1, blocking collectives, shards(): lax.all_gather(time_weight, 'fsdp', axis=0, tiled=True)  21.4 us
    reshape x1, local copies, waits for them, and re-layouts, shards(): conv_full.reshape(CO, 9, channels).transpose(1, 0, 2)  13.4 us
    all_gather x1, local copies, waits for them, and re-layouts, shards(): lax.all_gather(conv_weight, 'fsdp', axis=0, tiled=True)  12.1 us
  transfers between devices with their start and end apart: 3, of which 3 were waited for; matrix products, arithmetic and copies ran while one was open for 21% of the time, Pallas kernels for 0%

commit v1 on v0

v1 whole, which is shorter than its diff:
```python
import functools
import math

import jax
import jax.numpy as jnp
from jax import lax
from jax.experimental import pallas as pl
from jax.experimental.pallas import tpu as pltpu
from jax.sharding import PartitionSpec as P

GROUPS = 32
IMAGES = 4
LANES = 128
VMEM_BYTES = 56 * 1024 * 1024

bf16 = jnp.bfloat16
f32 = jnp.float32


def dot(a, b, dims=((1,), (0,))):
    return lax.dot_general(a, b, (dims, ((), ())), preferred_element_type=f32)


def split3(x):
    hi = x.astype(bf16)
    rest = x - hi.astype(f32)
    mid = rest.astype(bf16)
    low = (rest - mid.astype(f32)).astype(bf16)
    return hi, mid, low


def exact_dot(x, ones):
    rows = x.shape[0]
    out = dot(jnp.concatenate(split3(x), axis=0), ones)
    return out[:rows] + out[rows : 2 * rows] + out[2 * rows :]


def image_bounds(meta_ref, source):
    start = jnp.int32(0)
    found = []
    for j in range(IMAGES):
        height = meta_ref[source, j]
        width = meta_ref[source, IMAGES + j]
        area = height * width
        found.append((start, start + area, width, area))
        start = start + area
    return found


def inverse_area(area):
    return 1.0 / jnp.maximum(area, 1).astype(f32)


def masks(bounds, shape):
    row = lax.broadcasted_iota(jnp.int32, shape, 0)
    return [(row >= start) & (row < end) for start, end, _, _ in bounds]


def spread(members, table, shape):
    out = jnp.zeros(shape, f32)
    for j in range(IMAGES):
        out = jnp.where(members[j], table[j : j + 1, :], out)
    return out


def image_sums(members, values, bounds):
    sums = []
    for j in range(IMAGES):
        total = jnp.sum(jnp.where(members[j], values, 0.0), axis=0, keepdims=True)
        sums.append(total * inverse_area(bounds[j][3]))
    return jnp.concatenate(sums, axis=0)


def tap_matrices(bounds, rows):
    shape = (rows, rows)
    row = lax.broadcasted_iota(jnp.int32, shape, 0)
    gap = lax.broadcasted_iota(jnp.int32, shape, 1) - row
    width = jnp.zeros(shape, jnp.int32)
    area = jnp.zeros(shape, jnp.int32)
    first = jnp.zeros(shape, jnp.int32)
    for start, end, wide, size in bounds:
        member = (row >= start) & (row < end)
        width = jnp.where(member, wide, width)
        area = jnp.where(member, size, area)
        first = jnp.where(member, start, first)
    offset = row - first
    column = offset & (width - 1)
    columns = {-1: column >= 1, 0: column >= 0, 1: column + 1 < width}
    taps = []
    for shift_row in (-1, 0, 1):
        moved = offset + shift_row * width
        inside = (moved >= 0) & (moved < area)
        left = gap - shift_row * width
        for shift_col in (-1, 0, 1):
            hit = inside & columns[shift_col] & (left == shift_col)
            taps.append(jnp.where(hit, 1.0, 0.0).astype(bf16))
    return taps


def weight_grad_kernel(
    count,
    low_taps,
    source_ref,
    meta_ref,
    *refs,
):
    features = refs[:count]
    (
        cotan_ref,
        embed_ref,
        same_ref,
        gain_ref,
        shift_ref,
        low_ref,
        high_ref,
        act_ref,
        normed_ref,
        rstd_ref,
        taps_ref,
        stats,
        sums,
        turned,
    ) = refs[count:]
    rows, channels = features[0].shape
    owned = cotan_ref.shape[2]
    padded = turned.shape[0] // 9
    group_size = channels // GROUPS
    same = same_ref[...]
    for b in range(count):
        bounds = image_bounds(meta_ref, source_ref[b])
        members = masks(bounds, (rows, channels))
        stats[b * IMAGES : (b + 1) * IMAGES, :] = image_sums(
            members, features[b][...].astype(f32), bounds
        )
    means = exact_dot(stats[...], same) * (1.0 / group_size)
    for b in range(count):
        bounds = image_bounds(meta_ref, source_ref[b])
        members = masks(bounds, (rows, channels))
        mean = spread(members, means[b * IMAGES : (b + 1) * IMAGES], (rows, channels))
        centered = features[b][...].astype(f32) - mean
        normed_ref[b] = centered
        stats[b * IMAGES : (b + 1) * IMAGES, :] = image_sums(members, centered * centered, bounds)
    variance = exact_dot(stats[...], same) * (1.0 / group_size)
    rstds = lax.rsqrt(variance + 1e-05)
    gain = gain_ref[...]
    shift = shift_ref[...]
    for b in range(count):
        source = source_ref[b]
        bounds = image_bounds(meta_ref, source)
        members = masks(bounds, (rows, channels))
        rstd = spread(members, rstds[b * IMAGES : (b + 1) * IMAGES], (rows, channels))
        if b == 0:
            rstd_ref[...] = rstd
        normed = normed_ref[b] * rstd
        normed_ref[b] = normed
        shifted = normed * gain + shift
        act_ref[b * rows : (b + 1) * rows, :] = (shifted * jax.nn.sigmoid(shifted)).astype(bf16)

        taps = jnp.concatenate(tap_matrices(bounds, rows), axis=1)
        taps_ref[b] = taps
        cotan = cotan_ref[source, :rows, :]
        wide = cotan.astype(f32)
        if owned < LANES:
            wide = jnp.concatenate([wide, jnp.zeros((rows, LANES - owned), f32)], axis=1)
        moved = dot(wide.T.astype(bf16), taps).astype(bf16)
        for t in range(9):
            turned[t * padded : (t + 1) * padded, b * rows : (b + 1) * rows] = moved[
                :padded, t * rows : (t + 1) * rows
            ]
        image = lax.broadcasted_iota(jnp.int32, (2 * IMAGES, rows), 0)
        place = lax.broadcasted_iota(jnp.int32, (2 * IMAGES, rows), 1)
        member = jnp.zeros((2 * IMAGES, rows), f32)
        for j in range(IMAGES):
            start, end, _, _ = bounds[j]
            member = jnp.where((image == j) & (place >= start) & (place < end), 1.0, member)
        sums[source] = dot(member.astype(bf16), cotan)
    grad = dot(turned[...], act_ref[...])
    for t in range(9):
        part = grad[t * padded : t * padded + owned].astype(bf16)
        if t < low_taps:
            low_ref[:, t * channels : (t + 1) * channels] = part
        else:
            high_ref[:, (t - low_taps) * channels : (t - low_taps + 1) * channels] = part
    totals = jnp.concatenate([sums[s] for s in range(count)], axis=0)
    embed = embed_ref[...]
    time_grad = jnp.zeros((owned, embed.shape[1]), f32)
    for term in split3(totals):
        time_grad = time_grad + dot(term, embed, ((0,), (0,)))
    spare = low_ref.shape[1] - low_taps * channels - embed.shape[1]
    low_ref[:, low_taps * channels :] = jnp.concatenate(
        [time_grad, jnp.zeros((owned, spare), f32)], axis=1
    ).astype(bf16)


def conv_kernel(
    count,
    source_ref,
    meta_ref,
    act_ref,
    normed_ref,
    taps_ref,
    cotan_ref,
    embed_ref,
    conv_ref,
    time_ref,
    gain_ref,
    shift_ref,
    out_ref,
    own_ref,
    other_ref,
    terms_ref,
    weights,
    biases,
    moved,
    product,
):
    _, rows, channels = normed_ref.shape
    owned = cotan_ref.shape[2]
    weights[...] = jnp.zeros_like(weights)
    for t in range(9):
        weights[t * LANES : t * LANES + owned, :] = conv_ref[:, t * channels : (t + 1) * channels]
    bias = dot(embed_ref[...], time_ref[...], ((1,), (1,)))
    for s in range(count):
        biases[s] = bias[s * 2 * IMAGES : (s + 1) * 2 * IMAGES]
    gain = gain_ref[...]
    shift = shift_ref[...]
    gain_term = jnp.zeros((1, channels), f32)
    shift_term = jnp.zeros((1, channels), f32)
    for b in range(count):
        taps = taps_ref[b]
        stacked = jnp.concatenate([taps[:, (8 - t) * rows : (9 - t) * rows] for t in range(9)], axis=0)
        cotan = cotan_ref[source_ref[b], :rows, :]
        if owned < LANES:
            cotan = jnp.concatenate([cotan, jnp.zeros((rows, LANES - owned), bf16)], axis=1)
        shifted_cotan = dot(stacked, cotan).astype(bf16)
        for t in range(9):
            moved[b * rows : (b + 1) * rows, t * LANES : (t + 1) * LANES] = shifted_cotan[
                t * rows : (t + 1) * rows
            ]
    for pair in range(count // 2):
        grad_act = dot(moved[2 * pair * rows : 2 * (pair + 1) * rows, :], weights[...])
        own_ref[pair] = grad_act[:rows].astype(bf16)
        other_ref[pair] = grad_act[rows:].astype(bf16)
        normed = normed_ref[2 * pair : 2 * pair + 2].reshape(2 * rows, channels)
        shifted = normed * gain + shift
        sig = jax.nn.sigmoid(shifted)
        slope = grad_act * (sig * (1.0 + shifted * (1.0 - sig)))
        gain_term = gain_term + jnp.sum(slope * normed, axis=0, keepdims=True)
        shift_term = shift_term + jnp.sum(slope, axis=0, keepdims=True)
        product[...] = dot(
            act_ref[2 * pair * rows : 2 * (pair + 1) * rows, :], weights[...], ((1,), (1,))
        )
        for half in range(2):
            b = 2 * pair + half
            source = source_ref[b]
            values = product[half * rows : (half + 1) * rows, :]
            high = values.astype(bf16)
            low = (values - high.astype(f32)).astype(bf16)
            tiles = [high[:, t * LANES : (t + 1) * LANES] for t in range(9)]
            tiles += [low[:, t * LANES : (t + 1) * LANES] for t in range(9)]
            taps = taps_ref[b]
            total = dot(
                jnp.concatenate([taps, taps], axis=1), jnp.concatenate(tiles, axis=0)
            )[:, :owned]
            bounds = image_bounds(meta_ref, source)
            members = masks(bounds, (rows, owned))
            total = total + spread(members, biases[source], (rows, owned))
            out_ref[source] = total.astype(bf16)
    terms_ref[...] = jnp.concatenate(
        [gain_term, shift_term, jnp.zeros((6, channels), f32)], axis=0
    )


def norm_grad_kernel(
    source_ref, meta_ref, grad_ref, normed_ref, rstd_ref, same_ref, gain_ref, shift_ref, out_ref
):
    rows, channels = grad_ref.shape
    group_size = channels // GROUPS
    normed = normed_ref[0]
    gain = gain_ref[...]
    shifted = normed * gain + shift_ref[...]
    sig = jax.nn.sigmoid(shifted)
    grad = grad_ref[...] * (sig * (1.0 + shifted * (1.0 - sig))) * gain
    bounds = image_bounds(meta_ref, source_ref[0])
    members = masks(bounds, (rows, channels))
    sums = jnp.concatenate(
        [image_sums(members, grad, bounds), image_sums(members, grad * normed, bounds)], axis=0
    )
    means = exact_dot(sums, same_ref[...]) * (1.0 / group_size)
    mean_grad = spread(members, means[:IMAGES], (rows, channels))
    mean_cross = spread(members, means[IMAGES:], (rows, channels))
    out_ref[...] = (rstd_ref[...] * (grad - mean_grad - normed * mean_cross)).astype(bf16)


def call(kernel, outs, scratch, flops, *args):
    smem = pl.BlockSpec(memory_space=pltpu.SMEM)
    vmem = pl.BlockSpec(memory_space=pltpu.VMEM)
    return pl.pallas_call(
        kernel,
        out_shape=outs,
        in_specs=[smem, smem] + [vmem] * (len(args) - 2),
        out_specs=jax.tree.map(lambda _: vmem, outs),
        scratch_shapes=scratch,
        compiler_params=pltpu.CompilerParams(vmem_limit_bytes=VMEM_BYTES),
        cost_estimate=pl.CostEstimate(flops=flops, bytes_accessed=8 << 20, transcendentals=0),
    )(*args)


def exchange(value, axis, bit):
    size = lax.axis_size(axis)
    return lax.ppermute(value, axis, [(i, i ^ bit) for i in range(size)])


def timestep_features(times, feature_count):
    half = feature_count // 2
    rates = jnp.exp(-math.log(10000.0) * jnp.arange(half, dtype=f32) / half)
    angles = times.astype(f32)[..., None] * rates
    return jnp.concatenate([jnp.sin(angles), jnp.cos(angles)], axis=-1).astype(bf16)


def shards(
    features, heights, widths, timesteps, norm_gain, norm_shift, conv_weight, time_weight, cotangent
):
    rows, channels = features.shape
    replicas = lax.axis_size("dp")
    holders = lax.axis_size("fsdp")
    chips = holders // 2
    owned = conv_weight.shape[0]
    out_channels = cotangent.shape[1]
    feature_count = time_weight.shape[1]
    scale = 1.0 / math.sqrt(replicas * holders * rows)
    me = lax.axis_index("fsdp")

    near = [features] + [exchange(features, "fsdp", 2 * k) for k in range(1, chips)]
    far = [exchange(block, "fsdp", 1) for block in near]
    blocks = [block for pair in zip(near, far) for block in pair]
    source = jnp.stack([me ^ b for b in range(holders)]).astype(jnp.int32)

    times = timesteps[0]
    facts = jnp.concatenate([heights[0], widths[0], times >> 5, times & 31]).astype(bf16)
    facts = jnp.tile(jnp.pad(facts, (0, owned - facts.shape[0])), holders)
    extra = jnp.pad(facts[None, :], ((0, 15), (0, 0)))
    cotan = lax.all_to_all(
        jnp.concatenate([cotangent, extra], axis=0).reshape(rows + 16, holders, owned),
        "fsdp",
        1,
        0,
    )
    facts = cotan[:, rows, : 4 * IMAGES].astype(jnp.int32)
    meta = facts[:, : 2 * IMAGES]
    times = facts[:, 2 * IMAGES : 3 * IMAGES] * 32 + facts[:, 3 * IMAGES :]
    embed = timestep_features(times, feature_count)
    embed = jnp.pad(embed, ((0, 0), (0, IMAGES), (0, 0))).reshape(holders * 2 * IMAGES, -1)

    group = jnp.arange(channels) // (channels // GROUPS)
    same = (group[:, None] == group[None, :]).astype(bf16)
    gain = norm_gain[None, :]
    shift = norm_shift[None, :]
    padded = -(-owned // 16) * 16
    low_taps = 4
    time_width = -(-feature_count // LANES) * LANES
    total_rows = holders * rows

    shape = jax.ShapeDtypeStruct
    low, high, act, normed, rstd, taps = call(
        functools.partial(weight_grad_kernel, holders, low_taps),
        (
            shape((owned, low_taps * channels + time_width), bf16),
            shape((owned, (9 - low_taps) * channels), bf16),
            shape((total_rows, channels), bf16),
            shape((holders, rows, channels), f32),
            shape((rows, channels), f32),
            shape((holders, rows, 9 * rows), bf16),
        ),
        [
            pltpu.VMEM((holders * IMAGES, channels), f32),
            pltpu.VMEM((holders, 2 * IMAGES, owned), f32),
            pltpu.VMEM((9 * padded, total_rows), bf16),
        ],
        4 * 9 * padded * total_rows * channels,
        source,
        meta,
        *blocks,
        cotan,
        embed,
        same,
        gain,
        shift,
    )
    block_out, own, other, terms = call(
        functools.partial(conv_kernel, holders),
        (
            shape((holders, rows, owned), bf16),
            shape((chips, rows, channels), bf16),
            shape((chips, rows, channels), bf16),
            shape((8, channels), f32),
        ),
        [
            pltpu.VMEM((9 * LANES, channels), bf16),
            pltpu.VMEM((holders, 2 * IMAGES, owned), f32),
            pltpu.VMEM((total_rows, 9 * LANES), bf16),
            pltpu.VMEM((2 * rows, 9 * LANES), f32),
        ],
        8 * 9 * padded * total_rows * channels,
        source,
        meta,
        act,
        normed,
        taps,
        cotan,
        embed,
        conv_weight,
        time_weight,
        gain,
        shift,
    )

    bits = [1 << i for i in range((replicas - 1).bit_length())]
    sums = []
    for part, order in ((low, bits), (high, bits[::-1])):
        total = part
        for step, bit in enumerate(order):
            total = total.astype(bf16)
            total = total.astype(f32) + exchange(total, "dp", bit).astype(f32)
        sums.append(total * scale)
    grad_conv = jnp.concatenate([sums[0][:, : low_taps * channels], sums[1]], axis=1)
    grad_time = sums[0][:, low_taps * channels : low_taps * channels + feature_count]

    met = exchange(other, "fsdp", 1)
    grad_act = own[0].astype(f32) + met[0].astype(f32)
    for k in range(1, chips):
        part = (own[k].astype(f32) + met[k].astype(f32)).astype(bf16)
        grad_act = grad_act + exchange(part, "fsdp", 2 * k).astype(f32)
    grad_features = call(
        norm_grad_kernel,
        shape((rows, channels), bf16),
        [],
        1 << 20,
        source,
        meta,
        grad_act,
        normed,
        rstd,
        same,
        gain,
        shift,
    )

    returned = lax.all_to_all(block_out, "fsdp", 0, 0)
    block_out = returned.transpose(1, 0, 2).reshape(rows, out_channels)

    for axis, size in (("fsdp", holders), ("dp", replicas)):
        for i in range((size - 1).bit_length()):
            terms = terms + exchange(terms, axis, 1 << i)
    return (block_out, grad_features, grad_conv, grad_time, terms[0] * scale, terms[1] * scale)


def solution(mesh):
    rows = P(("dp", "fsdp"), None)
    owned = P("fsdp", None)
    return jax.shard_map(
        shards,
        mesh=mesh,
        in_specs=(rows, rows, rows, rows, P(), P(), owned, owned, rows),
        out_specs=(rows, rows, owned, owned, P(), P()),
        check_vma=False,
    )
```

time: 380 us -> 107 us (0.28)
  waiting for transfers between devices: 221 us -> 31.5 us
  blocking collectives: 59.7 us -> 0 us
  local copies, waits for them, and re-layouts: 46 us -> 7.16 us
  starting transfers between devices: 0.12 us -> 30.7 us
  Pallas kernels: 0 us -> 26.2 us
  matrix products: 23.4 us -> 0 us
  between operations: 14.1 us -> 0.86 us
  other arithmetic: 15 us -> 10.1 us
    reduce_scatter x1 -> x0, waiting for transfers between devices: 157 us -> none  [shards(): lax.psum_scatter(full_term, 'fsdp', scatter_dimension=0, tiled=True)]
    psum x1 -> x0, blocking collectives: 38.2 us -> none  [shards(): grad_gain, grad_shift = lax.psum((gain_term, shift_term), ('dp', 'fsdp'))]
    all_gather x1 -> x0, waiting for transfers between devices: 35.6 us -> none  [shards(): lax.all_gather(conv_weight, 'fsdp', axis=0, tiled=True)]
    psum x1 -> x0, waiting for transfers between devices: 28 us -> none  [shards(): joined = lax.psum(reduced, 'dp')]
    pallas_call x0 -> x3, Pallas kernels: none -> 26.2 us  [call(): pl.pallas_call(kernel, out_shape=outs, in_specs=[smem, smem] + [vmem] * (...]
    ppermute x0 -> x20, waiting for transfers between devices: none -> 24.5 us  [exchange(): return lax.ppermute(value, axis, [(i, i ^ bit) for i in range(size)])]
    dot_general x15 -> x0, matrix products: 23.4 us -> none  [the longest x1 6.68 us: shards(): jnp.dot(cotan_taps, tap_weight, preferred_element_type=jnp.float32)]
    all_gather x1 -> x0, blocking collectives: 21.4 us -> none  [shards(): lax.all_gather(time_weight, 'fsdp', axis=0, tiled=True)]
  transfers between devices with their start and end apart: 3 -> 22, of which waited for: 3 -> 9; matrix products, arithmetic and copies ran while one was open for 21% -> 14% of each run, Pallas kernels for 0% -> 14%
where the time goes in v1:
time: 107 us; the launch traced here: 106 us
  waiting for transfers between devices  31.5 us (29%)
  starting transfers between devices  30.7 us (29%)
  Pallas kernels  26.2 us (24%)
  other arithmetic  10.1 us (9%)
  local copies, waits for them, and re-layouts  7.16 us (7%)
    pallas_call x3, Pallas kernels, call(): pl.pallas_call(kernel, out_shape=outs, in_specs=[smem, smem] + [vmem] * (...  26.2 us
    ppermute x20, waiting for transfers between devices, exchange(): return lax.ppermute(value, axis, [(i, i ^ bit) for i in range(size)])  24.5 us
    ppermute x20, starting transfers between devices, exchange(): return lax.ppermute(value, axis, [(i, i ^ bit) for i in range(size)])  20.8 us
    all_to_all x1, waiting for transfers between devices, shards(): lax.all_to_all(jnp.concatenate([cotangent, extra], axis=0).reshape(rows +...  6.94 us
    all_to_all x1, starting transfers between devices, shards(): lax.all_to_all(jnp.concatenate([cotangent, extra], axis=0).reshape(rows +...  5.1 us
    all_to_all x1, starting transfers between devices, shards(): returned = lax.all_to_all(block_out, 'fsdp', 0, 0)  4.77 us
  transfers between devices with their start and end apart: 22, of which 9 were waited for; matrix products, arithmetic and copies ran while one was open for 14% of the time, Pallas kernels for 14%

profile of v1, /device:TPU:0, one launch (start us, length us, event | category | flops | bytes accessed | tf_op | source)
XLA Modules:
  0.0 106.4 jit_solution(10460861361488277958)
XLA Ops:
  0.6 4.1 %collective-permute-start.3 = (bf16[128,640]{1,0:T(8,128)(2,1)}, bf16[128,640]{1,0:T(8,128)(2,1)S(1)}, u32[]{:S(2)}, u32[]{:S(2)}) collective-permute-start(bf16[128,640]{1,0:T(8,128)(2,1)} %refs_0_.1), channel_id=1, source_target_pairs={{0,4},{1,5},{2,6},{3,7},{4,0},{5,1},{6,2},{7,3},{8,12},{9,13},{10,... | collective-permute-start | bytes 491528 | tf_op jit(solution)/shard_map/ppermute | solution.py:311
  4.7 1.6 %collective-permute-start.1 = (bf16[128,640]{1,0:T(8,128)(2,1)}, bf16[128,640]{1,0:T(8,128)(2,1)S(1)}, u32[]{:S(2)}, u32[]{:S(2)}) collective-permute-start(bf16[128,640]{1,0:T(8,128)(2,1)} %refs_0_.1), channel_id=1, source_target_pairs={{0,2},{1,3},{2,0},{3,1},{4,6},{5,7},{6,4},{7,5},{8,10},{9,11},{10,... | collective-permute-start | bytes 491528 | tf_op jit(solution)/shard_map/ppermute | solution.py:311
  6.3 0.7 convert_bitcast_fusion.3
  7.0 0.7 convert_bitcast_fusion.1
  7.8 0.9 fusion.3
  8.8 0.3 broadcast_in_dim_reshape.3
  9.1 0.8 copy.18
  9.9 5.1 %all-to-all-start = ((bf16[1,144,8,96]{3,1,0,2:T(8,128)(2,1)}), bf16[1,144,8,96]{3,1,0,2:T(8,128)(2,1)S(1)}, u32[]{:S(2)}, u32[]{:S(2)}) async-start(bf16[1,144,8,96]{3,1,0,2:T(8,128)(2,1)} %copy.18), calls=%async_computation | async-start | bytes 589824 | tf_op jit(solution)/shard_map/all_to_all | solution.py:343
  15.0 1.1 %compare_convert_fusion.refs_10_.same_ref = bf16[640,640]{1,0:T(8,128)(2,1)} fusion(s32[640]{0:T(1024)S(1)} %add_select_fusion), kind=kLoop, calls=%fused_computation.1 | loop fusion | flops 819200 | bytes 821760 | tf_op jit(solution)/shard_map/convert_element_type | solution.py:356
  16.1 0.6 broadcast_in_dim.4.refs_11_.gain_ref
  16.7 0.6 broadcast_in_dim.5.refs_12_.shift_ref
  17.3 0.7 stack.35.source_ref
  18.0 0.6 collective-permute-start.4
  18.6 0.4 collective-permute-start.6
  19.1 6.9 %all-to-all-done = bf16[1,144,8,96]{3,1,0,2:T(8,128)(2,1)S(1)} async-done(((bf16[1,144,8,96]{3,1,0,2:T(8,128)(2,1)}), bf16[1,144,8,96]{3,1,0,2:T(8,128)(2,1)S(1)}, u32[]{:S(2)}, u32[]{:S(2)}) %all-to-all-start) | async-done | bytes 221216 | tf_op jit(solution)/shard_map/all_to_all | solution.py:343
  26.4 0.7 fusion.10.refs_9_.embed_ref
  27.2 0.6 copy-done.9
  28.0 11.5 %shard_map.136 = (bf16[96,2944]{1,0:T(8,128)(2,1)}, bf16[96,3200]{1,0:T(8,128)(2,1)}, bf16[1024,640]{1,0:T(8,128)(2,1)}, f32[8,128,640]{2,1,0:T(8,128)}, f32[128...) custom-call(s32[8]{0:T(128)} %stack.35.source_ref, s32[8,8]{1,0:T(8,128)} %bitcast.45, bf16[128,640]{1,0:T(8,128)(2,1)} %refs_0_.1, ...), custom_call_target="tpu_custom_call" | custom-call | flops 2264924160 | bytes 8388608 | tf_op jit(solution)/shard_map/pallas_call | solution.py:298
  39.4 1.6 %collective-permute-start.11 = (bf16[96,2944]{1,0:T(8,128)(2,1)}, bf16[96,2944]{1,0:T(8,128)(2,1)}, u32[]{:S(2)}, u32[]{:S(2)}) collective-permute-start(bf16[96,2944]{1,0:T(8,128)(2,1)} %get-tuple-element.23), channel_id=1, source_target_pairs={{0,8},{8,0},{16,24},{24,16},{1,9},{9,1},{17,25},{25,17},{2,10},{10... | collective-permute-start | bytes 1695752 | tf_op jit(solution)/shard_map/ppermute | solution.py:311
  41.0 11.1 %shard_map.137 = (bf16[8,128,96]{2,1,0:T(8,128)(2,1)}, bf16[4,128,640]{2,1,0:T(8,128)(2,1)}, bf16[4,128,640]{2,1,0:T(8,128)(2,1)}, f32[8,640]{1,0:T(8,128)}) custom-call(s32[8]{0:T(128)} %stack.35.source_ref, s32[8,8]{1,0:T(8,128)} %bitcast.46, bf16[1024,640]{1,0:T(8,128)(2,1)} %get-tuple-element.16.act_ref, f32[8,128,640]{2,1,0:T(8,128)} %get-tuple-element.17.normed_ref, ...), custom_call_target="tpu_custom_call" | custom-call | flops 4529848320 | bytes 8388608 | tf_op jit(solution)/shard_map/pallas_call | solution.py:298
  52.1 1.8 %copy.19 = bf16[8,128,96]{1,2,0:T(8,128)(2,1)} copy(bf16[8,128,96]{2,1,0:T(8,128)(2,1)} %get-tuple-element.19) | data formatting | bytes 393216 | tf_op jit(solution)/shard_map/pallas_call | solution.py:298
  54.0 4.8 %all-to-all-start.1 = ((bf16[8,128,96]{1,2,0:T(8,128)(2,1)}), bf16[8,128,96]{1,2,0:T(8,128)(2,1)S(1)}, u32[]{:S(2)}, u32[]{:S(2)}) async-start(bf16[8,128,96]{1,2,0:T(8,128)(2,1)} %copy.19), calls=%async_computation.1 | async-start | bytes 393216 | tf_op jit(solution)/shard_map/all_to_all | solution.py:449
  58.7 0.5 collective-permute-start.15
  59.2 1.1 collective-permute-done.15
  60.3 0.7 add.85
  61.0 1.9 %collective-permute-start.16 = (f32[8,640]{1,0:T(8,128)S(1)}, f32[8,640]{1,0:T(8,128)S(1)}, u32[]{:S(2)}, u32[]{:S(2)}) collective-permute-start(f32[8,640]{1,0:T(8,128)S(1)} %add.85), channel_id=1, source_target_pairs={{0,2},{1,3},{2,0},{3,1},{4,6},{5,7},{6,4},{7,5},{8,10},{9,11},{10,... | collective-permute-start | bytes 61448 | tf_op jit(solution)/shard_map/ppermute | solution.py:311
  62.9 3.3 %collective-permute-done.16 = f32[8,640]{1,0:T(8,128)S(1)} collective-permute-done((f32[8,640]{1,0:T(8,128)S(1)}, f32[8,640]{1,0:T(8,128)S(1)}, u32[]{:S(2)}, u32[]{:S(2)}) %collective-permute-start.16) | collective-permute-done | bytes 20512 | tf_op jit(solution)/shard_map/ppermute | solution.py:311
  66.2 1.7 %collective-permute-start.17 = (f32[8,640]{1,0:T(8,128)S(1)}, f32[8,640]{1,0:T(8,128)S(1)}, u32[]{:S(2)}, u32[]{:S(2)}) collective-permute-start(f32[8,640]{1,0:T(8,128)S(1)} %add.86), channel_id=1, source_target_pairs={{0,4},{1,5},{2,6},{3,7},{4,0},{5,1},{6,2},{7,3},{8,12},{9,13},{10,... | collective-permute-start | bytes 61448 | tf_op jit(solution)/shard_map/ppermute | solution.py:311
  67.9 3.1 %collective-permute-done.17 = f32[8,640]{1,0:T(8,128)S(1)} collective-permute-done((f32[8,640]{1,0:T(8,128)S(1)}, f32[8,640]{1,0:T(8,128)S(1)}, u32[]{:S(2)}, u32[]{:S(2)}) %collective-permute-start.17) | collective-permute-done | bytes 20512 | tf_op jit(solution)/shard_map/ppermute | solution.py:311
  71.0 0.5 collective-permute-start.18
  71.6 3.2 %collective-permute-done.18 = f32[8,640]{1,0:T(8,128)S(1)} collective-permute-done((f32[8,640]{1,0:T(8,128)S(1)}, f32[8,640]{1,0:T(8,128)S(1)}, u32[]{:S(2)}, u32[]{:S(2)}) %collective-permute-start.18) | collective-permute-done | bytes 20512 | tf_op jit(solution)/shard_map/ppermute | solution.py:311
  74.8 1.5 %collective-permute-start.19 = (f32[8,640]{1,0:T(8,128)S(1)}, f32[8,640]{1,0:T(8,128)S(1)}, u32[]{:S(2)}, u32[]{:S(2)}) collective-permute-start(f32[8,640]{1,0:T(8,128)S(1)} %add.88), channel_id=1, source_target_pairs={{0,16},{8,24},{16,0},{24,8},{1,17},{9,25},{17,1},{25,9},{2,18},{10... | collective-permute-start | bytes 61448 | tf_op jit(solution)/shard_map/ppermute | solution.py:311
  76.3 0.5 collective-permute-start.13
  76.8 2.0 %collective-permute-done.19 = f32[8,640]{1,0:T(8,128)S(1)} collective-permute-done((f32[8,640]{1,0:T(8,128)S(1)}, f32[8,640]{1,0:T(8,128)S(1)}, u32[]{:S(2)}, u32[]{:S(2)}) %collective-permute-start.19) | collective-permute-done | bytes 20512 | tf_op jit(solution)/shard_map/ppermute | solution.py:311
  78.9 0.6 fusion.16
  79.5 0.8 copy.20
  80.3 1.2 %add_convert_fusion.1 = bf16[96,2944]{1,0:T(8,128)(2,1)S(1)} fusion(bf16[96,2944]{1,0:T(8,128)(2,1)} %collective-permute-done.11, bf16[96,2944]{1,0:T(8,128)(2,1)S(1)} %copy-done.2), kind=kLoop, calls=%fused_computation.5 | loop fusion | flops 1130496 | bytes 1695744 | tf_op jit(solution)/shard_map/convert_element_type | solution.py:423
  81.5 1.6 %collective-permute-start.12 = (bf16[96,2944]{1,0:T(8,128)(2,1)S(1)}, bf16[96,2944]{1,0:T(8,128)(2,1)S(1)}, u32[]{:S(2)}, u32[]{:S(2)}) collective-permute-start(bf16[96,2944]{1,0:T(8,128)(2,1)S(1)} %add_convert_fusion.1), channel_id=1, source_target_pairs={{0,16},{8,24},{16,0},{24,8},{1,17},{9,25},{17,1},{25,9},{2,18},{10... | collective-permute-start | bytes 1695752 | tf_op jit(solution)/shard_map/ppermute | solution.py:311
  83.2 0.4 collective-permute-start.8
  83.7 2.7 %collective-permute-start.10 = (bf16[128,640]{1,0:T(8,128)(2,1)S(1)}, bf16[128,640]{1,0:T(8,128)(2,1)S(1)}, u32[]{:S(2)}, u32[]{:S(2)}) collective-permute-start(bf16[128,640]{1,0:T(8,128)(2,1)S(1)} %get-tuple-element.41), channel_id=1, source_target_pairs={{0,6},{1,7},{2,4},{3,5},{4,2},{5,3},{6,0},{7,1},{8,14},{9,15},{10,... | collective-permute-start | bytes 491528 | tf_op jit(solution)/shard_map/ppermute | solution.py:311
  86.4 0.4 collective-permute-start.9
  86.8 6.3 %collective-permute-done.13 = bf16[96,3200]{1,0:T(8,128)(2,1)S(1)} collective-permute-done((bf16[96,3200]{1,0:T(8,128)(2,1)S(1)}, bf16[96,3200]{1,0:T(8,128)(2,1)S(1)}, u32[]{:S(2)}, u32[]{:S(2)}) %collective-permute-start.13) | collective-permute-done | bytes 614432 | tf_op jit(solution)/shard_map/ppermute | solution.py:311
  93.3 0.6 collective-permute-start.14
  94.0 5.4 %collective-permute-done.9 = bf16[128,640]{1,0:T(8,128)(2,1)S(1)} collective-permute-done((bf16[128,640]{1,0:T(8,128)(2,1)S(1)}, bf16[128,640]{1,0:T(8,128)(2,1)S(1)}, u32[]{:S(2)}, u32[]{:S(2)}) %collective-permute-start.9) | collective-permute-done | bytes 163872 | tf_op jit(solution)/shard_map/ppermute | solution.py:311
  99.3 0.8 fusion.2.grad_ref
  100.2 3.6 %shard_map.138 = bf16[128,640]{1,0:T(8,128)(2,1)} custom-call(s32[8]{0:T(128)} %stack.35.source_ref, s32[8,8]{1,0:T(8,128)} %bitcast.47, f32[128,640]{1,0:T(8,128)} %fusion.2.grad_ref, f32[8,128,640]{2,1,0:T(8,128)} %get-tuple-element.17.normed_ref, f32[128,640]{1,0:T(8,128)} %get-tuple-element.22.rstd_ref, ...), custom_call_target="tpu_custom_call" | custom-call | flops 1048576 | bytes 8388608 | tf_op jit(solution)/shard_map/pallas_call | solution.py:298
  103.9 0.7 slice.70
  104.9 1.5 %pad_maximum_fusion = f32[96,5760]{1,0:T(8,128)} fusion(f32[96,3200]{1,0:T(8,128)S(1)} %add_multiply_fusion, f32[96,2560]{1,0:T(8,128)S(1)} %slice.69), kind=kLoop, calls=%fused_computation | loop fusion | flops 552960 | bytes 4423680 | tf_op jit(solution)/shard_map/concatenate | solution.py:426
  (62 shorter events, 1.7 us)
Async XLA Ops:
  0.6 17.3 %collective-permute-start.3 = (bf16[128,640]{1,0:T(8,128)(2,1)}, bf16[128,640]{1,0:T(8,128)(2,1)S(1)}, u32[]{:S(2)}, u32[]{:S(2)}) collective-permute-start(bf16[128,640]{1,0:T(8,128)(2,1)} %refs_0_.1), channel_id=1, source_target_pairs={{0,4},{1,5},{2,6},{3,7},{4,0},{5,1},{6,2},{7,3},{8,12},{9,13},{10,... | collective-permute-start | bytes 491528 | tf_op jit(solution)/shard_map/ppermute | solution.py:311
  4.7 13.8 %collective-permute-start.1 = (bf16[128,640]{1,0:T(8,128)(2,1)}, bf16[128,640]{1,0:T(8,128)(2,1)S(1)}, u32[]{:S(2)}, u32[]{:S(2)}) collective-permute-start(bf16[128,640]{1,0:T(8,128)(2,1)} %refs_0_.1), channel_id=1, source_target_pairs={{0,2},{1,3},{2,0},{3,1},{4,6},{5,7},{6,4},{7,5},{8,10},{9,11},{10,... | collective-permute-start | bytes 491528 | tf_op jit(solution)/shard_map/ppermute | solution.py:311
  6.3 20.8 %collective-permute-start = (bf16[128,640]{1,0:T(8,128)(2,1)}, bf16[128,640]{1,0:T(8,128)(2,1)S(1)}, u32[]{:S(2)}, u32[]{:S(2)}) collective-permute-start(bf16[128,640]{1,0:T(8,128)(2,1)} %refs_0_.1), channel_id=1, source_target_pairs={{0,1},{1,0},{2,3},{3,2},{4,5},{5,4},{6,7},{7,6},{8,9},{9,8},{10,11... | collective-permute-start | bytes 491528 | tf_op jit(solution)/shard_map/ppermute | solution.py:311
  6.3 12.3 %collective-permute-start.5 = (bf16[128,640]{1,0:T(8,128)(2,1)}, bf16[128,640]{1,0:T(8,128)(2,1)S(1)}, u32[]{:S(2)}, u32[]{:S(2)}) collective-permute-start(bf16[128,640]{1,0:T(8,128)(2,1)} %refs_0_.1), channel_id=1, source_target_pairs={{0,6},{1,7},{2,4},{3,5},{4,2},{5,3},{6,0},{7,1},{8,14},{9,15},{10,... | collective-permute-start | bytes 491528 | tf_op jit(solution)/shard_map/ppermute | solution.py:311
  8.8 7.3 %copy-start.5 = (f32[640]{0:T(1024)S(1)}, f32[640]{0:T(1024)}, u32[]{:S(2)}) copy-start(f32[640]{0:T(1024)} %param.13) | copy-start | bytes 7684
  8.8 7.9 %copy-start.6 = (f32[640]{0:T(1024)S(1)}, f32[640]{0:T(1024)}, u32[]{:S(2)}) copy-start(f32[640]{0:T(1024)} %param.14) | copy-start | bytes 7684
  9.9 16.1 %all-to-all-start = ((bf16[1,144,8,96]{3,1,0,2:T(8,128)(2,1)}), bf16[1,144,8,96]{3,1,0,2:T(8,128)(2,1)S(1)}, u32[]{:S(2)}, u32[]{:S(2)}) async-start(bf16[1,144,8,96]{3,1,0,2:T(8,128)(2,1)} %copy.18), calls=%async_computation | async-start | bytes 589824 | tf_op jit(solution)/shard_map/all_to_all | solution.py:343
  18.0 9.2 %copy-start.7 = (bf16[128,640]{1,0:T(8,128)(2,1)}, bf16[128,640]{1,0:T(8,128)(2,1)S(1)}, u32[]{:S(2)}) copy-start(bf16[128,640]{1,0:T(8,128)(2,1)S(1)} %collective-permute-done.3.refs_4_) | copy-start | bytes 491524
  18.0 9.2 %collective-permute-start.4 = (bf16[128,640]{1,0:T(8,128)(2,1)S(1)}, bf16[128,640]{1,0:T(8,128)(2,1)S(1)}, u32[]{:S(2)}, u32[]{:S(2)}) collective-permute-start(bf16[128,640]{1,0:T(8,128)(2,1)S(1)} %collective-permute-done.3.refs_4_), channel_id=1, source_target_pairs={{0,1},{1,0},{2,3},{3,2},{4,5},{5,4},{6,7},{7,6},{8,9},{9,8},{10,11... | collective-permute-start | bytes 491528 | tf_op jit(solution)/shard_map/ppermute | solution.py:311
  18.5 8.7 %copy-start.8 = (bf16[128,640]{1,0:T(8,128)(2,1)}, bf16[128,640]{1,0:T(8,128)(2,1)S(1)}, u32[]{:S(2)}) copy-start(bf16[128,640]{1,0:T(8,128)(2,1)S(1)} %collective-permute-done.1.refs_2_) | copy-start | bytes 491524
  18.5 8.6 %collective-permute-start.2 = (bf16[128,640]{1,0:T(8,128)(2,1)S(1)}, bf16[128,640]{1,0:T(8,128)(2,1)S(1)}, u32[]{:S(2)}, u32[]{:S(2)}) collective-permute-start(bf16[128,640]{1,0:T(8,128)(2,1)S(1)} %collective-permute-done.1.refs_2_), channel_id=1, source_target_pairs={{0,1},{1,0},{2,3},{3,2},{4,5},{5,4},{6,7},{7,6},{8,9},{9,8},{10,11... | collective-permute-start | bytes 491528 | tf_op jit(solution)/shard_map/ppermute | solution.py:311
  18.6 8.6 %copy-start.10 = (bf16[128,640]{1,0:T(8,128)(2,1)}, bf16[128,640]{1,0:T(8,128)(2,1)S(1)}, u32[]{:S(2)}) copy-start(bf16[128,640]{1,0:T(8,128)(2,1)S(1)} %collective-permute-done.5.refs_6_) | copy-start | bytes 491524
  18.6 8.5 %collective-permute-start.6 = (bf16[128,640]{1,0:T(8,128)(2,1)S(1)}, bf16[128,640]{1,0:T(8,128)(2,1)S(1)}, u32[]{:S(2)}, u32[]{:S(2)}) collective-permute-start(bf16[128,640]{1,0:T(8,128)(2,1)S(1)} %collective-permute-done.5.refs_6_), channel_id=1, source_target_pairs={{0,1},{1,0},{2,3},{3,2},{4,5},{5,4},{6,7},{7,6},{8,9},{9,8},{10,11... | collective-permute-start | bytes 491528 | tf_op jit(solution)/shard_map/ppermute | solution.py:311
  26.0 1.2 %copy-start.3 = (bf16[1,144,8,96]{3,1,0,2:T(8,128)(2,1)}, bf16[1,144,8,96]{3,1,0,2:T(8,128)(2,1)S(1)}, u32[]{:S(2)}) copy-start(bf16[1,144,8,96]{3,1,0,2:T(8,128)(2,1)S(1)} %all-to-all-done) | copy-start | bytes 663556
  26.0 1.2 %copy-start.4 = (s32[8,1,16]{2,1,0:T(1,128)}, s32[8,1,16]{2,1,0:T(1,128)S(1)}, u32[]{:S(2)}) copy-start(s32[8,1,16]{2,1,0:T(1,128)S(1)} %slice_convert_fusion) | copy-start | bytes 1540
  27.1 0.7 copy-start.9
  27.1 0.7 copy-start.11
  27.2 0.8 copy-start.12
  27.2 0.8 copy-start.13
  39.4 40.9 %collective-permute-start.11 = (bf16[96,2944]{1,0:T(8,128)(2,1)}, bf16[96,2944]{1,0:T(8,128)(2,1)}, u32[]{:S(2)}, u32[]{:S(2)}) collective-permute-start(bf16[96,2944]{1,0:T(8,128)(2,1)} %get-tuple-element.23), channel_id=1, source_target_pairs={{0,8},{8,0},{16,24},{24,16},{1,9},{9,1},{17,25},{25,17},{2,10},{10... | collective-permute-start | bytes 1695752 | tf_op jit(solution)/shard_map/ppermute | solution.py:311
  41.0 35.3 %copy-start.1 = (bf16[96,3200]{1,0:T(8,128)(2,1)S(1)}, bf16[96,3200]{1,0:T(8,128)(2,1)}, u32[]{:S(2)}) copy-start(bf16[96,3200]{1,0:T(8,128)(2,1)} %get-tuple-element.24) | copy-start | bytes 1843204
  52.1 28.2 %copy-start.2 = (bf16[96,2944]{1,0:T(8,128)(2,1)S(1)}, bf16[96,2944]{1,0:T(8,128)(2,1)}, u32[]{:S(2)}) copy-start(bf16[96,2944]{1,0:T(8,128)(2,1)} %get-tuple-element.23) | copy-start | bytes 1695748
  54.0 25.5 %all-to-all-start.1 = ((bf16[8,128,96]{1,2,0:T(8,128)(2,1)}), bf16[8,128,96]{1,2,0:T(8,128)(2,1)S(1)}, u32[]{:S(2)}, u32[]{:S(2)}) async-start(bf16[8,128,96]{1,2,0:T(8,128)(2,1)} %copy.19), calls=%async_computation.1 | async-start | bytes 393216 | tf_op jit(solution)/shard_map/all_to_all | solution.py:449
  58.7 24.4 %copy-start = (bf16[4,128,640]{2,1,0:T(8,128)(2,1)S(1)}, bf16[4,128,640]{2,1,0:T(8,128)(2,1)}, u32[]{:S(2)}) copy-start(bf16[4,128,640]{2,1,0:T(8,128)(2,1)} %get-tuple-element.20) | copy-start | bytes 1966084
  58.7 1.6 %collective-permute-start.15 = (f32[8,640]{1,0:T(8,128)}, f32[8,640]{1,0:T(8,128)S(1)}, u32[]{:S(2)}, u32[]{:S(2)}) collective-permute-start(f32[8,640]{1,0:T(8,128)} %get-tuple-element.25), channel_id=1, source_target_pairs={{0,1},{1,0},{2,3},{3,2},{4,5},{5,4},{6,7},{7,6},{8,9},{9,8},{10,11... | collective-permute-start | bytes 61448 | tf_op jit(solution)/shard_map/ppermute | solution.py:311
  61.0 5.1 %collective-permute-start.16 = (f32[8,640]{1,0:T(8,128)S(1)}, f32[8,640]{1,0:T(8,128)S(1)}, u32[]{:S(2)}, u32[]{:S(2)}) collective-permute-start(f32[8,640]{1,0:T(8,128)S(1)} %add.85), channel_id=1, source_target_pairs={{0,2},{1,3},{2,0},{3,1},{4,6},{5,7},{6,4},{7,5},{8,10},{9,11},{10,... | collective-permute-start | bytes 61448 | tf_op jit(solution)/shard_map/ppermute | solution.py:311
  66.2 4.8 %collective-permute-start.17 = (f32[8,640]{1,0:T(8,128)S(1)}, f32[8,640]{1,0:T(8,128)S(1)}, u32[]{:S(2)}, u32[]{:S(2)}) collective-permute-start(f32[8,640]{1,0:T(8,128)S(1)} %add.86), channel_id=1, source_target_pairs={{0,4},{1,5},{2,6},{3,7},{4,0},{5,1},{6,2},{7,3},{8,12},{9,13},{10,... | collective-permute-start | bytes 61448 | tf_op jit(solution)/shard_map/ppermute | solution.py:311
  71.0 3.8 %collective-permute-start.18 = (f32[8,640]{1,0:T(8,128)S(1)}, f32[8,640]{1,0:T(8,128)S(1)}, u32[]{:S(2)}, u32[]{:S(2)}) collective-permute-start(f32[8,640]{1,0:T(8,128)S(1)} %add.87), channel_id=1, source_target_pairs={{0,8},{8,0},{16,24},{24,16},{1,9},{9,1},{17,25},{25,17},{2,10},{10... | collective-permute-start | bytes 61448 | tf_op jit(solution)/shard_map/ppermute | solution.py:311
  74.8 4.1 %collective-permute-start.19 = (f32[8,640]{1,0:T(8,128)S(1)}, f32[8,640]{1,0:T(8,128)S(1)}, u32[]{:S(2)}, u32[]{:S(2)}) collective-permute-start(f32[8,640]{1,0:T(8,128)S(1)} %add.88), channel_id=1, source_target_pairs={{0,16},{8,24},{16,0},{24,8},{1,17},{9,25},{17,1},{25,9},{2,18},{10... | collective-permute-start | bytes 61448 | tf_op jit(solution)/shard_map/ppermute | solution.py:311
  76.3 16.8 %collective-permute-start.13 = (bf16[96,3200]{1,0:T(8,128)(2,1)S(1)}, bf16[96,3200]{1,0:T(8,128)(2,1)S(1)}, u32[]{:S(2)}, u32[]{:S(2)}) collective-permute-start(bf16[96,3200]{1,0:T(8,128)(2,1)S(1)} %copy-done.1), channel_id=1, source_target_pairs={{0,16},{8,24},{16,0},{24,8},{1,17},{9,25},{17,1},{25,9},{2,18},{10... | collective-permute-start | bytes 1843208 | tf_op jit(solution)/shard_map/ppermute | solution.py:311
  76.8 6.3 %collective-permute-start.7 = (bf16[4,128,640]{2,1,0:T(8,128)(2,1)}, bf16[4,128,640]{2,1,0:T(8,128)(2,1)S(1)}, u32[]{:S(2)}, u32[]{:S(2)}) collective-permute-start(bf16[4,128,640]{2,1,0:T(8,128)(2,1)} %get-tuple-element.21), channel_id=1, source_target_pairs={{0,1},{1,0},{2,3},{3,2},{4,5},{5,4},{6,7},{7,6},{8,9},{9,8},{10,11... | collective-permute-start | bytes 1966088 | tf_op jit(solution)/shard_map/ppermute | solution.py:311
  81.5 22.3 %collective-permute-start.12 = (bf16[96,2944]{1,0:T(8,128)(2,1)S(1)}, bf16[96,2944]{1,0:T(8,128)(2,1)S(1)}, u32[]{:S(2)}, u32[]{:S(2)}) collective-permute-start(bf16[96,2944]{1,0:T(8,128)(2,1)S(1)} %add_convert_fusion.1), channel_id=1, source_target_pairs={{0,16},{8,24},{16,0},{24,8},{1,17},{9,25},{17,1},{25,9},{2,18},{10... | collective-permute-start | bytes 1695752 | tf_op jit(solution)/shard_map/ppermute | solution.py:311
  83.2 10.6 %collective-permute-start.8 = (bf16[128,640]{1,0:T(8,128)(2,1)S(1)}, bf16[128,640]{1,0:T(8,128)(2,1)S(1)}, u32[]{:S(2)}, u32[]{:S(2)}) collective-permute-start(bf16[128,640]{1,0:T(8,128)(2,1)S(1)} %get-tuple-element.40), channel_id=1, source_target_pairs={{0,2},{1,3},{2,0},{3,1},{4,6},{5,7},{6,4},{7,5},{8,10},{9,11},{10,... | collective-permute-start | bytes 491528 | tf_op jit(solution)/shard_map/ppermute | solution.py:311
  83.7 10.3 %collective-permute-start.10 = (bf16[128,640]{1,0:T(8,128)(2,1)S(1)}, bf16[128,640]{1,0:T(8,128)(2,1)S(1)}, u32[]{:S(2)}, u32[]{:S(2)}) collective-permute-start(bf16[128,640]{1,0:T(8,128)(2,1)S(1)} %get-tuple-element.41), channel_id=1, source_target_pairs={{0,6},{1,7},{2,4},{3,5},{4,2},{5,3},{6,0},{7,1},{8,14},{9,15},{10,... | collective-permute-start | bytes 491528 | tf_op jit(solution)/shard_map/ppermute | solution.py:311
  86.4 12.9 %collective-permute-start.9 = (bf16[128,640]{1,0:T(8,128)(2,1)S(1)}, bf16[128,640]{1,0:T(8,128)(2,1)S(1)}, u32[]{:S(2)}, u32[]{:S(2)}) collective-permute-start(bf16[128,640]{1,0:T(8,128)(2,1)S(1)} %get-tuple-element.42), channel_id=1, source_target_pairs={{0,4},{1,5},{2,6},{3,7},{4,0},{5,1},{6,2},{7,3},{8,12},{9,13},{10,... | collective-permute-start | bytes 491528 | tf_op jit(solution)/shard_map/ppermute | solution.py:311
  93.3 11.4 %collective-permute-start.14 = (bf16[96,3200]{1,0:T(8,128)(2,1)S(1)}, bf16[96,3200]{1,0:T(8,128)(2,1)S(1)}, u32[]{:S(2)}, u32[]{:S(2)}) collective-permute-start(bf16[96,3200]{1,0:T(8,128)(2,1)S(1)} %add_convert_fusion), channel_id=1, source_target_pairs={{0,8},{8,0},{16,24},{24,16},{1,9},{9,1},{17,25},{25,17},{2,10},{10... | collective-permute-start | bytes 1843208 | tf_op jit(solution)/shard_map/ppermute | solution.py:311

commit v2 on v0

v2 whole, which is shorter than its diff:
```python
import functools
import math

import jax
import jax.numpy as jnp
from jax import lax
from jax.experimental import pallas as pl
from jax.experimental.pallas import tpu as pltpu
from jax.sharding import PartitionSpec as P

GROUPS = 32
IMAGES = 4
LANES = 128

bf16 = jnp.bfloat16
f32 = jnp.float32


def dot(a, b, dims=((1,), (0,))):
    return lax.dot_general(a, b, (dims, ((), ())), preferred_element_type=f32)


def split3(x):
    hi = x.astype(bf16)
    rest = x - hi.astype(f32)
    mid = rest.astype(bf16)
    low = (rest - mid.astype(f32)).astype(bf16)
    return hi, mid, low


def exact_dot(x, ones):
    rows = x.shape[0]
    out = dot(jnp.concatenate(split3(x), axis=0), ones)
    return out[:rows] + out[rows : 2 * rows] + out[2 * rows :]


def bounds_of(heights, widths):
    start = heights[0] * 0
    found = []
    for height, width in zip(heights, widths):
        area = height * width
        found.append((start, start + area, width, area))
        start = start + area
    return found


def inverse_area(area):
    return 1.0 / jnp.maximum(area, 1).astype(f32)


def masks(bounds, shape):
    row = lax.broadcasted_iota(jnp.int32, shape, 0)
    return [(row >= start) & (row < end) for start, end, _, _ in bounds]


def spread(members, table, shape):
    out = jnp.zeros(shape, f32)
    for j in range(IMAGES):
        out = jnp.where(members[j], table[j : j + 1, :], out)
    return out


def image_sums(members, values, bounds):
    sums = []
    for j in range(IMAGES):
        total = jnp.sum(jnp.where(members[j], values, 0.0), axis=0, keepdims=True)
        sums.append(total * inverse_area(bounds[j][3]))
    return jnp.concatenate(sums, axis=0)


def tap_matrices(bounds, rows):
    shape = (rows, rows)
    row = lax.broadcasted_iota(jnp.int32, shape, 0)
    gap = lax.broadcasted_iota(jnp.int32, shape, 1) - row
    width = jnp.zeros(shape, jnp.int32)
    area = jnp.zeros(shape, jnp.int32)
    first = jnp.zeros(shape, jnp.int32)
    for start, end, wide, size in bounds:
        member = (row >= start) & (row < end)
        width = jnp.where(member, wide, width)
        area = jnp.where(member, size, area)
        first = jnp.where(member, start, first)
    offset = row - first
    column = offset & (width - 1)
    columns = {-1: column >= 1, 0: column >= 0, 1: column + 1 < width}
    taps = []
    for shift_row in (-1, 0, 1):
        moved = offset + shift_row * width
        inside = (moved >= 0) & (moved < area)
        left = gap - shift_row * width
        for shift_col in (-1, 0, 1):
            hit = inside & columns[shift_col] & (left == shift_col)
            taps.append(jnp.where(hit, 1.0, 0.0).astype(bf16))
    return taps


def group_matrices(channels):
    size = channels // GROUPS
    channel = lax.broadcasted_iota(jnp.int32, (channels, LANES), 0)
    group = lax.broadcasted_iota(jnp.int32, (channels, LANES), 1)
    down = jnp.where((channel >= group * size) & (channel < (group + 1) * size), 1.0, 0.0)
    channel = lax.broadcasted_iota(jnp.int32, (LANES, channels), 1)
    group = lax.broadcasted_iota(jnp.int32, (LANES, channels), 0)
    back = jnp.where((channel >= group * size) & (channel < (group + 1) * size), 1.0, 0.0)
    return down.astype(bf16), back.astype(bf16)


def group_means(sums, matrices):
    down, back = matrices
    size = down.shape[0] // GROUPS
    return exact_dot(exact_dot(sums, down) * (1.0 / size), back)


def prepare_kernel(
    owned, me_ref, heights_ref, widths_ref, times_ref, features_ref, cotan_ref, *sent
):
    rows, channels = features_ref.shape
    holders = cotan_ref.shape[1] // owned
    padded = -(-owned // 16) * 16
    place = lax.broadcasted_iota(jnp.int32, (16, LANES), 0)
    facts = jnp.zeros((16, LANES), f32)
    for j in range(IMAGES):
        time = times_ref[0, j]
        for i, value in enumerate((heights_ref[0, j], widths_ref[0, j], time >> 5, time & 31)):
            facts = jnp.where(place == i * IMAGES + j, value.astype(f32), facts)
    facts = facts.astype(bf16)
    turned = cotan_ref[...].astype(f32).T
    chip = me_ref[0] >> 1
    slots = []
    for s in range(holders):
        part = turned[s * owned : (s + 1) * owned]
        if padded > owned:
            part = jnp.concatenate([part, jnp.zeros((padded - owned, rows), f32)], axis=0)
        slots.append(part.astype(bf16))
    first = 0
    for ref in sent:
        count = max(first, 1)
        for s in range(holders):
            slot = (chip ^ (s // 2)) - first

            @pl.when((slot >= 0) & (slot < count))
            def _():
                start = pl.multiple_of((2 * slot + s % 2) * padded, 16)
                ref[pl.ds(start, padded), :] = slots[s]

        top = count * 2 * padded
        ref[top : top + 16, :] = facts
        for q in range(channels // LANES):
            start = top + 16 + q * rows
            ref[start : start + rows, :] = features_ref[:, q * LANES : (q + 1) * LANES]
        first = max(2 * first, 1)


def weight_kernel(me_ref, conv_ref, out_ref):
    owned = conv_ref.shape[0]
    channels = out_ref.shape[1]
    padded = -(-owned // 16) * 16
    for t in range(9):
        part = conv_ref[:, t * channels : (t + 1) * channels]
        if padded > owned:
            part = jnp.concatenate([part, jnp.zeros((padded - owned, channels), bf16)], axis=0)
        out_ref[t * LANES : t * LANES + padded, :] = part
        if padded < LANES:
            out_ref[t * LANES + padded : (t + 1) * LANES, :] = jnp.zeros(
                (LANES - padded, channels), bf16
            )


def chunk_sums(members, chunks, inverses):
    out = []
    for chunk in chunks:
        sums = [
            jnp.sum(jnp.where(member, chunk, 0.0), axis=0, keepdims=True) * inverse
            for member, inverse in zip(members, inverses)
        ]
        out.append(jnp.concatenate(sums, axis=0))
    return jnp.concatenate(out, axis=1)


def block_facts(ref, top):
    facts = ref[top : top + 16, :].astype(f32)
    sizes = [facts[j : j + 1, :].astype(jnp.int32) for j in range(2 * IMAGES)]
    times = facts[2 * IMAGES : 3 * IMAGES] * 32.0 + facts[3 * IMAGES :]
    return bounds_of(sizes[:IMAGES], sizes[IMAGES:]), times


def norm_kernel(
    slot,
    top,
    keep,
    features,
    me_ref,
    near_ref,
    far_ref,
    affine_ref,
    turned_ref,
    act_ref,
    sums_ref,
    embed_ref,
    taps_ref,
    slopes_ref,
    norms_ref,
    *kept,
):
    padded = turned_ref.shape[0] // 9
    rows = LANES
    channels = act_ref.shape[1]
    count = channels // LANES
    start = pl.multiple_of((2 * slot + (me_ref[0] & 1)) * padded, 16)
    found = []
    chunks = []
    times = []
    for b, ref in enumerate((near_ref, far_ref)):
        bounds, time = block_facts(ref, top)
        times.append(time)
        taps = jnp.concatenate(tap_matrices(bounds, rows), axis=1)
        taps_ref[b * rows : (b + 1) * rows, :] = taps
        found.append((masks(bounds, (rows, LANES)), [inverse_area(size) for *_, size in bounds]))
        cotan = ref[pl.ds(start, padded), :]
        turned = dot(cotan, taps).astype(bf16)
        for t in range(9):
            turned_ref[t * padded : (t + 1) * padded, b * rows : (b + 1) * rows] = turned[
                :, t * rows : (t + 1) * rows
            ]
        image = lax.broadcasted_iota(jnp.int32, (IMAGES, rows), 0)
        place = lax.broadcasted_iota(jnp.int32, (IMAGES, rows), 1)
        member = jnp.zeros((IMAGES, rows), f32)
        for j in range(IMAGES):
            begin, end, _, _ = bounds[j]
            member = jnp.where((image == j) & (place >= begin) & (place < end), 1.0, member)
        sums_ref[b * IMAGES : (b + 1) * IMAGES, :] = dot(member.astype(bf16), cotan, ((1,), (1,)))
        first = top + 16
        chunks.append(
            [ref[first + q * rows : first + (q + 1) * rows, :].astype(f32) for q in range(count)]
        )

    matrices = group_matrices(channels)
    sums = [chunk_sums(found[b][0], chunks[b], found[b][1]) for b in range(2)]
    means = group_means(jnp.concatenate(sums, axis=0), matrices)
    sums = []
    for b in range(2):
        members, inverses = found[b]
        for q in range(count):
            mean = means[b * IMAGES : (b + 1) * IMAGES, q * LANES : (q + 1) * LANES]
            chunks[b][q] = chunks[b][q] - spread(members, mean, (rows, LANES))
        sums.append(chunk_sums(members, [c * c for c in chunks[b]], inverses))
    rstds = lax.rsqrt(group_means(jnp.concatenate(sums, axis=0), matrices) + 1e-05)
    for b in range(2):
        members = found[b][0]
        for q in range(count):
            here = slice(b * rows, (b + 1) * rows), slice(q * LANES, (q + 1) * LANES)
            rstd = rstds[b * IMAGES : (b + 1) * IMAGES, q * LANES : (q + 1) * LANES]
            rstd = spread(members, rstd, (rows, LANES))
            normed = chunks[b][q] * rstd
            shifted = normed * affine_ref[0:1, here[1]] + affine_ref[1:2, here[1]]
            sig = jax.nn.sigmoid(shifted)
            act_ref[here] = (shifted * sig).astype(bf16)
            slopes_ref[here] = sig * (1.0 + shifted * (1.0 - sig))
            norms_ref[here] = normed
            if keep and b == 0:
                kept[0][:, here[1]] = rstd

    half = features // 2
    place = lax.broadcasted_iota(jnp.int32, (2 * IMAGES, half), 1).astype(f32)
    rates = jnp.exp(-math.log(10000.0) * place / half)
    angles = jnp.concatenate(times, axis=0)[:, :1] * rates
    embed_ref[...] = jnp.concatenate([jnp.sin(angles), jnp.cos(angles)], axis=1)


def conv_kernel(
    slot,
    top,
    owned,
    me_ref,
    near_ref,
    far_ref,
    act_ref,
    embed_ref,
    taps_ref,
    slopes_ref,
    norms_ref,
    weights_ref,
    time_ref,
    before_ref,
    own_ref,
    other_ref,
    terms_ref,
    product,
):
    rows = LANES
    channels = act_ref.shape[1]
    count = channels // LANES
    padded = own_ref.shape[0] - count * rows
    start = pl.multiple_of((2 * slot + (me_ref[0] & 1)) * padded, 16)
    weights = weights_ref[...]
    moved = []
    tiles = []
    for b, ref in enumerate((near_ref, far_ref)):
        taps = taps_ref[b * rows : (b + 1) * rows, :]
        tiles.append(taps)
        cotan = ref[pl.ds(start, padded), :]
        if padded < LANES:
            cotan = jnp.concatenate([cotan, jnp.zeros((LANES - padded, rows), bf16)], axis=0)
        stacked = [taps[:, (8 - t) * rows : (9 - t) * rows] for t in range(9)]
        shifted = dot(jnp.concatenate(stacked, axis=0), cotan, ((1,), (1,))).astype(bf16)
        moved.append(
            jnp.concatenate([shifted[t * rows : (t + 1) * rows] for t in range(9)], axis=1)
        )
    grad_act = dot(jnp.concatenate(moved, axis=0), weights)
    slope = grad_act * slopes_ref[...]
    terms_ref[...] = before_ref[...] + jnp.concatenate(
        [
            jnp.sum(slope * norms_ref[...], axis=0, keepdims=True),
            jnp.sum(slope, axis=0, keepdims=True),
            jnp.zeros((6, channels), f32),
        ],
        axis=0,
    )
    grad_act = grad_act.astype(bf16)
    product[...] = dot(act_ref[...], weights, ((1,), (1,)))
    bias = dot(embed_ref[...].astype(bf16), time_ref[...], ((1,), (1,)))
    if owned < LANES:
        bias = jnp.concatenate([bias, jnp.zeros((2 * IMAGES, LANES - owned), f32)], axis=1)
    for b, (ref, source) in enumerate(((own_ref, near_ref), (other_ref, far_ref))):
        for q in range(count):
            ref[q * rows : (q + 1) * rows, :] = grad_act[
                b * rows : (b + 1) * rows, q * LANES : (q + 1) * LANES
            ]
        values = product[b * rows : (b + 1) * rows, :]
        high = values.astype(bf16)
        low = (values - high.astype(f32)).astype(bf16)
        parts = [high[:, t * LANES : (t + 1) * LANES] for t in range(9)]
        parts += [low[:, t * LANES : (t + 1) * LANES] for t in range(9)]
        total = dot(
            jnp.concatenate([tiles[b], tiles[b]], axis=1), jnp.concatenate(parts, axis=0)
        )
        members = masks(block_facts(source, top)[0], (rows, LANES))
        total = total + spread(members, bias[b * IMAGES : (b + 1) * IMAGES], (rows, LANES))
        ref[count * rows :, :] = total.T[:padded].astype(bf16)


def weight_grad_kernel(pairs, low_taps, owned, *refs):
    turned, act, sums, embed = (
        [ref[...] for ref in refs[i * pairs : (i + 1) * pairs]] for i in range(4)
    )
    low_ref, high_ref = refs[4 * pairs :]
    channels = act[0].shape[1]
    padded = turned[0].shape[0] // 9
    grad = dot(jnp.concatenate(turned, axis=1), jnp.concatenate(act, axis=0))
    for t in range(9):
        part = grad[t * padded : t * padded + owned].astype(bf16)
        if t < low_taps:
            low_ref[:, t * channels : (t + 1) * channels] = part
        else:
            high_ref[:, (t - low_taps) * channels : (t - low_taps + 1) * channels] = part
    embed = jnp.concatenate(embed, axis=0).astype(bf16)
    time_grad = jnp.zeros((padded, embed.shape[1]), f32)
    for term in split3(jnp.concatenate(sums, axis=0)):
        time_grad = time_grad + dot(term, embed, ((0,), (0,)))
    spare = low_ref.shape[1] - low_taps * channels - embed.shape[1]
    low_ref[:, low_taps * channels :] = jnp.concatenate(
        [time_grad[:owned], jnp.zeros((owned, spare), f32)], axis=1
    ).astype(bf16)


def join_kernel(owned, own_ref, met_ref, out_ref):
    size = own_ref.shape[0]
    padded = -(-owned // 16) * 16
    top = size - padded
    total = own_ref[:top, :].astype(f32) + met_ref[:top, :].astype(f32)
    out_ref[:top, :] = total.astype(out_ref.dtype)
    out_ref[top:size, :] = own_ref[top:, :].astype(out_ref.dtype)
    out_ref[size:, :] = met_ref[top:, :].astype(out_ref.dtype)


def norm_grad_kernel(
    owned,
    chips,
    me_ref,
    heights_ref,
    widths_ref,
    *refs,
):
    terms = refs[:chips]
    normed_ref, rstd_ref, affine_ref, out_ref, grad_ref, joined = refs[chips:]
    rows, channels = rstd_ref.shape
    top = channels // LANES * rows
    padded = (terms[0].shape[0] - top) // 2
    me = me_ref[0]
    pieces = []
    for ref in terms:
        pieces += [ref[top : top + padded, :], ref[top + padded :, :]]
    for b, piece in enumerate(pieces):
        start = pl.multiple_of((me ^ b) * owned, 8)
        joined[pl.ds(start, owned), :] = piece[:owned].astype(f32)
    out_ref[...] = joined[...].T.astype(bf16)

    total = terms[0][:top, :]
    for ref in terms[1:]:
        total = total + ref[:top, :].astype(f32)
    total = jnp.concatenate(
        [total[q * rows : (q + 1) * rows] for q in range(channels // LANES)], axis=1
    )
    normed = normed_ref[:rows, :]
    gain = affine_ref[0:1, :]
    shifted = normed * gain + affine_ref[1:2, :]
    sig = jax.nn.sigmoid(shifted)
    slope = total * (sig * (1.0 + shifted * (1.0 - sig)))
    grad = slope * gain
    bounds = bounds_of(
        [heights_ref[0, j] for j in range(IMAGES)], [widths_ref[0, j] for j in range(IMAGES)]
    )
    members = masks(bounds, (rows, channels))
    sums = jnp.concatenate(
        [image_sums(members, grad, bounds), image_sums(members, grad * normed, bounds)], axis=0
    )
    means = group_means(sums, group_matrices(channels))
    mean_grad = spread(members, means[:IMAGES], (rows, channels))
    mean_cross = spread(members, means[IMAGES:], (rows, channels))
    grad_ref[...] = (rstd_ref[...] * (grad - mean_grad - normed * mean_cross)).astype(bf16)


def finish_kernel(scale, low_ref, low_met_ref, high_ref, high_met_ref, conv_ref, time_ref):
    low = (low_ref[...].astype(f32) + low_met_ref[...].astype(f32)) * scale
    width = conv_ref.shape[1] - high_ref.shape[1]
    conv_ref[:, :width] = low[:, :width]
    time_ref[...] = low[:, width : width + time_ref.shape[1]]
    conv_ref[:, width:] = (high_ref[...].astype(f32) + high_met_ref[...].astype(f32)) * scale


def call(kernel, outs, scratch, limit, scalars, microseconds, *args):
    smem = pl.BlockSpec(memory_space=pltpu.SMEM)
    vmem = pl.BlockSpec(memory_space=pltpu.VMEM)
    return pl.pallas_call(
        kernel,
        out_shape=outs,
        in_specs=[smem] * scalars + [vmem] * (len(args) - scalars),
        out_specs=jax.tree.map(lambda _: vmem, outs),
        scratch_shapes=scratch,
        compiler_params=pltpu.CompilerParams(vmem_limit_bytes=limit << 20),
        cost_estimate=pl.CostEstimate(
            flops=int(microseconds * 0.01 * 1e9),
            bytes_accessed=int(microseconds * 0.01 * 3e6),
            transcendentals=0,
        ),
    )(*args)


def exchange(value, axis, bit):
    size = lax.axis_size(axis)
    return lax.ppermute(value, axis, [(i, i ^ bit) for i in range(size)])


def together(*values):
    return lax.optimization_barrier(values)


def shards(
    features, heights, widths, timesteps, norm_gain, norm_shift, conv_weight, time_weight, cotangent
):
    rows, channels = features.shape
    replicas = lax.axis_size("dp")
    holders = lax.axis_size("fsdp")
    chips = holders // 2
    owned = conv_weight.shape[0]
    out_channels = cotangent.shape[1]
    feature_count = time_weight.shape[1]
    scale = 1.0 / math.sqrt(replicas * holders * rows)
    me = lax.axis_index("fsdp").astype(jnp.int32)[None]
    padded = -(-owned // 16) * 16
    low_taps = 4
    time_width = -(-feature_count // LANES) * LANES
    shape = jax.ShapeDtypeStruct
    affine = jnp.stack([norm_gain, norm_shift])

    roots = [0] + [1 << i for i in range((chips - 1).bit_length())]
    tops = [2 * padded * max(root, 1) for root in roots]
    sent = call(
        functools.partial(prepare_kernel, owned),
        [shape((top + 16 + channels // LANES * rows, LANES), bf16) for top in tops],
        [],
        60,
        4,
        2.0,
        me,
        heights,
        widths,
        timesteps,
        features,
        cotangent,
    )
    returned = channels // LANES * rows + padded
    near, far, normed, results = [sent[0]], [], [], {}
    terms = jnp.zeros((8, channels), f32)

    def slot_and_top(k):
        return k - roots[k.bit_length()], tops[k.bit_length()]

    def convolve(k, me, weights, terms):
        return call(
            functools.partial(conv_kernel, *slot_and_top(k), owned),
            (
                shape((returned, LANES), bf16),
                shape((returned, LANES), bf16),
                shape((8, channels), f32),
            ),
            [pltpu.VMEM((2 * rows, 9 * LANES), f32)],
            16,
            1,
            2.0,
            me,
            near[k],
            far[k],
            normed[k][1],
            *normed[k][3:7],
            weights,
            time_weight,
            terms,
        )

    def join(k, dtype):
        own, other = results[k]
        return call(
            functools.partial(join_kernel, owned),
            shape((returned + padded, LANES), dtype),
            [],
            8,
            0,
            0.1,
            own,
            exchange(other, "fsdp", 1),
        )

    here = me
    for k in range(chips):
        low_bit = k & -k
        if k:
            from_here = sent[k.bit_length()] if k == low_bit else near[k - low_bit]
            near.append(exchange(from_here, "fsdp", 2 * low_bit))
            if k > 1:
                near[k], normed[-1][2], terms = together(near[k], normed[-1][2], terms)
            if k == chips - 1 and k > 1:
                *results[k - 1], terms = convolve(k - 1, here, weights, terms)
            near[k], here, terms = together(near[k], here, terms)
            if k - 1 not in results:
                *results[k - 1], terms = convolve(k - 1, here, weights, terms)
        far.append(exchange(near[k], "fsdp", 1))
        normed.append(
            call(
                functools.partial(norm_kernel, *slot_and_top(k), k == 0, feature_count),
                [
                    shape((9 * padded, 2 * rows), bf16),
                    shape((2 * rows, channels), bf16),
                    shape((2 * IMAGES, padded), f32),
                    shape((2 * IMAGES, feature_count), f32),
                    shape((2 * rows, 9 * rows), bf16),
                    shape((2 * rows, channels), f32),
                    shape((2 * rows, channels), f32),
                ]
                + [shape((rows, channels), f32)] * (k == 0),
                [],
                16,
                1,
                2.0,
                me,
                near[k],
                far[k],
                affine,
            )
        )
        normed[-1] = list(normed[-1])
        if k == 0:
            normed[0][2], here = together(normed[0][2], me)
            weights = call(
                weight_kernel,
                shape((9 * LANES, channels), bf16),
                [],
                16,
                1,
                2.0,
                here,
                conv_weight,
            )
            *results[0], terms = convolve(0, here, weights, terms)
    rstd = normed[0][7]
    joined = [join(k, bf16 if k else f32) for k in range(chips - 1)]
    normed[-1][2], *joined = together(normed[-1][2], *joined)
    low, high = call(
        functools.partial(weight_grad_kernel, chips, low_taps, owned),
        (
            shape((owned, low_taps * channels + time_width), bf16),
            shape((owned, (9 - low_taps) * channels), bf16),
        ),
        [],
        min(60, 6 * chips),
        0,
        1.5,
        *(result[i] for i in range(4) for result in normed),
    )

    bits = [1 << i for i in range((replicas - 1).bit_length())]
    low, high, here = together(low, high, here)
    totals = [low, high]
    received = [exchange(t, "dp", bit) for t, bit in zip(totals, (bits[0], bits[-1]))]

    grads = [joined[0]] + [exchange(joined[k], "fsdp", 2 * k) for k in range(1, chips - 1)]
    last = chips - 1
    *results[last], terms = convolve(last, here, weights, terms)
    part, *grads[1:] = together(join(last, bf16), *grads[1:])
    grads.append(exchange(part, "fsdp", 2 * last))
    for i in range((holders - 1).bit_length()):
        if i == 1:
            received, terms, grads[1:last] = together(received, terms, grads[1:last])
        terms = terms + exchange(terms, "fsdp", 1 << i)

    for step in range(1, len(bits)):
        totals = [
            (t.astype(f32) + r.astype(f32)).astype(bf16) for t, r in zip(totals, received)
        ]
        orders = (bits[step], bits[-1 - step])
        received = [exchange(t, "dp", bit) for t, bit in zip(totals, orders)]
    totals, grads[0], terms = lax.optimization_barrier((totals, grads[0], terms))
    grad_conv, grad_time = call(
        functools.partial(finish_kernel, scale),
        (shape((owned, 9 * channels), f32), shape((owned, feature_count), f32)),
        [],
        16,
        0,
        1.5,
        totals[0],
        received[0],
        totals[1],
        received[1],
    )
    block_out, grad_features = call(
        functools.partial(norm_grad_kernel, owned, chips),
        (shape((rows, out_channels), bf16), shape((rows, channels), bf16)),
        [pltpu.VMEM((out_channels, rows), f32)],
        16,
        3,
        2.5,
        me,
        heights,
        widths,
        *grads,
        normed[0][6],
        rstd,
        affine,
    )
    for bit in bits:
        terms = terms + exchange(terms, "dp", bit)
    return (block_out, grad_features, grad_conv, grad_time, terms[0] * scale, terms[1] * scale)


def solution(mesh):
    rows = P(("dp", "fsdp"), None)
    owned = P("fsdp", None)
    return jax.shard_map(
        shards,
        mesh=mesh,
        in_specs=(rows, rows, rows, rows, P(), P(), owned, owned, rows),
        out_specs=(rows, rows, owned, owned, P(), P()),
        check_vma=False,
    )
```

time: 380 us -> 81.3 us (0.21)
  waiting for transfers between devices: 221 us -> 28.9 us
  blocking collectives: 59.7 us -> 0 us
  local copies, waits for them, and re-layouts: 46 us -> 4.31 us
  Pallas kernels: 0 us -> 25.2 us
  matrix products: 23.4 us -> 0 us
  starting transfers between devices: 0.12 us -> 20.8 us
  other arithmetic: 15 us -> 0.93 us
  between operations: 14.1 us -> 0.84 us
    reduce_scatter x1 -> x0, waiting for transfers between devices: 157 us -> none  [shards(): lax.psum_scatter(full_term, 'fsdp', scatter_dimension=0, tiled=True)]
    psum x1 -> x0, blocking collectives: 38.2 us -> none  [shards(): grad_gain, grad_shift = lax.psum((gain_term, shift_term), ('dp', 'fsdp'))]
    all_gather x1 -> x0, waiting for transfers between devices: 35.6 us -> none  [shards(): lax.all_gather(conv_weight, 'fsdp', axis=0, tiled=True)]
    ppermute x0 -> x23, waiting for transfers between devices: none -> 28.9 us  [exchange(): return lax.ppermute(value, axis, [(i, i ^ bit) for i in range(size)])]
    psum x1 -> x0, waiting for transfers between devices: 28 us -> none  [shards(): joined = lax.psum(reduced, 'dp')]
    pallas_call x0 -> x17, Pallas kernels: none -> 25.2 us  [call(): pl.pallas_call(kernel, out_shape=outs, in_specs=[smem] * scalars + [vmem]...]
    dot_general x15 -> x0, matrix products: 23.4 us -> none  [the longest x1 6.68 us: shards(): jnp.dot(cotan_taps, tap_weight, preferred_element_type=jnp.float32)]
    all_gather x1 -> x0, blocking collectives: 21.4 us -> none  [shards(): lax.all_gather(time_weight, 'fsdp', axis=0, tiled=True)]
  transfers between devices with their start and end apart: 3 -> 23, of which waited for: 3 -> 14; matrix products, arithmetic and copies ran while one was open for 21% -> 3% of each run, Pallas kernels for 0% -> 19%
where the time goes in v2:
time: 81.3 us; the launch traced here: 81 us
  waiting for transfers between devices  28.9 us (36%)
  Pallas kernels  25.2 us (31%)
  starting transfers between devices  20.8 us (26%)
  local copies, waits for them, and re-layouts  4.31 us (5%)
  other arithmetic  0.93 us (1%)
  between operations  0.84 us (1%)
    ppermute x23, waiting for transfers between devices, exchange(): return lax.ppermute(value, axis, [(i, i ^ bit) for i in range(size)])  28.9 us
    pallas_call x17, Pallas kernels, call(): pl.pallas_call(kernel, out_shape=outs, in_specs=[smem] * scalars + [vmem]...  25.2 us
    ppermute x23, starting transfers between devices, exchange(): return lax.ppermute(value, axis, [(i, i ^ bit) for i in range(size)])  20.8 us
    unnamed x10, local copies, waits for them, and re-layouts  2.93 us
  transfers between devices with their start and end apart: 23, of which 14 were waited for; matrix products, arithmetic and copies ran while one was open for 3% of the time, Pallas kernels for 19%

profile of v2, /device:TPU:0, one launch (start us, length us, event | category | flops | bytes accessed | tf_op | source)
XLA Modules:
  0.0 81.0 jit_solution(5377605981858595491)
XLA Ops:
  0.6 2.2 %shard_map.136 = (bf16[848,128]{1,0:T(8,128)(2,1)}, bf16[848,128]{1,0:T(8,128)(2,1)}, bf16[1040,128]{1,0:T(8,128)(2,1)}) custom-call(s32[1]{0:T(128)} %bitcast.me_ref, s32[1,4]{1,0:T(1,128)} %heights_ref.3, s32[1,4]{1,0:T(1,128)} %widths_ref.3, s32[1,4]{1,0:T(1,128)} %times_ref.1, bf16[128,640]{1,0:T(8,128)(2,1)} %features_ref.1, bf16[128,768]{1,0:T(8,128)(2,1)} %cotan_ref.1), custom_call_target="tpu_custom_call" | custom-call | flops 20000000 | bytes 60000 | tf_op jit(solution)/shard_map/pallas_call | solution.py:434
  2.8 0.5 collective-permute-start
  3.2 2.6 %collective-permute-start.1 = (bf16[848,128]{1,0:T(8,128)(2,1)}, bf16[848,128]{1,0:T(8,128)(2,1)S(1)}, u32[]{:S(2)}, u32[]{:S(2)}) collective-permute-start(bf16[848,128]{1,0:T(8,128)(2,1)} %get-tuple-element.94), channel_id=1, source_target_pairs={{0,2},{1,3},{2,0},{3,1},{4,6},{5,7},{6,4},{7,5},{8,10},{9,11},{10,... | collective-permute-start | bytes 651272 | tf_op jit(solution)/shard_map/ppermute | solution.py:451
  5.8 2.6 %collective-permute-start.3 = (bf16[1040,128]{1,0:T(8,128)(2,1)}, bf16[1040,128]{1,0:T(8,128)(2,1)S(1)}, u32[]{:S(2)}, u32[]{:S(2)}) collective-permute-start(bf16[1040,128]{1,0:T(8,128)(2,1)} %get-tuple-element.105), channel_id=1, source_target_pairs={{0,4},{1,5},{2,6},{3,7},{4,0},{5,1},{6,2},{7,3},{8,12},{9,13},{10,... | collective-permute-start | bytes 798728 | tf_op jit(solution)/shard_map/ppermute | solution.py:451
  8.4 0.7 stack.9
  9.1 0.7 stack.10
  9.8 0.9 %copy-done.2 = bf16[848,128]{1,0:T(8,128)(2,1)S(1)} copy-done((bf16[848,128]{1,0:T(8,128)(2,1)S(1)}, bf16[848,128]{1,0:T(8,128)(2,1)}, u32[]{:S(2)}) %copy-start.2) | copy-done | bytes 217112
  10.7 2.4 %shard_map.137 = (bf16[864,256]{1,0:T(8,128)(2,1)S(1)}, bf16[256,640]{1,0:T(8,128)(2,1)S(1)}, f32[8,96]{1,0:T(8,128)S(1)}, f32[8,320]{1,0:T(8,128)S(1)}, bf16[25...) custom-call(s32[1]{0:T(128)} %bitcast.me_ref, ...), custom_call_target="tpu_custom_call" | custom-call | flops 20000000 | bytes 60000 | tf_op jit(solution)/shard_map/pallas_call | solution.py:434
  13.2 1.2 %copy-done.1 = bf16[96,5760]{1,0:T(8,128)(2,1)S(1)} copy-done((bf16[96,5760]{1,0:T(8,128)(2,1)S(1)}, bf16[96,5760]{1,0:T(8,128)(2,1)}, u32[]{:S(2)}) %copy-start.1) | copy-done | bytes 1105944
  14.6 0.8 copy-done
  15.3 1.9 %shard_map.139 = (bf16[736,128]{1,0:T(8,128)(2,1)S(1)}, bf16[736,128]{1,0:T(8,128)(2,1)S(1)}, f32[8,640]{1,0:T(8,128)S(1)}) custom-call(s32[1]{0:T(128)} %bitcast.me_ref, bf16[848,128]{1,0:T(8,128)(2,1)S(1)} %copy-done.2, bf16[848,128]{1,0:T(8,128)(2,1)S(1)} %collective-permute-done.far_ref, bf16[256,640]{1,0:T(8,128)(2,1)S(1)} %get-tuple-element.97.act_ref.refs_4_, ...), custom_call_target="tpu_custom_call" | custom-call | flops 20000000 | bytes 60000 | tf_op jit(solution)/shard_map/pallas_call | solution.py:434
  17.3 1.5 %collective-permute-done.2.far_ref = bf16[848,128]{1,0:T(8,128)(2,1)S(1)} collective-permute-done((bf16[848,128]{1,0:T(8,128)(2,1)S(1)}, bf16[848,128]{1,0:T(8,128)(2,1)S(1)}, u32[]{:S(2)}, u32[]{:S(2)}) %collective-permute-start.2) | collective-permute-done | bytes 217120 | tf_op jit(solution)/shard_map/ppermute | solution.py:451
  18.7 2.4 %shard_map.140 = (bf16[864,256]{1,0:T(8,128)(2,1)S(1)}, bf16[256,640]{1,0:T(8,128)(2,1)S(1)}, f32[8,96]{1,0:T(8,128)S(1)}, f32[8,320]{1,0:T(8,128)S(1)}, bf16[25...) custom-call(s32[1]{0:T(128)} %bitcast.me_ref, ...), custom_call_target="tpu_custom_call" | custom-call | flops 20000000 | bytes 60000 | tf_op jit(solution)/shard_map/pallas_call | solution.py:434
  21.4 0.5 collective-permute-start.5
  21.8 1.9 %shard_map.142 = (bf16[736,128]{1,0:T(8,128)(2,1)S(1)}, bf16[736,128]{1,0:T(8,128)(2,1)S(1)}, f32[8,640]{1,0:T(8,128)S(1)}) custom-call(s32[1]{0:T(128)} %bitcast.me_ref, bf16[848,128]{1,0:T(8,128)(2,1)S(1)} %collective-permute-done.1.near_ref, bf16[848,128]{1,0:T(8,128)(2,1)S(1)} %collective-permute-done.2.far_ref, ...), custom_call_target="tpu_custom_call" | custom-call | flops 20000000 | bytes 60000 | tf_op jit(solution)/shard_map/pallas_call | solution.py:434
  23.7 2.4 %shard_map.141 = (bf16[864,256]{1,0:T(8,128)(2,1)S(1)}, bf16[256,640]{1,0:T(8,128)(2,1)S(1)}, f32[8,96]{1,0:T(8,128)S(1)}, f32[8,320]{1,0:T(8,128)S(1)}, bf16[25...) custom-call(s32[1]{0:T(128)} %bitcast.me_ref, ...), custom_call_target="tpu_custom_call" | custom-call | flops 20000000 | bytes 60000 | tf_op jit(solution)/shard_map/pallas_call | solution.py:434
  26.2 3.9 %collective-permute-done.5.near_ref = bf16[1040,128]{1,0:T(8,128)(2,1)S(1)} collective-permute-done((bf16[1040,128]{1,0:T(8,128)(2,1)S(1)}, bf16[1040,128]{1,0:T(8,128)(2,1)S(1)}, u32[]{:S(2)}, u32[]{:S(2)}) %collective-permute-start.5) | collective-permute-done | bytes 266272 | tf_op jit(solution)/shard_map/ppermute | solution.py:451
  30.1 1.8 %shard_map.143 = (bf16[736,128]{1,0:T(8,128)(2,1)S(1)}, bf16[736,128]{1,0:T(8,128)(2,1)S(1)}, f32[8,640]{1,0:T(8,128)S(1)}) custom-call(s32[1]{0:T(128)} %bitcast.me_ref, bf16[1040,128]{1,0:T(8,128)(2,1)S(1)} %collective-permute-done.3.near_ref, bf16[1040,128]{1,0:T(8,128)(2,1)S(1)} %collective-permute-done.4.far_ref, ...), custom_call_target="tpu_custom_call" | custom-call | flops 20000000 | bytes 60000 | tf_op jit(solution)/shard_map/pallas_call | solution.py:434
  31.9 0.3 collective-permute-start.6
  32.2 0.5 collective-permute-start.7
  32.7 0.4 collective-permute-start.9
  33.2 0.8 collective-permute-done.7.met_ref
  34.3 0.2 collective-permute-done.9.met_ref
  34.6 2.4 %shard_map.144 = (bf16[864,256]{1,0:T(8,128)(2,1)S(1)}, bf16[256,640]{1,0:T(8,128)(2,1)S(1)}, f32[8,96]{1,0:T(8,128)S(1)}, f32[8,320]{1,0:T(8,128)S(1)}, bf16[25...) custom-call(s32[1]{0:T(128)} %bitcast.me_ref, ...), custom_call_target="tpu_custom_call" | custom-call | flops 20000000 | bytes 60000 | tf_op jit(solution)/shard_map/pallas_call | solution.py:434
  37.0 1.6 %shard_map.148 = (bf16[96,2944]{1,0:T(8,128)(2,1)S(1)}, bf16[96,3200]{1,0:T(8,128)(2,1)S(1)}) custom-call(bf16[864,256]{1,0:T(8,128)(2,1)S(1)} %get-tuple-element.93.refs_0_, bf16[864,256]{1,0:T(8,128)(2,1)S(1)} %get-tuple-element.104.refs_1_, bf16[864,256]{1,0:T(8,128)(2,1)S(1)} %get-tuple-element.112.refs_2_, ...), custom_call_target="tpu_custom_call" | custom-call | flops 15000000 | bytes 45000 | tf_op jit(solution)/shard_map/pallas_call | solution.py:434
  38.6 1.6 %collective-permute-start.11 = (bf16[96,3200]{1,0:T(8,128)(2,1)S(1)}, bf16[96,3200]{1,0:T(8,128)(2,1)S(1)}, u32[]{:S(2)}, u32[]{:S(2)}) collective-permute-start(bf16[96,3200]{1,0:T(8,128)(2,1)S(1)} %get-tuple-element.149), channel_id=1, source_target_pairs={{0,16},{8,24},{16,0},{24,8},{1,17},{9,25},{17,1},{25,9},{2,18},{10... | collective-permute-start | bytes 1843208 | tf_op jit(solution)/shard_map/ppermute | solution.py:451
  40.2 1.5 %collective-permute-start.10 = (bf16[96,2944]{1,0:T(8,128)(2,1)S(1)}, bf16[96,2944]{1,0:T(8,128)(2,1)S(1)}, u32[]{:S(2)}, u32[]{:S(2)}) collective-permute-start(bf16[96,2944]{1,0:T(8,128)(2,1)S(1)} %get-tuple-element.148), channel_id=1, source_target_pairs={{0,8},{8,0},{16,24},{24,16},{1,9},{9,1},{17,25},{25,17},{2,10},{10... | collective-permute-start | bytes 1695752 | tf_op jit(solution)/shard_map/ppermute | solution.py:451
  41.7 0.4 collective-permute-start.14
  42.1 2.5 %collective-permute-start.15 = (bf16[832,128]{1,0:T(8,128)(2,1)S(1)}, bf16[832,128]{1,0:T(8,128)(2,1)S(1)}, u32[]{:S(2)}, u32[]{:S(2)}) collective-permute-start(bf16[832,128]{1,0:T(8,128)(2,1)S(1)} %shard_map.147), channel_id=1, source_target_pairs={{0,4},{1,5},{2,6},{3,7},{4,0},{5,1},{6,2},{7,3},{8,12},{9,13},{10,... | collective-permute-start | bytes 638984 | tf_op jit(solution)/shard_map/ppermute | solution.py:451
  44.7 1.9 %shard_map.149 = (bf16[736,128]{1,0:T(8,128)(2,1)S(1)}, bf16[736,128]{1,0:T(8,128)(2,1)S(1)}, f32[8,640]{1,0:T(8,128)S(1)}) custom-call(s32[1]{0:T(128)} %bitcast.me_ref, bf16[1040,128]{1,0:T(8,128)(2,1)S(1)} %collective-permute-done.5.near_ref, bf16[1040,128]{1,0:T(8,128)(2,1)S(1)} %collective-permute-done.6.far_ref, ...), custom_call_target="tpu_custom_call" | custom-call | flops 20000000 | bytes 60000 | tf_op jit(solution)/shard_map/pallas_call | solution.py:434
  46.6 1.2 %collective-permute-done.12 = f32[8,640]{1,0:T(8,128)S(1)} collective-permute-done((f32[8,640]{1,0:T(8,128)S(1)}, f32[8,640]{1,0:T(8,128)S(1)}, u32[]{:S(2)}, u32[]{:S(2)}) %collective-permute-start.12) | collective-permute-done | bytes 20512 | tf_op jit(solution)/shard_map/ppermute | solution.py:451
  48.0 1.3 %collective-permute-done.13.met_ref = bf16[736,128]{1,0:T(8,128)(2,1)S(1)} collective-permute-done((bf16[736,128]{1,0:T(8,128)(2,1)S(1)}, bf16[736,128]{1,0:T(8,128)(2,1)S(1)}, u32[]{:S(2)}, u32[]{:S(2)}) %collective-permute-start.13) | collective-permute-done | bytes 188448 | tf_op jit(solution)/shard_map/ppermute | solution.py:451
  49.3 3.4 %collective-permute-done.14.refs_1_ = bf16[832,128]{1,0:T(8,128)(2,1)S(1)} collective-permute-done((bf16[832,128]{1,0:T(8,128)(2,1)S(1)}, bf16[832,128]{1,0:T(8,128)(2,1)S(1)}, u32[]{:S(2)}, u32[]{:S(2)}) %collective-permute-start.14) | collective-permute-done | bytes 213024 | tf_op jit(solution)/shard_map/ppermute | solution.py:451
  52.7 1.4 %collective-permute-done.15.refs_2_ = bf16[832,128]{1,0:T(8,128)(2,1)S(1)} collective-permute-done((bf16[832,128]{1,0:T(8,128)(2,1)S(1)}, bf16[832,128]{1,0:T(8,128)(2,1)S(1)}, u32[]{:S(2)}, u32[]{:S(2)}) %collective-permute-start.15) | collective-permute-done | bytes 213024 | tf_op jit(solution)/shard_map/ppermute | solution.py:451
  54.1 0.7 collective-permute-done.10
  54.9 1.6 %collective-permute-start.20 = (bf16[96,3200]{1,0:T(8,128)(2,1)S(1)}, bf16[96,3200]{1,0:T(8,128)(2,1)S(1)}, u32[]{:S(2)}, u32[]{:S(2)}) collective-permute-start(bf16[96,3200]{1,0:T(8,128)(2,1)S(1)} %add_convert_fusion.high_ref), channel_id=1, source_target_pairs={{0,8},{8,0},{16,24},{24,16},{1,9},{9,1},{17,25},{25,17},{2,10},{10... | collective-permute-start | bytes 1843208 | tf_op jit(solution)/shard_map/ppermute | solution.py:451
  56.6 1.4 %collective-permute-start.19 = (bf16[96,2944]{1,0:T(8,128)(2,1)S(1)}, bf16[96,2944]{1,0:T(8,128)(2,1)S(1)}, u32[]{:S(2)}, u32[]{:S(2)}) collective-permute-start(bf16[96,2944]{1,0:T(8,128)(2,1)S(1)} %add_convert_fusion.1.low_ref), channel_id=1, source_target_pairs={{0,16},{8,24},{16,0},{24,8},{1,17},{9,25},{17,1},{25,9},{2,18},{10... | collective-permute-start | bytes 1695752 | tf_op jit(solution)/shard_map/ppermute | solution.py:451
  58.0 2.4 %collective-permute-start.18 = (bf16[832,128]{1,0:T(8,128)(2,1)S(1)}, bf16[832,128]{1,0:T(8,128)(2,1)S(1)}, u32[]{:S(2)}, u32[]{:S(2)}) collective-permute-start(bf16[832,128]{1,0:T(8,128)(2,1)S(1)} %shard_map.150), channel_id=1, source_target_pairs={{0,6},{1,7},{2,4},{3,5},{4,2},{5,3},{6,0},{7,1},{8,14},{9,15},{10,... | collective-permute-start | bytes 638984 | tf_op jit(solution)/shard_map/ppermute | solution.py:451
  60.5 5.8 %collective-permute-done.16 = f32[8,640]{1,0:T(8,128)S(1)} collective-permute-done((f32[8,640]{1,0:T(8,128)S(1)}, f32[8,640]{1,0:T(8,128)S(1)}, u32[]{:S(2)}, u32[]{:S(2)}) %collective-permute-start.16) | collective-permute-done | bytes 20512 | tf_op jit(solution)/shard_map/ppermute | solution.py:451
  66.3 0.5 collective-permute-start.17
  66.8 4.4 %collective-permute-done.17 = f32[8,640]{1,0:T(8,128)S(1)} collective-permute-done((f32[8,640]{1,0:T(8,128)S(1)}, f32[8,640]{1,0:T(8,128)S(1)}, u32[]{:S(2)}, u32[]{:S(2)}) %collective-permute-start.17) | collective-permute-done | bytes 20512 | tf_op jit(solution)/shard_map/ppermute | solution.py:451
  71.2 0.5 collective-permute-start.21
  71.7 3.2 %collective-permute-done.21 = f32[8,640]{1,0:T(8,128)S(1)} collective-permute-done((f32[8,640]{1,0:T(8,128)S(1)}, f32[8,640]{1,0:T(8,128)S(1)}, u32[]{:S(2)}, u32[]{:S(2)}) %collective-permute-start.21) | collective-permute-done | bytes 20512 | tf_op jit(solution)/shard_map/ppermute | solution.py:451
  75.0 0.5 collective-permute-start.22
  75.5 2.3 %shard_map.151 = (bf16[128,768]{1,0:T(8,128)(2,1)}, bf16[128,640]{1,0:T(8,128)(2,1)}) custom-call(s32[1]{0:T(128)} %bitcast.me_ref, s32[1,4]{1,0:T(1,128)S(1)} %copy-done.3, s32[1,4]{1,0:T(1,128)S(1)} %copy-done.4, f32[832,128]{1,0:T(8,128)S(1)} %shard_map.145.refs_0_, bf16[832,128]{1,0:T(8,128)(2,1)S(1)} %collective-permute-done.14.refs_1_, ...), custom_call_target="tpu_custom_call" | custom-call | flops 25000000 | bytes 75000 | tf_op jit(solution)/shard_map/pallas_call | solution.py:434
  77.8 0.9 %collective-permute-done.22 = f32[8,640]{1,0:T(8,128)S(1)} collective-permute-done((f32[8,640]{1,0:T(8,128)S(1)}, f32[8,640]{1,0:T(8,128)S(1)}, u32[]{:S(2)}, u32[]{:S(2)}) %collective-permute-start.22) | collective-permute-done | bytes 20512 | tf_op jit(solution)/shard_map/ppermute | solution.py:451
  78.7 0.6 fusion
  79.4 1.7 %shard_map.152 = (f32[96,5760]{1,0:T(8,128)}, f32[96,320]{1,0:T(8,128)}) custom-call(bf16[96,2944]{1,0:T(8,128)(2,1)S(1)} %add_convert_fusion.1.low_ref, bf16[96,2944]{1,0:T(8,128)(2,1)S(1)} %collective-permute-done.19.low_met_ref, bf16[96,3200]{1,0:T(8,128)(2,1)S(1)} %add_convert_fusion.high_ref, bf16[96,3200]{1,0:T(8,128)(2,1)S(1)} %collective-permute-done.20.high_met_ref), custom_call_target="tpu_custom_call" | custom-call | flops 15000000 | bytes 45000 | tf_op jit(solution)/shard_map/pallas_call | solution.py:434
  (37 shorter events, 1.5 us)
Async XLA Ops:
  2.8 7.0 %collective-permute-start = (bf16[848,128]{1,0:T(8,128)(2,1)}, bf16[848,128]{1,0:T(8,128)(2,1)S(1)}, u32[]{:S(2)}, u32[]{:S(2)}) collective-permute-start(bf16[848,128]{1,0:T(8,128)(2,1)} %get-tuple-element.92.near_ref), channel_id=1, source_target_pairs={{0,1},{1,0},{2,3},{3,2},{4,5},{5,4},{6,7},{7,6},{8,9},{9,8},{10,11... | collective-permute-start | bytes 651272 | tf_op jit(solution)/shard_map/ppermute | solution.py:451
  3.2 13.9 %collective-permute-start.1 = (bf16[848,128]{1,0:T(8,128)(2,1)}, bf16[848,128]{1,0:T(8,128)(2,1)S(1)}, u32[]{:S(2)}, u32[]{:S(2)}) collective-permute-start(bf16[848,128]{1,0:T(8,128)(2,1)} %get-tuple-element.94), channel_id=1, source_target_pairs={{0,2},{1,3},{2,0},{3,1},{4,6},{5,7},{6,4},{7,5},{8,10},{9,11},{10,... | collective-permute-start | bytes 651272 | tf_op jit(solution)/shard_map/ppermute | solution.py:451
  5.8 15.4 %collective-permute-start.3 = (bf16[1040,128]{1,0:T(8,128)(2,1)}, bf16[1040,128]{1,0:T(8,128)(2,1)S(1)}, u32[]{:S(2)}, u32[]{:S(2)}) collective-permute-start(bf16[1040,128]{1,0:T(8,128)(2,1)} %get-tuple-element.105), channel_id=1, source_target_pairs={{0,4},{1,5},{2,6},{3,7},{4,0},{5,1},{6,2},{7,3},{8,12},{9,13},{10,... | collective-permute-start | bytes 798728 | tf_op jit(solution)/shard_map/ppermute | solution.py:451
  9.8 0.9 %copy-start.2 = (bf16[848,128]{1,0:T(8,128)(2,1)S(1)}, bf16[848,128]{1,0:T(8,128)(2,1)}, u32[]{:S(2)}) copy-start(bf16[848,128]{1,0:T(8,128)(2,1)} %get-tuple-element.92.near_ref) | copy-start | bytes 651268
  13.2 1.2 %copy-start.1 = (bf16[96,5760]{1,0:T(8,128)(2,1)S(1)}, bf16[96,5760]{1,0:T(8,128)(2,1)}, u32[]{:S(2)}) copy-start(bf16[96,5760]{1,0:T(8,128)(2,1)} %conv_ref.1) | copy-start | bytes 3317764
  14.4 0.9 %copy-start = (bf16[96,320]{1,0:T(8,128)(2,1)S(1)}, bf16[96,320]{1,0:T(8,128)(2,1)}, u32[]{:S(2)}) copy-start(bf16[96,320]{1,0:T(8,128)(2,1)} %time_ref.7) | copy-start | bytes 184324
  17.2 1.5 %collective-permute-start.2 = (bf16[848,128]{1,0:T(8,128)(2,1)S(1)}, bf16[848,128]{1,0:T(8,128)(2,1)S(1)}, u32[]{:S(2)}, u32[]{:S(2)}) collective-permute-start(bf16[848,128]{1,0:T(8,128)(2,1)S(1)} %collective-permute-done.1.near_ref), channel_id=1, source_target_pairs={{0,1},{1,0},{2,3},{3,2},{4,5},{5,4},{6,7},{7,6},{8,9},{9,8},{10,11... | collective-permute-start | bytes 651272 | tf_op jit(solution)/shard_map/ppermute | solution.py:451
  21.2 2.5 %collective-permute-start.4 = (bf16[1040,128]{1,0:T(8,128)(2,1)S(1)}, bf16[1040,128]{1,0:T(8,128)(2,1)S(1)}, u32[]{:S(2)}, u32[]{:S(2)}) collective-permute-start(bf16[1040,128]{1,0:T(8,128)(2,1)S(1)} %collective-permute-done.3.near_ref), channel_id=1, source_target_pairs={{0,1},{1,0},{2,3},{3,2},{4,5},{5,4},{6,7},{7,6},{8,9},{9,8},{10,11... | collective-permute-start | bytes 798728 | tf_op jit(solution)/shard_map/ppermute | solution.py:451
  21.4 8.7 %collective-permute-start.5 = (bf16[1040,128]{1,0:T(8,128)(2,1)S(1)}, bf16[1040,128]{1,0:T(8,128)(2,1)S(1)}, u32[]{:S(2)}, u32[]{:S(2)}) collective-permute-start(bf16[1040,128]{1,0:T(8,128)(2,1)S(1)} %collective-permute-done.3.near_ref), channel_id=1, source_target_pairs={{0,2},{1,3},{2,0},{3,1},{4,6},{5,7},{6,4},{7,5},{8,10},{9,11},{10,... | collective-permute-start | bytes 798728 | tf_op jit(solution)/shard_map/ppermute | solution.py:451
  31.9 2.6 %collective-permute-start.6 = (bf16[1040,128]{1,0:T(8,128)(2,1)S(1)}, bf16[1040,128]{1,0:T(8,128)(2,1)S(1)}, u32[]{:S(2)}, u32[]{:S(2)}) collective-permute-start(bf16[1040,128]{1,0:T(8,128)(2,1)S(1)} %collective-permute-done.5.near_ref), channel_id=1, source_target_pairs={{0,1},{1,0},{2,3},{3,2},{4,5},{5,4},{6,7},{7,6},{8,9},{9,8},{10,11... | collective-permute-start | bytes 798728 | tf_op jit(solution)/shard_map/ppermute | solution.py:451
  32.2 1.8 %collective-permute-start.7 = (bf16[736,128]{1,0:T(8,128)(2,1)S(1)}, bf16[736,128]{1,0:T(8,128)(2,1)S(1)}, u32[]{:S(2)}, u32[]{:S(2)}) collective-permute-start(bf16[736,128]{1,0:T(8,128)(2,1)S(1)} %get-tuple-element.138), channel_id=1, source_target_pairs={{0,1},{1,0},{2,3},{3,2},{4,5},{5,4},{6,7},{7,6},{8,9},{9,8},{10,11... | collective-permute-start | bytes 565256 | tf_op jit(solution)/shard_map/ppermute | solution.py:451
  32.7 1.6 %collective-permute-start.8 = (bf16[736,128]{1,0:T(8,128)(2,1)S(1)}, bf16[736,128]{1,0:T(8,128)(2,1)S(1)}, u32[]{:S(2)}, u32[]{:S(2)}) collective-permute-start(bf16[736,128]{1,0:T(8,128)(2,1)S(1)} %get-tuple-element.140), channel_id=1, source_target_pairs={{0,1},{1,0},{2,3},{3,2},{4,5},{5,4},{6,7},{7,6},{8,9},{9,8},{10,11... | collective-permute-start | bytes 565256 | tf_op jit(solution)/shard_map/ppermute | solution.py:451
  32.7 1.8 %collective-permute-start.9 = (bf16[736,128]{1,0:T(8,128)(2,1)S(1)}, bf16[736,128]{1,0:T(8,128)(2,1)S(1)}, u32[]{:S(2)}, u32[]{:S(2)}) collective-permute-start(bf16[736,128]{1,0:T(8,128)(2,1)S(1)} %get-tuple-element.142), channel_id=1, source_target_pairs={{0,1},{1,0},{2,3},{3,2},{4,5},{5,4},{6,7},{7,6},{8,9},{9,8},{10,11... | collective-permute-start | bytes 565256 | tf_op jit(solution)/shard_map/ppermute | solution.py:451
  38.6 16.2 %collective-permute-start.11 = (bf16[96,3200]{1,0:T(8,128)(2,1)S(1)}, bf16[96,3200]{1,0:T(8,128)(2,1)S(1)}, u32[]{:S(2)}, u32[]{:S(2)}) collective-permute-start(bf16[96,3200]{1,0:T(8,128)(2,1)S(1)} %get-tuple-element.149), channel_id=1, source_target_pairs={{0,16},{8,24},{16,0},{24,8},{1,17},{9,25},{17,1},{25,9},{2,18},{10... | collective-permute-start | bytes 1843208 | tf_op jit(solution)/shard_map/ppermute | solution.py:451
  40.2 14.6 %collective-permute-start.10 = (bf16[96,2944]{1,0:T(8,128)(2,1)S(1)}, bf16[96,2944]{1,0:T(8,128)(2,1)S(1)}, u32[]{:S(2)}, u32[]{:S(2)}) collective-permute-start(bf16[96,2944]{1,0:T(8,128)(2,1)S(1)} %get-tuple-element.148), channel_id=1, source_target_pairs={{0,8},{8,0},{16,24},{24,16},{1,9},{9,1},{17,25},{25,17},{2,10},{10... | collective-permute-start | bytes 1695752 | tf_op jit(solution)/shard_map/ppermute | solution.py:451
  41.7 11.0 %collective-permute-start.14 = (bf16[832,128]{1,0:T(8,128)(2,1)S(1)}, bf16[832,128]{1,0:T(8,128)(2,1)S(1)}, u32[]{:S(2)}, u32[]{:S(2)}) collective-permute-start(bf16[832,128]{1,0:T(8,128)(2,1)S(1)} %shard_map.146), channel_id=1, source_target_pairs={{0,2},{1,3},{2,0},{3,1},{4,6},{5,7},{6,4},{7,5},{8,10},{9,11},{10,... | collective-permute-start | bytes 638984 | tf_op jit(solution)/shard_map/ppermute | solution.py:451
  42.1 12.0 %collective-permute-start.15 = (bf16[832,128]{1,0:T(8,128)(2,1)S(1)}, bf16[832,128]{1,0:T(8,128)(2,1)S(1)}, u32[]{:S(2)}, u32[]{:S(2)}) collective-permute-start(bf16[832,128]{1,0:T(8,128)(2,1)S(1)} %shard_map.147), channel_id=1, source_target_pairs={{0,4},{1,5},{2,6},{3,7},{4,0},{5,1},{6,2},{7,3},{8,12},{9,13},{10,... | collective-permute-start | bytes 638984 | tf_op jit(solution)/shard_map/ppermute | solution.py:451
  46.6 1.3 %collective-permute-start.12 = (f32[8,640]{1,0:T(8,128)S(1)}, f32[8,640]{1,0:T(8,128)S(1)}, u32[]{:S(2)}, u32[]{:S(2)}) collective-permute-start(f32[8,640]{1,0:T(8,128)S(1)} %get-tuple-element.155), channel_id=1, source_target_pairs={{0,1},{1,0},{2,3},{3,2},{4,5},{5,4},{6,7},{7,6},{8,9},{9,8},{10,11... | collective-permute-start | bytes 61448 | tf_op jit(solution)/shard_map/ppermute | solution.py:451
  47.8 1.4 %collective-permute-start.13 = (bf16[736,128]{1,0:T(8,128)(2,1)S(1)}, bf16[736,128]{1,0:T(8,128)(2,1)S(1)}, u32[]{:S(2)}, u32[]{:S(2)}) collective-permute-start(bf16[736,128]{1,0:T(8,128)(2,1)S(1)} %get-tuple-element.157), channel_id=1, source_target_pairs={{0,1},{1,0},{2,3},{3,2},{4,5},{5,4},{6,7},{7,6},{8,9},{9,8},{10,11... | collective-permute-start | bytes 565256 | tf_op jit(solution)/shard_map/ppermute | solution.py:451
  54.9 20.6 %copy-start.3 = (s32[1,4]{1,0:T(1,128)S(1)}, s32[1,4]{1,0:T(1,128)}, u32[]{:S(2)}) copy-start(s32[1,4]{1,0:T(1,128)} %heights_ref.3) | copy-start | bytes 52
  54.9 20.6 %copy-start.4 = (s32[1,4]{1,0:T(1,128)S(1)}, s32[1,4]{1,0:T(1,128)}, u32[]{:S(2)}) copy-start(s32[1,4]{1,0:T(1,128)} %widths_ref.3) | copy-start | bytes 52
  54.9 24.4 %collective-permute-start.20 = (bf16[96,3200]{1,0:T(8,128)(2,1)S(1)}, bf16[96,3200]{1,0:T(8,128)(2,1)S(1)}, u32[]{:S(2)}, u32[]{:S(2)}) collective-permute-start(bf16[96,3200]{1,0:T(8,128)(2,1)S(1)} %add_convert_fusion.high_ref), channel_id=1, source_target_pairs={{0,8},{8,0},{16,24},{24,16},{1,9},{9,1},{17,25},{25,17},{2,10},{10... | collective-permute-start | bytes 1843208 | tf_op jit(solution)/shard_map/ppermute | solution.py:451
  56.6 22.7 %collective-permute-start.19 = (bf16[96,2944]{1,0:T(8,128)(2,1)S(1)}, bf16[96,2944]{1,0:T(8,128)(2,1)S(1)}, u32[]{:S(2)}, u32[]{:S(2)}) collective-permute-start(bf16[96,2944]{1,0:T(8,128)(2,1)S(1)} %add_convert_fusion.1.low_ref), channel_id=1, source_target_pairs={{0,16},{8,24},{16,0},{24,8},{1,17},{9,25},{17,1},{25,9},{2,18},{10... | collective-permute-start | bytes 1695752 | tf_op jit(solution)/shard_map/ppermute | solution.py:451
  58.0 17.4 %collective-permute-start.18 = (bf16[832,128]{1,0:T(8,128)(2,1)S(1)}, bf16[832,128]{1,0:T(8,128)(2,1)S(1)}, u32[]{:S(2)}, u32[]{:S(2)}) collective-permute-start(bf16[832,128]{1,0:T(8,128)(2,1)S(1)} %shard_map.150), channel_id=1, source_target_pairs={{0,6},{1,7},{2,4},{3,5},{4,2},{5,3},{6,0},{7,1},{8,14},{9,15},{10,... | collective-permute-start | bytes 638984 | tf_op jit(solution)/shard_map/ppermute | solution.py:451
  60.5 5.8 %collective-permute-start.16 = (f32[8,640]{1,0:T(8,128)S(1)}, f32[8,640]{1,0:T(8,128)S(1)}, u32[]{:S(2)}, u32[]{:S(2)}) collective-permute-start(f32[8,640]{1,0:T(8,128)S(1)} %add.21), channel_id=1, source_target_pairs={{0,2},{1,3},{2,0},{3,1},{4,6},{5,7},{6,4},{7,5},{8,10},{9,11},{10,... | collective-permute-start | bytes 61448 | tf_op jit(solution)/shard_map/ppermute | solution.py:451
  66.3 4.9 %collective-permute-start.17 = (f32[8,640]{1,0:T(8,128)S(1)}, f32[8,640]{1,0:T(8,128)S(1)}, u32[]{:S(2)}, u32[]{:S(2)}) collective-permute-start(f32[8,640]{1,0:T(8,128)S(1)} %add.24), channel_id=1, source_target_pairs={{0,4},{1,5},{2,6},{3,7},{4,0},{5,1},{6,2},{7,3},{8,12},{9,13},{10,... | collective-permute-start | bytes 61448 | tf_op jit(solution)/shard_map/ppermute | solution.py:451
  71.2 3.8 %collective-permute-start.21 = (f32[8,640]{1,0:T(8,128)S(1)}, f32[8,640]{1,0:T(8,128)S(1)}, u32[]{:S(2)}, u32[]{:S(2)}) collective-permute-start(f32[8,640]{1,0:T(8,128)S(1)} %add.25), channel_id=1, source_target_pairs={{0,8},{8,0},{16,24},{24,16},{1,9},{9,1},{17,25},{25,17},{2,10},{10... | collective-permute-start | bytes 61448 | tf_op jit(solution)/shard_map/ppermute | solution.py:451
  75.0 3.8 %collective-permute-start.22 = (f32[8,640]{1,0:T(8,128)S(1)}, f32[8,640]{1,0:T(8,128)S(1)}, u32[]{:S(2)}, u32[]{:S(2)}) collective-permute-start(f32[8,640]{1,0:T(8,128)S(1)} %add.26), channel_id=1, source_target_pairs={{0,16},{8,24},{16,0},{24,8},{1,17},{9,25},{17,1},{25,9},{2,18},{10... | collective-permute-start | bytes 61448 | tf_op jit(solution)/shard_map/ppermute | solution.py:451

commit v3 on v2

--- a/solution.py
+++ b/solution.py
@@ -11,6 +11,7 @@
 GROUPS = 32
 IMAGES = 4
 LANES = 128
+TERM_ROWS = 32
 
 bf16 = jnp.bfloat16
 f32 = jnp.float32
@@ -151,21 +152,6 @@
         first = max(2 * first, 1)
 
 
-def weight_kernel(me_ref, conv_ref, out_ref):
-    owned = conv_ref.shape[0]
-    channels = out_ref.shape[1]
-    padded = -(-owned // 16) * 16
-    for t in range(9):
-        part = conv_ref[:, t * channels : (t + 1) * channels]
-        if padded > owned:
-            part = jnp.concatenate([part, jnp.zeros((padded - owned, channels), bf16)], axis=0)
-        out_ref[t * LANES : t * LANES + padded, :] = part
-        if padded < LANES:
-            out_ref[t * LANES + padded : (t + 1) * LANES, :] = jnp.zeros(
-                (LANES - padded, channels), bf16
-            )
-
-
 def chunk_sums(members, chunks, inverses):
     out = []
     for chunk in chunks:
@@ -184,15 +170,84 @@
     return bounds_of(sizes[:IMAGES], sizes[IMAGES:]), times
 
 
-def norm_kernel(
+def first_kernel(slot, top, owned, me_ref, near_ref, far_ref, gain_ref, shift_ref, *refs):
+    conv_ref, time_ref, own_ref, other_ref, terms_ref, turned_ref, act_ref, sums_ref, embed_ref = refs[:9]
+    normed_ref, rstd_ref, weights_ref, held_ref, taps, slopes, norms, product, copied = refs[9:]
+    padded = conv_ref.shape[0]
+    width = weights_ref.shape[1]
+    copies = [pltpu.make_async_copy(time_ref, held_ref, copied.at[9])]
+    for t in range(9):
+        copies.append(
+            pltpu.make_async_copy(
+                conv_ref.at[:, pl.ds(t * width, width)],
+                weights_ref.at[pl.ds(t * LANES, padded), :],
+                copied.at[t],
+            )
+        )
+        if padded < LANES:
+            weights_ref[t * LANES + padded : (t + 1) * LANES, :] = jnp.zeros(
+                (LANES - padded, width), bf16
+            )
+    for copy in copies:
+        copy.start()
+    blocks = me_ref, near_ref, far_ref
+    norm_part(
+        slot, top, time_ref.shape[1], *blocks, gain_ref, shift_ref, turned_ref, act_ref, sums_ref,
+        embed_ref, taps, slopes, norms, rstd_ref,
+    )
+    normed_ref[...] = norms[: normed_ref.shape[0], :]
+    for copy in copies:
+        copy.wait()
+    conv_part(
+        slot, top, owned, *blocks, act_ref, embed_ref, taps, slopes, norms, weights_ref, held_ref,
+        None, own_ref, other_ref, terms_ref, product,
+    )
+
+
+def pair_kernel(
     slot,
     top,
-    keep,
+    owned,
+    me_ref,
+    near_ref,
+    far_ref,
+    gain_ref,
+    shift_ref,
+    weights_ref,
+    time_ref,
+    before_ref,
+    own_ref,
+    other_ref,
+    terms_ref,
+    turned_ref,
+    act_ref,
+    sums_ref,
+    embed_ref,
+    taps,
+    slopes,
+    norms,
+    product,
+):
+    blocks = me_ref, near_ref, far_ref
+    norm_part(
+        slot, top, time_ref.shape[1], *blocks, gain_ref, shift_ref, turned_ref, act_ref, sums_ref,
+        embed_ref, taps, slopes, norms, None,
+    )
+    conv_part(
+        slot, top, owned, *blocks, act_ref, embed_ref, taps, slopes, norms, weights_ref, time_ref,
+        before_ref, own_ref, other_ref, terms_ref, product,
+    )
+
+
+def norm_part(
+    slot,
+    top,
     features,
     me_ref,
     near_ref,
     far_ref,
-    affine_ref,
+    gain_ref,
+    shift_ref,
     turned_ref,
     act_ref,
     sums_ref,
@@ -200,8 +255,10 @@
     taps_ref,
     slopes_ref,
     norms_ref,
-    *kept,
+    rstd_ref,
 ):
+    gain = gain_ref[...].reshape(1, -1)
+    shift = shift_ref[...].reshape(1, -1)
     padded = turned_ref.shape[0] // 9
     rows = LANES
     channels = act_ref.shape[1]
@@ -252,13 +309,13 @@
             rstd = rstds[b * IMAGES : (b + 1) * IMAGES, q * LANES : (q + 1) * LANES]
             rstd = spread(members, rstd, (rows, LANES))
             normed = chunks[b][q] * rstd
-            shifted = normed * affine_ref[0:1, here[1]] + affine_ref[1:2, here[1]]
+            shifted = normed * gain[:, here[1]] + shift[:, here[1]]
             sig = jax.nn.sigmoid(shifted)
             act_ref[here] = (shifted * sig).astype(bf16)
             slopes_ref[here] = sig * (1.0 + shifted * (1.0 - sig))
             norms_ref[here] = normed
-            if keep and b == 0:
-                kept[0][:, here[1]] = rstd
+            if rstd_ref is not None and b == 0:
+                rstd_ref[:, here[1]] = rstd
 
     half = features // 2
     place = lax.broadcasted_iota(jnp.int32, (2 * IMAGES, half), 1).astype(f32)
@@ -267,7 +324,7 @@
     embed_ref[...] = jnp.concatenate([jnp.sin(angles), jnp.cos(angles)], axis=1)
 
 
-def conv_kernel(
+def conv_part(
     slot,
     top,
     owned,
@@ -308,7 +365,7 @@
         )
     grad_act = dot(jnp.concatenate(moved, axis=0), weights)
     slope = grad_act * slopes_ref[...]
-    terms_ref[...] = before_ref[...] + jnp.concatenate(
+    terms = jnp.concatenate(
         [
             jnp.sum(slope * norms_ref[...], axis=0, keepdims=True),
             jnp.sum(slope, axis=0, keepdims=True),
@@ -316,6 +373,10 @@
         ],
         axis=0,
     )
+    if before_ref is not None:
+        terms = terms + before_ref[...]
+    terms_ref[...] = terms
+    other_ref[count * rows + padded :, :] = term_rows(terms)
     grad_act = grad_act.astype(bf16)
     product[...] = dot(act_ref[...], weights, ((1,), (1,)))
     bias = dot(embed_ref[...].astype(bf16), time_ref[...], ((1,), (1,)))
@@ -336,41 +397,79 @@
         )
         members = masks(block_facts(source, top)[0], (rows, LANES))
         total = total + spread(members, bias[b * IMAGES : (b + 1) * IMAGES], (rows, LANES))
-        ref[count * rows :, :] = total.T[:padded].astype(bf16)
+        ref[count * rows : count * rows + padded, :] = total.T[:padded].astype(bf16)
+
+
+def term_rows(terms):
+    count = terms.shape[1] // LANES
+    parts = [terms[r : r + 1, q * LANES : (q + 1) * LANES] for r in range(2) for q in range(count)]
+    whole = jnp.concatenate(parts, axis=0)
+    high = whole.astype(bf16).astype(f32)
+    rest = jnp.zeros((TERM_ROWS - 4 * count, LANES), f32)
+    return jnp.concatenate([high, whole - high, rest], axis=0).astype(bf16)
+
+
+def terms_of(rows, channels):
+    count = channels // LANES
+    rows = rows.astype(f32)
+    whole = rows[: 2 * count] + rows[2 * count : 4 * count]
+    return jnp.concatenate(
+        [
+            jnp.concatenate([whole[r * count + q : r * count + q + 1] for q in range(count)], axis=1)
+            for r in range(2)
+        ],
+        axis=0,
+    )
 
 
 def weight_grad_kernel(pairs, low_taps, owned, *refs):
     turned, act, sums, embed = (
         [ref[...] for ref in refs[i * pairs : (i + 1) * pairs]] for i in range(4)
     )
-    low_ref, high_ref = refs[4 * pairs :]
+    outs = refs[4 * pairs :]
+
+    def put(part, columns, values):
+        outs[part][:, columns] = values[:owned].astype(bf16)
+
     channels = act[0].shape[1]
     padded = turned[0].shape[0] // 9
     grad = dot(jnp.concatenate(turned, axis=1), jnp.concatenate(act, axis=0))
     for t in range(9):
-        part = grad[t * padded : t * padded + owned].astype(bf16)
-        if t < low_taps:
-            low_ref[:, t * channels : (t + 1) * channels] = part
-        else:
-            high_ref[:, (t - low_taps) * channels : (t - low_taps + 1) * channels] = part
+        part, place = (0, t) if t < low_taps else (1, t - low_taps)
+        columns = slice(place * channels, (place + 1) * channels)
+        put(part, columns, grad[t * padded : (t + 1) * padded])
     embed = jnp.concatenate(embed, axis=0).astype(bf16)
     time_grad = jnp.zeros((padded, embed.shape[1]), f32)
     for term in split3(jnp.concatenate(sums, axis=0)):
         time_grad = time_grad + dot(term, embed, ((0,), (0,)))
-    spare = low_ref.shape[1] - low_taps * channels - embed.shape[1]
-    low_ref[:, low_taps * channels :] = jnp.concatenate(
-        [time_grad[:owned], jnp.zeros((owned, spare), f32)], axis=1
-    ).astype(bf16)
-
-
-def join_kernel(owned, own_ref, met_ref, out_ref):
+    width = outs[0].shape[1]
+    spare = width - low_taps * channels - embed.shape[1]
+    time_grad = jnp.concatenate([time_grad, jnp.zeros((padded, spare), f32)], axis=1)
+    put(0, slice(low_taps * channels, width), time_grad)
+
+
+def join_kernel(own_ref, met_ref, out_ref):
     size = own_ref.shape[0]
-    padded = -(-owned // 16) * 16
-    top = size - padded
+    top = 2 * size - out_ref.shape[0]
     total = own_ref[:top, :].astype(f32) + met_ref[:top, :].astype(f32)
     out_ref[:top, :] = total.astype(out_ref.dtype)
     out_ref[top:size, :] = own_ref[top:, :].astype(out_ref.dtype)
-    out_ref[size:, :] = met_ref[top:, :].astype(out_ref.dtype)
+    out_ref[size:, :] = met_ref[top:size, :].astype(out_ref.dtype)
+
+
+def join_last_kernel(own_ref, met_ref, terms_ref, out_ref, sums_ref):
+    join_kernel(own_ref, met_ref, out_ref.at[: out_ref.shape[0] - TERM_ROWS, :])
+    channels = terms_ref.shape[1]
+    mine = terms_of(term_rows(terms_ref[...]), channels)
+    terms = term_rows(mine + terms_of(met_ref[-TERM_ROWS:, :], channels))
+    out_ref[out_ref.shape[0] - TERM_ROWS :, :] = terms
+    sums_ref[...] = terms
+
+
+def add_terms_kernel(terms_ref, met_ref, out_ref):
+    channels = out_ref.shape[1]
+    total = terms_of(terms_ref[...], channels) + terms_of(met_ref[-TERM_ROWS:, :], channels)
+    out_ref[...] = jnp.concatenate([total, jnp.zeros((6, channels), f32)], axis=0)
 
 
 def norm_grad_kernel(
@@ -382,14 +481,15 @@
     *refs,
 ):
     terms = refs[:chips]
-    normed_ref, rstd_ref, affine_ref, out_ref, grad_ref, joined = refs[chips:]
+    normed_ref, rstd_ref, gain_ref, shift_ref, out_ref, grad_ref, joined = refs[chips:]
     rows, channels = rstd_ref.shape
     top = channels // LANES * rows
     padded = (terms[0].shape[0] - top) // 2
+    end = top + 2 * padded
     me = me_ref[0]
     pieces = []
     for ref in terms:
-        pieces += [ref[top : top + padded, :], ref[top + padded :, :]]
+        pieces += [ref[top : top + padded, :], ref[top + padded : end, :]]
     for b, piece in enumerate(pieces):
         start = pl.multiple_of((me ^ b) * owned, 8)
         joined[pl.ds(start, owned), :] = piece[:owned].astype(f32)
@@ -401,9 +501,9 @@
     total = jnp.concatenate(
         [total[q * rows : (q + 1) * rows] for q in range(channels // LANES)], axis=1
     )
-    normed = normed_ref[:rows, :]
-    gain = affine_ref[0:1, :]
-    shifted = normed * gain + affine_ref[1:2, :]
+    normed = normed_ref[...]
+    gain = gain_ref[...].reshape(1, -1)
+    shifted = normed * gain + shift_ref[...].reshape(1, -1)
     sig = jax.nn.sigmoid(shifted)
     slope = total * (sig * (1.0 + shifted * (1.0 - sig)))
     grad = slope * gain
@@ -428,22 +528,24 @@
     conv_ref[:, width:] = (high_ref[...].astype(f32) + high_met_ref[...].astype(f32)) * scale
 
 
-def call(kernel, outs, scratch, limit, scalars, microseconds, *args):
+def call(kernel, outs, scratch, limit, scalars, microseconds, *args, left=()):
     smem = pl.BlockSpec(memory_space=pltpu.SMEM)
     vmem = pl.BlockSpec(memory_space=pltpu.VMEM)
     return pl.pallas_call(
         kernel,
         out_shape=outs,
-        in_specs=[smem] * scalars + [vmem] * (len(args) - scalars),
+        in_specs=[smem] * scalars
+        + [vmem] * (len(args) - scalars)
+        + [pl.BlockSpec(memory_space=pl.ANY)] * len(left),
         out_specs=jax.tree.map(lambda _: vmem, outs),
         scratch_shapes=scratch,
         compiler_params=pltpu.CompilerParams(vmem_limit_bytes=limit << 20),
         cost_estimate=pl.CostEstimate(
-            flops=int(microseconds * 0.01 * 1e9),
-            bytes_accessed=int(microseconds * 0.01 * 3e6),
+            flops=int(microseconds * 0.5 * 1e9),
+            bytes_accessed=int(microseconds * 0.5 * 3e6),
             transcendentals=0,
         ),
-    )(*args)
+    )(*args, *left)
 
 
 def exchange(value, axis, bit):
@@ -471,7 +573,6 @@
     low_taps = 4
     time_width = -(-feature_count // LANES) * LANES
     shape = jax.ShapeDtypeStruct
-    affine = jnp.stack([norm_gain, norm_shift])
 
     roots = [0] + [1 << i for i in range((chips - 1).bit_length())]
     tops = [2 * padded * max(root, 1) for root in roots]
@@ -481,7 +582,7 @@
         [],
         60,
         4,
-        2.0,
+        4.0,
         me,
         heights,
         widths,
@@ -490,101 +591,102 @@
         cotangent,
     )
     returned = channels // LANES * rows + padded
-    near, far, normed, results = [sent[0]], [], [], {}
-    terms = jnp.zeros((8, channels), f32)
-
-    def slot_and_top(k):
-        return k - roots[k.bit_length()], tops[k.bit_length()]
-
-    def convolve(k, me, weights, terms):
+    last = chips - 1
+    if padded > owned:
+        conv_rows = jnp.pad(conv_weight, ((0, padded - owned), (0, 0)))
+    else:
+        conv_rows = conv_weight
+    own_shapes = [
+        shape((returned, LANES), bf16),
+        shape((returned + TERM_ROWS, LANES), bf16),
+        shape((8, channels), f32),
+    ]
+    norm_shapes = [
+        shape((9 * padded, 2 * rows), bf16),
+        shape((2 * rows, channels), bf16),
+        shape((2 * IMAGES, padded), f32),
+        shape((2 * IMAGES, feature_count), f32),
+    ]
+    held = [
+        ((2 * rows, 9 * rows), bf16),
+        ((2 * rows, channels), f32),
+        ((2 * rows, channels), f32),
+    ]
+    product = pltpu.VMEM((2 * rows, 9 * LANES), f32)
+
+    near, far, ours, normed = [sent[0]], [], [], []
+    here = me
+
+    def arrive(k):
+        low_bit = k & -k
+        from_here = sent[k.bit_length()] if k == low_bit else near[k - low_bit]
+        return exchange(from_here, "fsdp", 2 * low_bit)
+
+    for k in range(chips):
+        root = roots[k.bit_length()]
+        where = k - root, tops[k.bit_length()]
+        if k == 1:
+            arrived, here, terms = together(arrive(1), here, terms)
+            near.append(arrived)
+        if k == 1 and k < last:
+            arrived, here, terms = together(arrive(k + 1), here, terms)
+            near.append(arrived)
+        far.append(exchange(near[k], "fsdp", 1))
+        common = [here, near[k], far[k], norm_gain, norm_shift]
+        if k == 0:
+            *made, own_normed, rstd, weights, time_held = call(
+                functools.partial(first_kernel, *where, owned),
+                own_shapes
+                + norm_shapes
+                + [
+                    shape((rows, channels), f32),
+                    shape((rows, channels), f32),
+                    shape((9 * LANES, channels), bf16),
+                    shape((owned, feature_count), bf16),
+                ],
+                [pltpu.VMEM(*s) for s in held] + [product, pltpu.SemaphoreType.DMA((10,))],
+                16,
+                1,
+                2.0,
+                *common,
+                left=(conv_rows, time_weight),
+            )
+        else:
+            made = call(
+                functools.partial(pair_kernel, *where, owned),
+                own_shapes + norm_shapes,
+                [pltpu.VMEM(*s) for s in held] + [product],
+                16,
+                1,
+                2.0,
+                *common,
+                weights,
+                time_held,
+                terms,
+            )
+        ours.append(list(made[:2]))
+        terms = made[2]
+        normed.append(list(made[3:]))
+        if 1 < k < last:
+            arrived, here, terms = together(arrive(k + 1), here, terms)
+            near.append(arrived)
+
+    met = [exchange(ours[k][1], "fsdp", 1) for k in range(chips)]
+
+    def join(k):
         return call(
-            functools.partial(conv_kernel, *slot_and_top(k), owned),
-            (
-                shape((returned, LANES), bf16),
-                shape((returned, LANES), bf16),
-                shape((8, channels), f32),
-            ),
-            [pltpu.VMEM((2 * rows, 9 * LANES), f32)],
-            16,
-            1,
-            2.0,
-            me,
-            near[k],
-            far[k],
-            normed[k][1],
-            *normed[k][3:7],
-            weights,
-            time_weight,
-            terms,
-        )
-
-    def join(k, dtype):
-        own, other = results[k]
-        return call(
-            functools.partial(join_kernel, owned),
-            shape((returned + padded, LANES), dtype),
+            join_kernel,
+            shape((returned + padded, LANES), bf16 if k else f32),
             [],
             8,
             0,
             0.1,
-            own,
-            exchange(other, "fsdp", 1),
+            ours[k][0],
+            met[k],
         )
 
-    here = me
-    for k in range(chips):
-        low_bit = k & -k
-        if k:
-            from_here = sent[k.bit_length()] if k == low_bit else near[k - low_bit]
-            near.append(exchange(from_here, "fsdp", 2 * low_bit))
-            if k > 1:
-                near[k], normed[-1][2], terms = together(near[k], normed[-1][2], terms)
-            if k == chips - 1 and k > 1:
-                *results[k - 1], terms = convolve(k - 1, here, weights, terms)
-            near[k], here, terms = together(near[k], here, terms)
-            if k - 1 not in results:
-                *results[k - 1], terms = convolve(k - 1, here, weights, terms)
-        far.append(exchange(near[k], "fsdp", 1))
-        normed.append(
-            call(
-                functools.partial(norm_kernel, *slot_and_top(k), k == 0, feature_count),
-                [
-                    shape((9 * padded, 2 * rows), bf16),
-                    shape((2 * rows, channels), bf16),
-                    shape((2 * IMAGES, padded), f32),
-                    shape((2 * IMAGES, feature_count), f32),
-                    shape((2 * rows, 9 * rows), bf16),
-                    shape((2 * rows, channels), f32),
-                    shape((2 * rows, channels), f32),
-                ]
-                + [shape((rows, channels), f32)] * (k == 0),
-                [],
-                16,
-                1,
-                2.0,
-                me,
-                near[k],
-                far[k],
-                affine,
-            )
-        )
-        normed[-1] = list(normed[-1])
-        if k == 0:
-            normed[0][2], here = together(normed[0][2], me)
-            weights = call(
-                weight_kernel,
-                shape((9 * LANES, channels), bf16),
-                [],
-                16,
-                1,
-                2.0,
-                here,
-                conv_weight,
-            )
-            *results[0], terms = convolve(0, here, weights, terms)
-    rstd = normed[0][7]
-    joined = [join(k, bf16 if k else f32) for k in range(chips - 1)]
-    normed[-1][2], *joined = together(normed[-1][2], *joined)
+    grads = [join(k) for k in range(last)]
+    normed[-1][2], *grads = together(normed[-1][2], *grads)
     low, high = call(
         functools.partial(weight_grad_kernel, chips, low_taps, owned),
         (
@@ -597,29 +699,41 @@
         1.5,
         *(result[i] for i in range(4) for result in normed),
     )
+    part, terms = call(
+        join_last_kernel,
+        (shape((returned + padded + TERM_ROWS, LANES), bf16), shape((TERM_ROWS, LANES), bf16)),
+        [],
+        8,
+        0,
+        0.1,
+        ours[last][0],
+        met[last],
+        terms,
+    )
+    grads.append(part)
 
     bits = [1 << i for i in range((replicas - 1).bit_length())]
-    low, high, here = together(low, high, here)
     totals = [low, high]
-    received = [exchange(t, "dp", bit) for t, bit in zip(totals, (bits[0], bits[-1]))]
-
-    grads = [joined[0]] + [exchange(joined[k], "fsdp", 2 * k) for k in range(1, chips - 1)]
-    last = chips - 1
-    *results[last], terms = convolve(last, here, weights, terms)
-    part, *grads[1:] = together(join(last, bf16), *grads[1:])
-    grads.append(exchange(part, "fsdp", 2 * last))
-    for i in range((holders - 1).bit_length()):
-        if i == 1:
-            received, terms, grads[1:last] = together(received, terms, grads[1:last])
-        terms = terms + exchange(terms, "fsdp", 1 << i)
-
-    for step in range(1, len(bits)):
-        totals = [
-            (t.astype(f32) + r.astype(f32)).astype(bf16) for t, r in zip(totals, received)
-        ]
+    early = [1, last] if last > 1 else [1]
+    for step in range(len(bits)):
         orders = (bits[step], bits[-1 - step])
         received = [exchange(t, "dp", bit) for t, bit in zip(totals, orders)]
-    totals, grads[0], terms = lax.optimization_barrier((totals, grads[0], terms))
+        if step == 0:
+            for k in early:
+                grads[k] = exchange(grads[k], "fsdp", 2 * k)
+            received, grads, terms = together(received, grads, terms)
+        if step < len(bits) - 1:
+            totals = [
+                (t.astype(f32) + r.astype(f32)).astype(bf16) for t, r in zip(totals, received)
+            ]
+    for k in range(1, chips):
+        if k not in early:
+            grads[k] = exchange(grads[k], "fsdp", 2 * k)
+    terms = call(
+        add_terms_kernel, shape((8, channels), f32), [], 8, 0, 0.1, terms, grads[last]
+    )
+    for i in range((chips - 1).bit_length() - 1):
+        terms = terms + exchange(terms, "fsdp", 2 << i)
     grad_conv, grad_time = call(
         functools.partial(finish_kernel, scale),
         (shape((owned, 9 * channels), f32), shape((owned, feature_count), f32)),
@@ -634,7 +748,10 @@
     )
     block_out, grad_features = call(
         functools.partial(norm_grad_kernel, owned, chips),
-        (shape((rows, out_channels), bf16), shape((rows, channels), bf16)),
+        (
+            shape((rows, out_channels), bf16),
+            shape((rows, channels), bf16),
+        ),
         [pltpu.VMEM((out_channels, rows), f32)],
         16,
         3,
@@ -643,13 +760,17 @@
         heights,
         widths,
         *grads,
-        normed[0][6],
+        own_normed,
         rstd,
-        affine,
-    )
-    for bit in bits:
-        terms = terms + exchange(terms, "dp", bit)
-    return (block_out, grad_features, grad_conv, grad_time, terms[0] * scale, terms[1] * scale)
+        norm_gain,
+        norm_shift,
+    )
+    values = [terms] + [exchange(terms, "dp", bit) for bit in range(1, replicas)]
+    grad_time, *values = together(grad_time, *values)
+    while len(values) > 1:
+        values = [a + b for a, b in zip(values[::2], values[1::2])]
+    terms = values[0] * scale
+    return (block_out, grad_features, grad_conv, grad_time, terms[0], terms[1])
 
 
 def solution(mesh):

time: 81.3 us -> 75.2 us (0.925)
  waiting for transfers between devices: 28.9 us -> 25.9 us
  local copies, waits for them, and re-layouts: 4.31 us -> 1.57 us
  starting transfers between devices: 20.8 us -> 22.6 us
  Pallas kernels: 25.2 us -> 23.8 us
    ppermute x23 -> x22, waiting for transfers between devices: 28.9 us -> 25.9 us  [exchange(): return lax.ppermute(value, axis, [(i, i ^ bit) for i in range(size)])]
    unnamed x10 -> x14, local copies, waits for them, and re-layouts: 2.93 us -> 0.96 us
    ppermute x23 -> x22, starting transfers between devices: 20.8 us -> 22.6 us  [exchange(): return lax.ppermute(value, axis, [(i, i ^ bit) for i in range(size)])]
    pallas_call x17 -> x13, Pallas kernels: 25.2 us -> 23.8 us  [call(): pl.pallas_call(kernel, out_shape=outs, in_specs=[smem] * scalars + [vmem]...]
    another operation x2 -> x0, local copies, waits for them, and re-layouts: 1.38 us -> none  [shards(): affine = jnp.stack([norm_gain, norm_shift])]
  transfers between devices with their start and end apart: 23 -> 22, of which waited for: 14 -> 10; matrix products, arithmetic and copies ran while one was open for 3% -> 0% of each run, Pallas kernels for 19% -> 21%
where the time goes in v3:
time: 75.2 us; the launch traced here: 75 us
  waiting for transfers between devices  25.9 us (34%)
  Pallas kernels  23.8 us (32%)
  starting transfers between devices  22.6 us (30%)
  local copies, waits for them, and re-layouts  1.57 us (2%)
  between operations  0.83 us (1%)
    ppermute x22, waiting for transfers between devices, exchange(): return lax.ppermute(value, axis, [(i, i ^ bit) for i in range(size)])  25.9 us
    pallas_call x13, Pallas kernels, call(): pl.pallas_call(kernel, out_shape=outs, in_specs=[smem] * scalars + [vmem]...  23.8 us
    ppermute x22, starting transfers between devices, exchange(): return lax.ppermute(value, axis, [(i, i ^ bit) for i in range(size)])  22.6 us
  transfers between devices with their start and end apart: 22, of which 10 were waited for; matrix products, arithmetic and copies ran while one was open for 0% of the time, Pallas kernels for 21%

profile of v3, /device:TPU:0, one launch (start us, length us, event | category | flops | bytes accessed | tf_op | source)
XLA Modules:
  0.0 75.0 jit_solution(3529489404360532714)
XLA Ops:
  0.7 2.2 %shard_map.136 = (bf16[848,128]{1,0:T(8,128)(2,1)}, bf16[848,128]{1,0:T(8,128)(2,1)}, bf16[1040,128]{1,0:T(8,128)(2,1)}) custom-call(s32[1]{0:T(128)} %bitcast.me_ref, s32[1,4]{1,0:T(1,128)} %heights_ref.3, s32[1,4]{1,0:T(1,128)} %widths_ref.3, s32[1,4]{1,0:T(1,128)} %times_ref.1, bf16[128,640]{1,0:T(8,128)(2,1)} %features_ref.1, bf16[128,768]{1,0:T(8,128)(2,1)} %cotan_ref.1), custom_call_target="tpu_custom_call" | custom-call | flops 2000000000 | bytes 6000000 | tf_op jit(solution)/shard_map/pallas_call | solution.py:534
  2.9 0.5 collective-permute-start
  3.4 3.6 %collective-permute-start.1 = (bf16[1040,128]{1,0:T(8,128)(2,1)}, bf16[1040,128]{1,0:T(8,128)(2,1)S(1)}, u32[]{:S(2)}, u32[]{:S(2)}) collective-permute-start(bf16[1040,128]{1,0:T(8,128)(2,1)} %get-tuple-element.76), channel_id=1, source_target_pairs={{0,4},{1,5},{2,6},{3,7},{4,0},{5,1},{6,2},{7,3},{8,12},{9,13},{10,... | collective-permute-start | bytes 798728 | tf_op jit(solution)/shard_map/ppermute | solution.py:553
  7.0 1.6 %collective-permute-start.2 = (bf16[848,128]{1,0:T(8,128)(2,1)}, bf16[848,128]{1,0:T(8,128)(2,1)S(1)}, u32[]{:S(2)}, u32[]{:S(2)}) collective-permute-start(bf16[848,128]{1,0:T(8,128)(2,1)} %get-tuple-element.77), channel_id=1, source_target_pairs={{0,2},{1,3},{2,0},{3,1},{4,6},{5,7},{6,4},{7,5},{8,10},{9,11},{10,... | collective-permute-start | bytes 651272 | tf_op jit(solution)/shard_map/ppermute | solution.py:553
  8.5 0.0 collective-permute-done.far_ref
  8.6 0.9 %copy-done.1 = bf16[848,128]{1,0:T(8,128)(2,1)S(1)} copy-done((bf16[848,128]{1,0:T(8,128)(2,1)S(1)}, bf16[848,128]{1,0:T(8,128)(2,1)}, u32[]{:S(2)}) %copy-start.1) | copy-done | bytes 217112
  9.5 4.6 %shard_map.137 = (bf16[736,128]{1,0:T(8,128)(2,1)S(1)}, bf16[768,128]{1,0:T(8,128)(2,1)S(1)}, f32[8,640]{1,0:T(8,128)S(1)}, bf16[864,256]{1,0:T(8,128)(2,1)S(1)}...) custom-call(s32[1]{0:T(128)} %bitcast.me_ref, ...), custom_call_target="tpu_custom_call" | custom-call | flops 1000000000 | bytes 3000000 | tf_op jit(solution)/shard_map/pallas_call | solution.py:534
  14.1 4.2 %collective-permute-done.2.near_ref = bf16[848,128]{1,0:T(8,128)(2,1)S(1)} collective-permute-done((bf16[848,128]{1,0:T(8,128)(2,1)}, bf16[848,128]{1,0:T(8,128)(2,1)S(1)}, u32[]{:S(2)}, u32[]{:S(2)}) %collective-permute-start.2) | collective-permute-done | bytes 217120 | tf_op jit(solution)/shard_map/ppermute | solution.py:553
  18.3 1.6 %collective-permute-done.1.near_ref = bf16[1040,128]{1,0:T(8,128)(2,1)S(1)} collective-permute-done((bf16[1040,128]{1,0:T(8,128)(2,1)}, bf16[1040,128]{1,0:T(8,128)(2,1)S(1)}, u32[]{:S(2)}, u32[]{:S(2)}) %collective-permute-start.1) | collective-permute-done | bytes 266272 | tf_op jit(solution)/shard_map/ppermute | solution.py:553
  19.9 0.0 collective-permute-start.4
  19.9 1.2 %collective-permute-start.5 = (bf16[1040,128]{1,0:T(8,128)(2,1)S(1)}, bf16[1040,128]{1,0:T(8,128)(2,1)S(1)}, u32[]{:S(2)}, u32[]{:S(2)}) collective-permute-start(bf16[1040,128]{1,0:T(8,128)(2,1)S(1)} %collective-permute-done.1.near_ref), channel_id=1, source_target_pairs={{0,2},{1,3},{2,0},{3,1},{4,6},{5,7},{6,4},{7,5},{8,10},{9,11},{10,... | collective-permute-start | bytes 798728 | tf_op jit(solution)/shard_map/ppermute | solution.py:553
  21.2 0.0 collective-permute-done.3.far_ref
  21.2 3.7 %shard_map.138 = (bf16[736,128]{1,0:T(8,128)(2,1)S(1)}, bf16[768,128]{1,0:T(8,128)(2,1)S(1)}, f32[8,640]{1,0:T(8,128)S(1)}, bf16[864,256]{1,0:T(8,128)(2,1)S(1)}...) custom-call(s32[1]{0:T(128)} %bitcast.me_ref, ...), custom_call_target="tpu_custom_call" | custom-call | flops 1000000000 | bytes 3000000 | tf_op jit(solution)/shard_map/pallas_call | solution.py:534
  24.9 0.0 collective-permute-done.4.far_ref
  24.9 3.7 %shard_map.139 = (bf16[736,128]{1,0:T(8,128)(2,1)S(1)}, bf16[768,128]{1,0:T(8,128)(2,1)S(1)}, f32[8,640]{1,0:T(8,128)S(1)}, bf16[864,256]{1,0:T(8,128)(2,1)S(1)}...) custom-call(s32[1]{0:T(128)} %bitcast.me_ref, ...), custom_call_target="tpu_custom_call" | custom-call | flops 1000000000 | bytes 3000000 | tf_op jit(solution)/shard_map/pallas_call | solution.py:534
  28.5 0.2 collective-permute-done.5.near_ref
  28.8 0.0 collective-permute-start.6
  28.8 0.5 collective-permute-start.7
  29.3 0.0 collective-permute-start.8
  29.3 0.5 collective-permute-start.9
  29.8 0.8 %collective-permute-done.7.met_ref = bf16[768,128]{1,0:T(8,128)(2,1)S(1)} collective-permute-done((bf16[768,128]{1,0:T(8,128)(2,1)S(1)}, bf16[768,128]{1,0:T(8,128)(2,1)S(1)}, u32[]{:S(2)}, u32[]{:S(2)}) %collective-permute-start.7) | collective-permute-done | bytes 196640 | tf_op jit(solution)/shard_map/ppermute | solution.py:553
  30.6 0.2 collective-permute-done.8.met_ref
  30.9 0.2 collective-permute-done.9.met_ref
  31.2 0.0 collective-permute-done.6.far_ref
  31.2 3.8 %shard_map.140 = (bf16[736,128]{1,0:T(8,128)(2,1)S(1)}, bf16[768,128]{1,0:T(8,128)(2,1)S(1)}, f32[8,640]{1,0:T(8,128)S(1)}, bf16[864,256]{1,0:T(8,128)(2,1)S(1)}...) custom-call(s32[1]{0:T(128)} %bitcast.me_ref, ...), custom_call_target="tpu_custom_call" | custom-call | flops 1000000000 | bytes 3000000 | tf_op jit(solution)/shard_map/pallas_call | solution.py:534
  35.0 1.6 %shard_map.144 = (bf16[96,2944]{1,0:T(8,128)(2,1)S(1)}, bf16[96,3200]{1,0:T(8,128)(2,1)S(1)}) custom-call(bf16[864,256]{1,0:T(8,128)(2,1)S(1)} %get-tuple-element.75.refs_0_, bf16[864,256]{1,0:T(8,128)(2,1)S(1)} %get-tuple-element.86.refs_1_, bf16[864,256]{1,0:T(8,128)(2,1)S(1)} %get-tuple-element.89.refs_2_, ...), custom_call_target="tpu_custom_call" | custom-call | flops 750000000 | bytes 2250000 | tf_op jit(solution)/shard_map/pallas_call | solution.py:534
  36.6 1.6 %collective-permute-start.11 = (bf16[96,3200]{1,0:T(8,128)(2,1)S(1)}, bf16[96,3200]{1,0:T(8,128)(2,1)S(1)}, u32[]{:S(2)}, u32[]{:S(2)}) collective-permute-start(bf16[96,3200]{1,0:T(8,128)(2,1)S(1)} %get-tuple-element.115), channel_id=1, source_target_pairs={{0,16},{8,24},{16,0},{24,8},{1,17},{9,25},{17,1},{25,9},{2,18},{10... | collective-permute-start | bytes 1843208 | tf_op jit(solution)/shard_map/ppermute | solution.py:553
  38.3 1.5 %collective-permute-start.10 = (bf16[96,2944]{1,0:T(8,128)(2,1)S(1)}, bf16[96,2944]{1,0:T(8,128)(2,1)S(1)}, u32[]{:S(2)}, u32[]{:S(2)}) collective-permute-start(bf16[96,2944]{1,0:T(8,128)(2,1)S(1)} %get-tuple-element.114), channel_id=1, source_target_pairs={{0,8},{8,0},{16,24},{24,16},{1,9},{9,1},{17,25},{25,17},{2,10},{10... | collective-permute-start | bytes 1695752 | tf_op jit(solution)/shard_map/ppermute | solution.py:553
  39.8 1.4 %collective-permute-done.13.met_ref = bf16[768,128]{1,0:T(8,128)(2,1)S(1)} collective-permute-done((bf16[768,128]{1,0:T(8,128)(2,1)S(1)}, bf16[768,128]{1,0:T(8,128)(2,1)S(1)}, u32[]{:S(2)}, u32[]{:S(2)}) %collective-permute-start.13) | collective-permute-done | bytes 196640 | tf_op jit(solution)/shard_map/ppermute | solution.py:553
  41.2 0.1 shard_map.145
  41.3 3.6 %collective-permute-start.14 = (bf16[864,128]{1,0:T(8,128)(2,1)S(1)}, bf16[864,128]{1,0:T(8,128)(2,1)S(1)}, u32[]{:S(2)}, u32[]{:S(2)}) collective-permute-start(bf16[864,128]{1,0:T(8,128)(2,1)S(1)} %get-tuple-element.122), channel_id=1, source_target_pairs={{0,6},{1,7},{2,4},{3,5},{4,2},{5,3},{6,0},{7,1},{8,14},{9,15},{10,... | collective-permute-start | bytes 663560 | tf_op jit(solution)/shard_map/ppermute | solution.py:553
  44.9 10.4 %collective-permute-done.12.refs_1_ = bf16[832,128]{1,0:T(8,128)(2,1)S(1)} collective-permute-done((bf16[832,128]{1,0:T(8,128)(2,1)S(1)}, bf16[832,128]{1,0:T(8,128)(2,1)S(1)}, u32[]{:S(2)}, u32[]{:S(2)}) %collective-permute-start.12) | collective-permute-done | bytes 213024 | tf_op jit(solution)/shard_map/ppermute | solution.py:553
  55.3 0.1 add_convert_fusion.high_ref
  55.5 0.0 copy-start.5
  55.5 0.0 copy-start.6
  55.5 0.6 collective-permute-start.17
  56.1 0.1 add_convert_fusion.1.low_ref
  56.2 0.5 collective-permute-start.16
  56.8 2.1 %collective-permute-start.15 = (bf16[832,128]{1,0:T(8,128)(2,1)S(1)}, bf16[832,128]{1,0:T(8,128)(2,1)S(1)}, u32[]{:S(2)}, u32[]{:S(2)}) collective-permute-start(bf16[832,128]{1,0:T(8,128)(2,1)S(1)} %shard_map.143), channel_id=1, source_target_pairs={{0,4},{1,5},{2,6},{3,7},{4,0},{5,1},{6,2},{7,3},{8,12},{9,13},{10,... | collective-permute-start | bytes 638984 | tf_op jit(solution)/shard_map/ppermute | solution.py:553
  58.9 1.4 %collective-permute-start.18 = (f32[8,640]{1,0:T(8,128)S(1)}, f32[8,640]{1,0:T(8,128)S(1)}, u32[]{:S(2)}, u32[]{:S(2)}) collective-permute-start(f32[8,640]{1,0:T(8,128)S(1)} %shard_map.148), channel_id=1, source_target_pairs={{0,2},{1,3},{2,0},{3,1},{4,6},{5,7},{6,4},{7,5},{8,10},{9,11},{10,... | collective-permute-start | bytes 61448 | tf_op jit(solution)/shard_map/ppermute | solution.py:553
  60.3 2.6 %collective-permute-done.18 = f32[8,640]{1,0:T(8,128)S(1)} collective-permute-done((f32[8,640]{1,0:T(8,128)S(1)}, f32[8,640]{1,0:T(8,128)S(1)}, u32[]{:S(2)}, u32[]{:S(2)}) %collective-permute-start.18) | collective-permute-done | bytes 20512 | tf_op jit(solution)/shard_map/ppermute | solution.py:553
  62.9 1.3 %collective-permute-start.21 = (f32[8,640]{1,0:T(8,128)S(1)}, f32[8,640]{1,0:T(8,128)S(1)}, u32[]{:S(2)}, u32[]{:S(2)}) collective-permute-start(f32[8,640]{1,0:T(8,128)S(1)} %add.20), channel_id=1, source_target_pairs={{0,24},{8,16},{16,8},{24,0},{1,25},{9,17},{17,9},{25,1},{2,26},{10... | collective-permute-start | bytes 61448 | tf_op jit(solution)/shard_map/ppermute | solution.py:553
  64.2 0.6 collective-permute-start.20
  64.8 4.0 %collective-permute-done.15.refs_2_ = bf16[832,128]{1,0:T(8,128)(2,1)S(1)} collective-permute-done((bf16[832,128]{1,0:T(8,128)(2,1)S(1)}, bf16[832,128]{1,0:T(8,128)(2,1)S(1)}, u32[]{:S(2)}, u32[]{:S(2)}) %collective-permute-start.15) | collective-permute-done | bytes 213024 | tf_op jit(solution)/shard_map/ppermute | solution.py:553
  68.8 1.5 %collective-permute-start.19 = (f32[8,640]{1,0:T(8,128)S(1)}, f32[8,640]{1,0:T(8,128)S(1)}, u32[]{:S(2)}, u32[]{:S(2)}) collective-permute-start(f32[8,640]{1,0:T(8,128)S(1)} %add.20), channel_id=1, source_target_pairs={{0,8},{8,0},{16,24},{24,16},{1,9},{9,1},{17,25},{25,17},{2,10},{10... | collective-permute-start | bytes 61448 | tf_op jit(solution)/shard_map/ppermute | solution.py:553
  70.4 2.3 %shard_map.146 = (bf16[128,768]{1,0:T(8,128)(2,1)}, bf16[128,640]{1,0:T(8,128)(2,1)}) custom-call(s32[1]{0:T(128)} %bitcast.me_ref, s32[1,4]{1,0:T(1,128)S(1)} %copy-done.5, s32[1,4]{1,0:T(1,128)S(1)} %copy-done.6, f32[832,128]{1,0:T(8,128)S(1)} %shard_map.141.refs_0_, bf16[832,128]{1,0:T(8,128)(2,1)S(1)} %collective-permute-done.12.refs_1_, ...), custom_call_target="tpu_custom_call" | custom-call | flops 1250000000 | bytes 3750000 | tf_op jit(solution)/shard_map/pallas_call | solution.py:534
  72.7 1.7 %shard_map.147 = (f32[96,5760]{1,0:T(8,128)}, f32[96,320]{1,0:T(8,128)}) custom-call(bf16[96,2944]{1,0:T(8,128)(2,1)S(1)} %add_convert_fusion.1.low_ref, bf16[96,2944]{1,0:T(8,128)(2,1)S(1)} %collective-permute-done.16.low_met_ref, bf16[96,3200]{1,0:T(8,128)(2,1)S(1)} %add_convert_fusion.high_ref, bf16[96,3200]{1,0:T(8,128)(2,1)S(1)} %collective-permute-done.17.high_met_ref), custom_call_target="tpu_custom_call" | custom-call | flops 750000000 | bytes 2250000 | tf_op jit(solution)/shard_map/pallas_call | solution.py:534
  74.4 0.6 slice_reduce_fusion
  (28 shorter events, 0.2 us)
Async XLA Ops:
  0.6 7.9 %copy-start = (bf16[96,5760]{1,0:T(8,128)(2,1)S(1)}, bf16[96,5760]{1,0:T(8,128)(2,1)}, u32[]{:S(2)}) copy-start(bf16[96,5760]{1,0:T(8,128)(2,1)} %refs_0_.1) | copy-start | bytes 3317764
  0.6 7.9 %copy-start.2 = (bf16[96,320]{1,0:T(8,128)(2,1)S(1)}, bf16[96,320]{1,0:T(8,128)(2,1)}, u32[]{:S(2)}) copy-start(bf16[96,320]{1,0:T(8,128)(2,1)} %refs_1_.1) | copy-start | bytes 184324
  0.7 7.9 %copy-start.3 = (f32[640]{0:T(1024)S(1)}, f32[640]{0:T(1024)}, u32[]{:S(2)}) copy-start(f32[640]{0:T(1024)} %refs_6_.1) | copy-start | bytes 7684
  0.7 7.9 %copy-start.4 = (f32[640]{0:T(1024)S(1)}, f32[640]{0:T(1024)}, u32[]{:S(2)}) copy-start(f32[640]{0:T(1024)} %refs_7_.1) | copy-start | bytes 7684
  2.9 5.6 %collective-permute-start = (bf16[848,128]{1,0:T(8,128)(2,1)}, bf16[848,128]{1,0:T(8,128)(2,1)S(1)}, u32[]{:S(2)}, u32[]{:S(2)}) collective-permute-start(bf16[848,128]{1,0:T(8,128)(2,1)} %get-tuple-element.74.near_ref), channel_id=1, source_target_pairs={{0,1},{1,0},{2,3},{3,2},{4,5},{5,4},{6,7},{7,6},{8,9},{9,8},{10,11... | collective-permute-start | bytes 651272 | tf_op jit(solution)/shard_map/ppermute | solution.py:553
  3.4 16.6 %collective-permute-start.1 = (bf16[1040,128]{1,0:T(8,128)(2,1)}, bf16[1040,128]{1,0:T(8,128)(2,1)S(1)}, u32[]{:S(2)}, u32[]{:S(2)}) collective-permute-start(bf16[1040,128]{1,0:T(8,128)(2,1)} %get-tuple-element.76), channel_id=1, source_target_pairs={{0,4},{1,5},{2,6},{3,7},{4,0},{5,1},{6,2},{7,3},{8,12},{9,13},{10,... | collective-permute-start | bytes 798728 | tf_op jit(solution)/shard_map/ppermute | solution.py:553
  7.0 11.3 %collective-permute-start.2 = (bf16[848,128]{1,0:T(8,128)(2,1)}, bf16[848,128]{1,0:T(8,128)(2,1)S(1)}, u32[]{:S(2)}, u32[]{:S(2)}) collective-permute-start(bf16[848,128]{1,0:T(8,128)(2,1)} %get-tuple-element.77), channel_id=1, source_target_pairs={{0,2},{1,3},{2,0},{3,1},{4,6},{5,7},{6,4},{7,5},{8,10},{9,11},{10,... | collective-permute-start | bytes 651272 | tf_op jit(solution)/shard_map/ppermute | solution.py:553
  8.6 0.9 %copy-start.1 = (bf16[848,128]{1,0:T(8,128)(2,1)S(1)}, bf16[848,128]{1,0:T(8,128)(2,1)}, u32[]{:S(2)}) copy-start(bf16[848,128]{1,0:T(8,128)(2,1)} %get-tuple-element.74.near_ref) | copy-start | bytes 651268
  18.3 2.9 %collective-permute-start.3 = (bf16[848,128]{1,0:T(8,128)(2,1)S(1)}, bf16[848,128]{1,0:T(8,128)(2,1)S(1)}, u32[]{:S(2)}, u32[]{:S(2)}) collective-permute-start(bf16[848,128]{1,0:T(8,128)(2,1)S(1)} %collective-permute-done.2.near_ref), channel_id=1, source_target_pairs={{0,1},{1,0},{2,3},{3,2},{4,5},{5,4},{6,7},{7,6},{8,9},{9,8},{10,11... | collective-permute-start | bytes 651272 | tf_op jit(solution)/shard_map/ppermute | solution.py:553
  19.9 4.9 %collective-permute-start.4 = (bf16[1040,128]{1,0:T(8,128)(2,1)S(1)}, bf16[1040,128]{1,0:T(8,128)(2,1)S(1)}, u32[]{:S(2)}, u32[]{:S(2)}) collective-permute-start(bf16[1040,128]{1,0:T(8,128)(2,1)S(1)} %collective-permute-done.1.near_ref), channel_id=1, source_target_pairs={{0,1},{1,0},{2,3},{3,2},{4,5},{5,4},{6,7},{7,6},{8,9},{9,8},{10,11... | collective-permute-start | bytes 798728 | tf_op jit(solution)/shard_map/ppermute | solution.py:553
  19.9 8.8 %collective-permute-start.5 = (bf16[1040,128]{1,0:T(8,128)(2,1)S(1)}, bf16[1040,128]{1,0:T(8,128)(2,1)S(1)}, u32[]{:S(2)}, u32[]{:S(2)}) collective-permute-start(bf16[1040,128]{1,0:T(8,128)(2,1)S(1)} %collective-permute-done.1.near_ref), channel_id=1, source_target_pairs={{0,2},{1,3},{2,0},{3,1},{4,6},{5,7},{6,4},{7,5},{8,10},{9,11},{10,... | collective-permute-start | bytes 798728 | tf_op jit(solution)/shard_map/ppermute | solution.py:553
  28.8 2.4 %collective-permute-start.6 = (bf16[1040,128]{1,0:T(8,128)(2,1)S(1)}, bf16[1040,128]{1,0:T(8,128)(2,1)S(1)}, u32[]{:S(2)}, u32[]{:S(2)}) collective-permute-start(bf16[1040,128]{1,0:T(8,128)(2,1)S(1)} %collective-permute-done.5.near_ref), channel_id=1, source_target_pairs={{0,1},{1,0},{2,3},{3,2},{4,5},{5,4},{6,7},{7,6},{8,9},{9,8},{10,11... | collective-permute-start | bytes 798728 | tf_op jit(solution)/shard_map/ppermute | solution.py:553
  28.8 1.8 %collective-permute-start.7 = (bf16[768,128]{1,0:T(8,128)(2,1)S(1)}, bf16[768,128]{1,0:T(8,128)(2,1)S(1)}, u32[]{:S(2)}, u32[]{:S(2)}) collective-permute-start(bf16[768,128]{1,0:T(8,128)(2,1)S(1)} %get-tuple-element.104), channel_id=1, source_target_pairs={{0,1},{1,0},{2,3},{3,2},{4,5},{5,4},{6,7},{7,6},{8,9},{9,8},{10,11... | collective-permute-start | bytes 589832 | tf_op jit(solution)/shard_map/ppermute | solution.py:553
  29.3 1.6 %collective-permute-start.8 = (bf16[768,128]{1,0:T(8,128)(2,1)S(1)}, bf16[768,128]{1,0:T(8,128)(2,1)S(1)}, u32[]{:S(2)}, u32[]{:S(2)}) collective-permute-start(bf16[768,128]{1,0:T(8,128)(2,1)S(1)} %get-tuple-element.106), channel_id=1, source_target_pairs={{0,1},{1,0},{2,3},{3,2},{4,5},{5,4},{6,7},{7,6},{8,9},{9,8},{10,11... | collective-permute-start | bytes 589832 | tf_op jit(solution)/shard_map/ppermute | solution.py:553
  29.3 1.9 %collective-permute-start.9 = (bf16[768,128]{1,0:T(8,128)(2,1)S(1)}, bf16[768,128]{1,0:T(8,128)(2,1)S(1)}, u32[]{:S(2)}, u32[]{:S(2)}) collective-permute-start(bf16[768,128]{1,0:T(8,128)(2,1)S(1)} %get-tuple-element.108), channel_id=1, source_target_pairs={{0,1},{1,0},{2,3},{3,2},{4,5},{5,4},{6,7},{7,6},{8,9},{9,8},{10,11... | collective-permute-start | bytes 589832 | tf_op jit(solution)/shard_map/ppermute | solution.py:553
  36.6 18.7 %collective-permute-start.11 = (bf16[96,3200]{1,0:T(8,128)(2,1)S(1)}, bf16[96,3200]{1,0:T(8,128)(2,1)S(1)}, u32[]{:S(2)}, u32[]{:S(2)}) collective-permute-start(bf16[96,3200]{1,0:T(8,128)(2,1)S(1)} %get-tuple-element.115), channel_id=1, source_target_pairs={{0,16},{8,24},{16,0},{24,8},{1,17},{9,25},{17,1},{25,9},{2,18},{10... | collective-permute-start | bytes 1843208 | tf_op jit(solution)/shard_map/ppermute | solution.py:553
  38.3 17.0 %collective-permute-start.10 = (bf16[96,2944]{1,0:T(8,128)(2,1)S(1)}, bf16[96,2944]{1,0:T(8,128)(2,1)S(1)}, u32[]{:S(2)}, u32[]{:S(2)}) collective-permute-start(bf16[96,2944]{1,0:T(8,128)(2,1)S(1)} %get-tuple-element.114), channel_id=1, source_target_pairs={{0,8},{8,0},{16,24},{24,16},{1,9},{9,1},{17,25},{25,17},{2,10},{10... | collective-permute-start | bytes 1695752 | tf_op jit(solution)/shard_map/ppermute | solution.py:553
  39.8 1.4 %collective-permute-start.13 = (bf16[768,128]{1,0:T(8,128)(2,1)S(1)}, bf16[768,128]{1,0:T(8,128)(2,1)S(1)}, u32[]{:S(2)}, u32[]{:S(2)}) collective-permute-start(bf16[768,128]{1,0:T(8,128)(2,1)S(1)} %get-tuple-element.120), channel_id=1, source_target_pairs={{0,1},{1,0},{2,3},{3,2},{4,5},{5,4},{6,7},{7,6},{8,9},{9,8},{10,11... | collective-permute-start | bytes 589832 | tf_op jit(solution)/shard_map/ppermute | solution.py:553
  41.3 14.0 %collective-permute-start.14 = (bf16[864,128]{1,0:T(8,128)(2,1)S(1)}, bf16[864,128]{1,0:T(8,128)(2,1)S(1)}, u32[]{:S(2)}, u32[]{:S(2)}) collective-permute-start(bf16[864,128]{1,0:T(8,128)(2,1)S(1)} %get-tuple-element.122), channel_id=1, source_target_pairs={{0,6},{1,7},{2,4},{3,5},{4,2},{5,3},{6,0},{7,1},{8,14},{9,15},{10,... | collective-permute-start | bytes 663560 | tf_op jit(solution)/shard_map/ppermute | solution.py:553
  44.8 10.4 %collective-permute-start.12 = (bf16[832,128]{1,0:T(8,128)(2,1)S(1)}, bf16[832,128]{1,0:T(8,128)(2,1)S(1)}, u32[]{:S(2)}, u32[]{:S(2)}) collective-permute-start(bf16[832,128]{1,0:T(8,128)(2,1)S(1)} %shard_map.142), channel_id=1, source_target_pairs={{0,2},{1,3},{2,0},{3,1},{4,6},{5,7},{6,4},{7,5},{8,10},{9,11},{10,... | collective-permute-start | bytes 638984 | tf_op jit(solution)/shard_map/ppermute | solution.py:553
  55.5 14.9 %copy-start.5 = (s32[1,4]{1,0:T(1,128)S(1)}, s32[1,4]{1,0:T(1,128)}, u32[]{:S(2)}) copy-start(s32[1,4]{1,0:T(1,128)} %heights_ref.3) | copy-start | bytes 52
  55.5 14.9 %copy-start.6 = (s32[1,4]{1,0:T(1,128)S(1)}, s32[1,4]{1,0:T(1,128)}, u32[]{:S(2)}) copy-start(s32[1,4]{1,0:T(1,128)} %widths_ref.3) | copy-start | bytes 52
  55.5 17.2 %collective-permute-start.17 = (bf16[96,3200]{1,0:T(8,128)(2,1)S(1)}, bf16[96,3200]{1,0:T(8,128)(2,1)S(1)}, u32[]{:S(2)}, u32[]{:S(2)}) collective-permute-start(bf16[96,3200]{1,0:T(8,128)(2,1)S(1)} %add_convert_fusion.high_ref), channel_id=1, source_target_pairs={{0,8},{8,0},{16,24},{24,16},{1,9},{9,1},{17,25},{25,17},{2,10},{10... | collective-permute-start | bytes 1843208 | tf_op jit(solution)/shard_map/ppermute | solution.py:553
  56.2 16.5 %collective-permute-start.16 = (bf16[96,2944]{1,0:T(8,128)(2,1)S(1)}, bf16[96,2944]{1,0:T(8,128)(2,1)S(1)}, u32[]{:S(2)}, u32[]{:S(2)}) collective-permute-start(bf16[96,2944]{1,0:T(8,128)(2,1)S(1)} %add_convert_fusion.1.low_ref), channel_id=1, source_target_pairs={{0,16},{8,24},{16,0},{24,8},{1,17},{9,25},{17,1},{25,9},{2,18},{10... | collective-permute-start | bytes 1695752 | tf_op jit(solution)/shard_map/ppermute | solution.py:553
  56.8 12.1 %collective-permute-start.15 = (bf16[832,128]{1,0:T(8,128)(2,1)S(1)}, bf16[832,128]{1,0:T(8,128)(2,1)S(1)}, u32[]{:S(2)}, u32[]{:S(2)}) collective-permute-start(bf16[832,128]{1,0:T(8,128)(2,1)S(1)} %shard_map.143), channel_id=1, source_target_pairs={{0,4},{1,5},{2,6},{3,7},{4,0},{5,1},{6,2},{7,3},{8,12},{9,13},{10,... | collective-permute-start | bytes 638984 | tf_op jit(solution)/shard_map/ppermute | solution.py:553
  58.9 4.0 %collective-permute-start.18 = (f32[8,640]{1,0:T(8,128)S(1)}, f32[8,640]{1,0:T(8,128)S(1)}, u32[]{:S(2)}, u32[]{:S(2)}) collective-permute-start(f32[8,640]{1,0:T(8,128)S(1)} %shard_map.148), channel_id=1, source_target_pairs={{0,2},{1,3},{2,0},{3,1},{4,6},{5,7},{6,4},{7,5},{8,10},{9,11},{10,... | collective-permute-start | bytes 61448 | tf_op jit(solution)/shard_map/ppermute | solution.py:553
  62.9 11.5 %collective-permute-start.21 = (f32[8,640]{1,0:T(8,128)S(1)}, f32[8,640]{1,0:T(8,128)S(1)}, u32[]{:S(2)}, u32[]{:S(2)}) collective-permute-start(f32[8,640]{1,0:T(8,128)S(1)} %add.20), channel_id=1, source_target_pairs={{0,24},{8,16},{16,8},{24,0},{1,25},{9,17},{17,9},{25,1},{2,26},{10... | collective-permute-start | bytes 61448 | tf_op jit(solution)/shard_map/ppermute | solution.py:553
  64.2 10.2 %collective-permute-start.20 = (f32[8,640]{1,0:T(8,128)S(1)}, f32[8,640]{1,0:T(8,128)S(1)}, u32[]{:S(2)}, u32[]{:S(2)}) collective-permute-start(f32[8,640]{1,0:T(8,128)S(1)} %add.20), channel_id=1, source_target_pairs={{0,16},{8,24},{16,0},{24,8},{1,17},{9,25},{17,1},{25,9},{2,18},{10... | collective-permute-start | bytes 61448 | tf_op jit(solution)/shard_map/ppermute | solution.py:553
  68.8 5.6 %collective-permute-start.19 = (f32[8,640]{1,0:T(8,128)S(1)}, f32[8,640]{1,0:T(8,128)S(1)}, u32[]{:S(2)}, u32[]{:S(2)}) collective-permute-start(f32[8,640]{1,0:T(8,128)S(1)} %add.20), channel_id=1, source_target_pairs={{0,8},{8,0},{16,24},{24,16},{1,9},{9,1},{17,25},{25,17},{2,10},{10... | collective-permute-start | bytes 61448 | tf_op jit(solution)/shard_map/ppermute | solution.py:553

commit v4 on v3

--- a/solution.py
+++ b/solution.py
@@ -422,18 +422,21 @@
     )
 
 
-def weight_grad_kernel(pairs, low_taps, owned, *refs):
-    turned, act, sums, embed = (
-        [ref[...] for ref in refs[i * pairs : (i + 1) * pairs]] for i in range(4)
-    )
-    outs = refs[4 * pairs :]
+def early_grad_kernel(pairs, *refs):
+    turned, act = ([ref[...] for ref in refs[i * pairs : (i + 1) * pairs]] for i in range(2))
+    refs[-1][...] = dot(jnp.concatenate(turned, axis=1), jnp.concatenate(act, axis=0))
+
+
+def weight_grad_kernel(pairs, low_taps, owned, early_ref, turned_ref, act_ref, *refs):
+    sums, embed = ([ref[...] for ref in refs[i * pairs : (i + 1) * pairs]] for i in range(2))
+    outs = refs[2 * pairs :]
 
     def put(part, columns, values):
         outs[part][:, columns] = values[:owned].astype(bf16)
 
-    channels = act[0].shape[1]
-    padded = turned[0].shape[0] // 9
-    grad = dot(jnp.concatenate(turned, axis=1), jnp.concatenate(act, axis=0))
+    channels = act_ref.shape[1]
+    padded = turned_ref.shape[0] // 9
+    grad = early_ref[...] + dot(turned_ref[...], act_ref[...])
     for t in range(9):
         part, place = (0, t) if t < low_taps else (1, t - low_taps)
         columns = slice(place * channels, (place + 1) * channels)
@@ -520,7 +523,13 @@
     grad_ref[...] = (rstd_ref[...] * (grad - mean_grad - normed * mean_cross)).astype(bf16)
 
 
-def finish_kernel(scale, low_ref, low_met_ref, high_ref, high_met_ref, conv_ref, time_ref):
+def finish_kernel(scale, low_ref, low_met_ref, high_ref, high_met_ref, *refs):
+    conv_ref, time_ref, gain_ref, shift_ref = refs[-4:]
+    values = [ref[...] for ref in refs[:-4]]
+    while len(values) > 1:
+        values = [a + b for a, b in zip(values[::2], values[1::2])]
+    gain_ref[...] = (values[0][0:1, :] * scale).reshape(-1)
+    shift_ref[...] = (values[0][1:2, :] * scale).reshape(-1)
     low = (low_ref[...].astype(f32) + low_met_ref[...].astype(f32)) * scale
     width = conv_ref.shape[1] - high_ref.shape[1]
     conv_ref[:, :width] = low[:, :width]
@@ -668,8 +677,21 @@
         terms = made[2]
         normed.append(list(made[3:]))
         if 1 < k < last:
-            arrived, here, terms = together(arrive(k + 1), here, terms)
+            arrived, here, terms, normed[0][0] = together(
+                arrive(k + 1), here, terms, normed[0][0]
+            )
             near.append(arrived)
+        if k == last - 1:
+            early = call(
+                functools.partial(early_grad_kernel, last),
+                shape((9 * padded, channels), f32),
+                [],
+                min(60, 6 * chips),
+                0,
+                1.0,
+                *(result[i] for i in range(2) for result in normed),
+            )
+            here, early = together(here, early)
 
     met = [exchange(ours[k][1], "fsdp", 1) for k in range(chips)]
 
@@ -696,8 +718,10 @@
         [],
         min(60, 6 * chips),
         0,
-        1.5,
-        *(result[i] for i in range(4) for result in normed),
+        1.0,
+        early,
+        *normed[last][:2],
+        *(result[i] for i in (2, 3) for result in normed),
     )
     part, terms = call(
         join_last_kernel,
@@ -714,12 +738,12 @@
 
     bits = [1 << i for i in range((replicas - 1).bit_length())]
     totals = [low, high]
-    early = [1, last] if last > 1 else [1]
+    firsts = [1, last] if last > 1 else [1]
     for step in range(len(bits)):
         orders = (bits[step], bits[-1 - step])
         received = [exchange(t, "dp", bit) for t, bit in zip(totals, orders)]
         if step == 0:
-            for k in early:
+            for k in firsts:
                 grads[k] = exchange(grads[k], "fsdp", 2 * k)
             received, grads, terms = together(received, grads, terms)
         if step < len(bits) - 1:
@@ -727,25 +751,13 @@
                 (t.astype(f32) + r.astype(f32)).astype(bf16) for t, r in zip(totals, received)
             ]
     for k in range(1, chips):
-        if k not in early:
+        if k not in firsts:
             grads[k] = exchange(grads[k], "fsdp", 2 * k)
     terms = call(
         add_terms_kernel, shape((8, channels), f32), [], 8, 0, 0.1, terms, grads[last]
     )
     for i in range((chips - 1).bit_length() - 1):
         terms = terms + exchange(terms, "fsdp", 2 << i)
-    grad_conv, grad_time = call(
-        functools.partial(finish_kernel, scale),
-        (shape((owned, 9 * channels), f32), shape((owned, feature_count), f32)),
-        [],
-        16,
-        0,
-        1.5,
-        totals[0],
-        received[0],
-        totals[1],
-        received[1],
-    )
     block_out, grad_features = call(
         functools.partial(norm_grad_kernel, owned, chips),
         (
@@ -766,11 +778,21 @@
         norm_shift,
     )
     values = [terms] + [exchange(terms, "dp", bit) for bit in range(1, replicas)]
-    grad_time, *values = together(grad_time, *values)
-    while len(values) > 1:
-        values = [a + b for a, b in zip(values[::2], values[1::2])]
-    terms = values[0] * scale
-    return (block_out, grad_features, grad_conv, grad_time, terms[0], terms[1])
+    grad_conv, grad_time, grad_gain, grad_shift = call(
+        functools.partial(finish_kernel, scale),
+        (shape((owned, 9 * channels), f32), shape((owned, feature_count), f32))
+        + (shape((channels,), f32),) * 2,
+        [],
+        16,
+        0,
+        1.5,
+        totals[0],
+        received[0],
+        totals[1],
+        received[1],
+        *values,
+    )
+    return (block_out, grad_features, grad_conv, grad_time, grad_gain, grad_shift)
 
 
 def solution(mesh):

time: 75.2 us -> 74.4 us (0.989)
    pallas_call x13 -> x14, Pallas kernels: 23.8 us -> 24.2 us  [call(): pl.pallas_call(kernel, out_shape=outs, in_specs=[smem] * scalars + [vmem]...]
  transfers between devices with their start and end apart: 22 -> 22, of which waited for: 10 -> 8; matrix products, arithmetic and copies ran while one was open for 0% -> 0% of each run, Pallas kernels for 21% -> 21%
where the time goes in v4:
time: 74.4 us; the launch traced here: 74.2 us
  waiting for transfers between devices  25.3 us (34%)
  Pallas kernels  24.2 us (33%)
  starting transfers between devices  22.7 us (31%)
  local copies, waits for them, and re-layouts  0.96 us (1%)
  between operations  0.86 us (1%)
    ppermute x22, waiting for transfers between devices, exchange(): return lax.ppermute(value, axis, [(i, i ^ bit) for i in range(size)])  25.3 us
    pallas_call x14, Pallas kernels, call(): pl.pallas_call(kernel, out_shape=outs, in_specs=[smem] * scalars + [vmem]...  24.2 us
    ppermute x22, starting transfers between devices, exchange(): return lax.ppermute(value, axis, [(i, i ^ bit) for i in range(size)])  22.7 us
  transfers between devices with their start and end apart: 22, of which 8 were waited for; matrix products, arithmetic and copies ran while one was open for 0% of the time, Pallas kernels for 21%

profile of v4, /device:TPU:0, one launch (start us, length us, event | category | flops | bytes accessed | tf_op | source)
XLA Modules:
  0.0 74.2 jit_solution(4913010730907062797)
XLA Ops:
  0.7 2.2 %shard_map.136 = (bf16[848,128]{1,0:T(8,128)(2,1)}, bf16[848,128]{1,0:T(8,128)(2,1)}, bf16[1040,128]{1,0:T(8,128)(2,1)}) custom-call(s32[1]{0:T(128)} %bitcast.me_ref, s32[1,4]{1,0:T(1,128)} %heights_ref.3, s32[1,4]{1,0:T(1,128)} %widths_ref.3, s32[1,4]{1,0:T(1,128)} %times_ref.1, bf16[128,640]{1,0:T(8,128)(2,1)} %features_ref.1, bf16[128,768]{1,0:T(8,128)(2,1)} %cotan_ref.1), custom_call_target="tpu_custom_call" | custom-call | flops 2000000000 | bytes 6000000 | tf_op jit(solution)/shard_map/pallas_call | solution.py:543
  2.9 0.5 collective-permute-start.2
  3.4 3.6 %collective-permute-start = (bf16[1040,128]{1,0:T(8,128)(2,1)}, bf16[1040,128]{1,0:T(8,128)(2,1)S(1)}, u32[]{:S(2)}, u32[]{:S(2)}) collective-permute-start(bf16[1040,128]{1,0:T(8,128)(2,1)} %get-tuple-element.74), channel_id=1, source_target_pairs={{0,4},{1,5},{2,6},{3,7},{4,0},{5,1},{6,2},{7,3},{8,12},{9,13},{10,... | collective-permute-start | bytes 798728 | tf_op jit(solution)/shard_map/ppermute | solution.py:562
  7.0 1.6 %collective-permute-start.1 = (bf16[848,128]{1,0:T(8,128)(2,1)}, bf16[848,128]{1,0:T(8,128)(2,1)S(1)}, u32[]{:S(2)}, u32[]{:S(2)}) collective-permute-start(bf16[848,128]{1,0:T(8,128)(2,1)} %get-tuple-element.75), channel_id=1, source_target_pairs={{0,2},{1,3},{2,0},{3,1},{4,6},{5,7},{6,4},{7,5},{8,10},{9,11},{10,... | collective-permute-start | bytes 651272 | tf_op jit(solution)/shard_map/ppermute | solution.py:562
  8.5 0.0 collective-permute-done.2.far_ref
  8.6 0.9 %copy-done.1 = bf16[848,128]{1,0:T(8,128)(2,1)S(1)} copy-done((bf16[848,128]{1,0:T(8,128)(2,1)S(1)}, bf16[848,128]{1,0:T(8,128)(2,1)}, u32[]{:S(2)}) %copy-start.1) | copy-done | bytes 217112
  9.5 4.6 %shard_map.137 = (bf16[736,128]{1,0:T(8,128)(2,1)S(1)}, bf16[768,128]{1,0:T(8,128)(2,1)S(1)}, f32[8,640]{1,0:T(8,128)S(1)}, bf16[864,256]{1,0:T(8,128)(2,1)S(1)}...) custom-call(s32[1]{0:T(128)} %bitcast.me_ref, ...), custom_call_target="tpu_custom_call" | custom-call | flops 1000000000 | bytes 3000000 | tf_op jit(solution)/shard_map/pallas_call | solution.py:543
  14.1 4.2 %collective-permute-done.1.near_ref = bf16[848,128]{1,0:T(8,128)(2,1)S(1)} collective-permute-done((bf16[848,128]{1,0:T(8,128)(2,1)}, bf16[848,128]{1,0:T(8,128)(2,1)S(1)}, u32[]{:S(2)}, u32[]{:S(2)}) %collective-permute-start.1) | collective-permute-done | bytes 217120 | tf_op jit(solution)/shard_map/ppermute | solution.py:562
  18.3 1.6 %collective-permute-done.near_ref = bf16[1040,128]{1,0:T(8,128)(2,1)S(1)} collective-permute-done((bf16[1040,128]{1,0:T(8,128)(2,1)}, bf16[1040,128]{1,0:T(8,128)(2,1)S(1)}, u32[]{:S(2)}, u32[]{:S(2)}) %collective-permute-start) | collective-permute-done | bytes 266272 | tf_op jit(solution)/shard_map/ppermute | solution.py:562
  19.9 0.0 collective-permute-start.4
  19.9 1.2 %collective-permute-start.3 = (bf16[1040,128]{1,0:T(8,128)(2,1)S(1)}, bf16[1040,128]{1,0:T(8,128)(2,1)S(1)}, u32[]{:S(2)}, u32[]{:S(2)}) collective-permute-start(bf16[1040,128]{1,0:T(8,128)(2,1)S(1)} %collective-permute-done.near_ref), channel_id=1, source_target_pairs={{0,2},{1,3},{2,0},{3,1},{4,6},{5,7},{6,4},{7,5},{8,10},{9,11},{10,... | collective-permute-start | bytes 798728 | tf_op jit(solution)/shard_map/ppermute | solution.py:562
  21.2 0.0 collective-permute-done.5.far_ref
  21.2 3.7 %shard_map.138 = (bf16[736,128]{1,0:T(8,128)(2,1)S(1)}, bf16[768,128]{1,0:T(8,128)(2,1)S(1)}, f32[8,640]{1,0:T(8,128)S(1)}, bf16[864,256]{1,0:T(8,128)(2,1)S(1)}...) custom-call(s32[1]{0:T(128)} %bitcast.me_ref, ...), custom_call_target="tpu_custom_call" | custom-call | flops 1000000000 | bytes 3000000 | tf_op jit(solution)/shard_map/pallas_call | solution.py:543
  24.9 3.7 %shard_map.139 = (bf16[736,128]{1,0:T(8,128)(2,1)S(1)}, bf16[768,128]{1,0:T(8,128)(2,1)S(1)}, f32[8,640]{1,0:T(8,128)S(1)}, bf16[864,256]{1,0:T(8,128)(2,1)S(1)}...) custom-call(s32[1]{0:T(128)} %bitcast.me_ref, ...), custom_call_target="tpu_custom_call" | custom-call | flops 1000000000 | bytes 3000000 | tf_op jit(solution)/shard_map/pallas_call | solution.py:543
  28.7 0.1 collective-permute-done.3.near_ref
  28.8 0.0 collective-permute-start.6
  28.8 0.5 collective-permute-start.7
  29.3 0.1 collective-permute-start.8
  29.3 0.5 collective-permute-start.9
  29.8 0.8 %collective-permute-done.7.met_ref = bf16[768,128]{1,0:T(8,128)(2,1)S(1)} collective-permute-done((bf16[768,128]{1,0:T(8,128)(2,1)S(1)}, bf16[768,128]{1,0:T(8,128)(2,1)S(1)}, u32[]{:S(2)}, u32[]{:S(2)}) %collective-permute-start.7) | collective-permute-done | bytes 196640 | tf_op jit(solution)/shard_map/ppermute | solution.py:562
  30.6 1.2 %shard_map.140.early_ref = f32[864,640]{1,0:T(8,128)S(1)} custom-call(bf16[864,256]{1,0:T(8,128)(2,1)S(1)} %get-tuple-element.90.refs_0_, bf16[864,256]{1,0:T(8,128)(2,1)S(1)} %get-tuple-element.91.refs_1_, bf16[864,256]{1,0:T(8,128)(2,1)S(1)} %get-tuple-element.92.refs_2_, bf16[256,640]{1,0:T(8,128)(2,1)S(1)} %get-tuple-element.93.refs_3_, ...), custom_call_target="tpu_custom_call" | custom-call | flops 500000000 | bytes 1500000 | tf_op jit(solution)/shard_map/pallas_call | solution.py:543
  31.8 0.0 collective-permute-done.8.met_ref
  31.9 0.0 collective-permute-done.9.met_ref
  32.0 3.9 %shard_map.141 = (bf16[736,128]{1,0:T(8,128)(2,1)S(1)}, bf16[768,128]{1,0:T(8,128)(2,1)S(1)}, f32[8,640]{1,0:T(8,128)S(1)}, bf16[864,256]{1,0:T(8,128)(2,1)S(1)}...) custom-call(s32[1]{0:T(128)} %bitcast.me_ref, ...), custom_call_target="tpu_custom_call" | custom-call | flops 1000000000 | bytes 3000000 | tf_op jit(solution)/shard_map/pallas_call | solution.py:543
  35.9 0.6 shard_map.145
  36.4 1.6 %collective-permute-start.11 = (bf16[96,3200]{1,0:T(8,128)(2,1)S(1)}, bf16[96,3200]{1,0:T(8,128)(2,1)S(1)}, u32[]{:S(2)}, u32[]{:S(2)}) collective-permute-start(bf16[96,3200]{1,0:T(8,128)(2,1)S(1)} %get-tuple-element.118), channel_id=1, source_target_pairs={{0,16},{8,24},{16,0},{24,8},{1,17},{9,25},{17,1},{25,9},{2,18},{10... | collective-permute-start | bytes 1843208 | tf_op jit(solution)/shard_map/ppermute | solution.py:562
  38.1 1.5 %collective-permute-start.10 = (bf16[96,2944]{1,0:T(8,128)(2,1)S(1)}, bf16[96,2944]{1,0:T(8,128)(2,1)S(1)}, u32[]{:S(2)}, u32[]{:S(2)}) collective-permute-start(bf16[96,2944]{1,0:T(8,128)(2,1)S(1)} %get-tuple-element.117), channel_id=1, source_target_pairs={{0,8},{8,0},{16,24},{24,16},{1,9},{9,1},{17,25},{25,17},{2,10},{10... | collective-permute-start | bytes 1695752 | tf_op jit(solution)/shard_map/ppermute | solution.py:562
  39.6 0.0 collective-permute-start.13
  39.6 1.4 %collective-permute-done.13.met_ref = bf16[768,128]{1,0:T(8,128)(2,1)S(1)} collective-permute-done((bf16[768,128]{1,0:T(8,128)(2,1)S(1)}, bf16[768,128]{1,0:T(8,128)(2,1)S(1)}, u32[]{:S(2)}, u32[]{:S(2)}) %collective-permute-start.13) | collective-permute-done | bytes 196640 | tf_op jit(solution)/shard_map/ppermute | solution.py:562
  41.0 0.1 shard_map.146
  41.1 3.6 %collective-permute-start.14 = (bf16[864,128]{1,0:T(8,128)(2,1)S(1)}, bf16[864,128]{1,0:T(8,128)(2,1)S(1)}, u32[]{:S(2)}, u32[]{:S(2)}) collective-permute-start(bf16[864,128]{1,0:T(8,128)(2,1)S(1)} %get-tuple-element.125), channel_id=1, source_target_pairs={{0,6},{1,7},{2,4},{3,5},{4,2},{5,3},{6,0},{7,1},{8,14},{9,15},{10,... | collective-permute-start | bytes 663560 | tf_op jit(solution)/shard_map/ppermute | solution.py:562
  44.6 10.4 %collective-permute-done.12.refs_1_ = bf16[832,128]{1,0:T(8,128)(2,1)S(1)} collective-permute-done((bf16[832,128]{1,0:T(8,128)(2,1)S(1)}, bf16[832,128]{1,0:T(8,128)(2,1)S(1)}, u32[]{:S(2)}, u32[]{:S(2)}) %collective-permute-start.12) | collective-permute-done | bytes 213024 | tf_op jit(solution)/shard_map/ppermute | solution.py:562
  55.1 0.0 collective-permute-done.14.refs_3_.met_ref
  55.1 0.1 add_convert_fusion.high_ref
  55.2 0.0 copy-start.5
  55.3 0.0 copy-start.6
  55.3 0.6 collective-permute-start.17
  55.9 0.1 add_convert_fusion.1.low_ref
  56.0 0.5 collective-permute-start.16
  56.5 2.2 %collective-permute-start.15 = (bf16[832,128]{1,0:T(8,128)(2,1)S(1)}, bf16[832,128]{1,0:T(8,128)(2,1)S(1)}, u32[]{:S(2)}, u32[]{:S(2)}) collective-permute-start(bf16[832,128]{1,0:T(8,128)(2,1)S(1)} %shard_map.144), channel_id=1, source_target_pairs={{0,4},{1,5},{2,6},{3,7},{4,0},{5,1},{6,2},{7,3},{8,12},{9,13},{10,... | collective-permute-start | bytes 638984 | tf_op jit(solution)/shard_map/ppermute | solution.py:562
  58.8 1.2 %collective-permute-start.18 = (f32[8,640]{1,0:T(8,128)S(1)}, f32[8,640]{1,0:T(8,128)S(1)}, u32[]{:S(2)}, u32[]{:S(2)}) collective-permute-start(f32[8,640]{1,0:T(8,128)S(1)} %shard_map.148), channel_id=1, source_target_pairs={{0,2},{1,3},{2,0},{3,1},{4,6},{5,7},{6,4},{7,5},{8,10},{9,11},{10,... | collective-permute-start | bytes 61448 | tf_op jit(solution)/shard_map/ppermute | solution.py:562
  60.0 2.7 %collective-permute-done.18 = f32[8,640]{1,0:T(8,128)S(1)} collective-permute-done((f32[8,640]{1,0:T(8,128)S(1)}, f32[8,640]{1,0:T(8,128)S(1)}, u32[]{:S(2)}, u32[]{:S(2)}) %collective-permute-start.18) | collective-permute-done | bytes 20512 | tf_op jit(solution)/shard_map/ppermute | solution.py:562
  62.8 1.3 %collective-permute-start.21 = (f32[8,640]{1,0:T(8,128)S(1)}, f32[8,640]{1,0:T(8,128)S(1)}, u32[]{:S(2)}, u32[]{:S(2)}) collective-permute-start(f32[8,640]{1,0:T(8,128)S(1)} %add.11.refs_0_), channel_id=1, source_target_pairs={{0,24},{8,16},{16,8},{24,0},{1,25},{9,17},{17,9},{25,1},{2,26},{10... | collective-permute-start | bytes 61448 | tf_op jit(solution)/shard_map/ppermute | solution.py:562
  64.1 0.6 collective-permute-start.20
  64.7 3.9 %collective-permute-done.15.refs_2_ = bf16[832,128]{1,0:T(8,128)(2,1)S(1)} collective-permute-done((bf16[832,128]{1,0:T(8,128)(2,1)S(1)}, bf16[832,128]{1,0:T(8,128)(2,1)S(1)}, u32[]{:S(2)}, u32[]{:S(2)}) %collective-permute-start.15) | collective-permute-done | bytes 213024 | tf_op jit(solution)/shard_map/ppermute | solution.py:562
  68.6 1.5 %collective-permute-start.19 = (f32[8,640]{1,0:T(8,128)S(1)}, f32[8,640]{1,0:T(8,128)S(1)}, u32[]{:S(2)}, u32[]{:S(2)}) collective-permute-start(f32[8,640]{1,0:T(8,128)S(1)} %add.11.refs_0_), channel_id=1, source_target_pairs={{0,8},{8,0},{16,24},{24,16},{1,9},{9,1},{17,25},{25,17},{2,10},{10... | collective-permute-start | bytes 61448 | tf_op jit(solution)/shard_map/ppermute | solution.py:562
  70.2 2.3 %shard_map.147 = (bf16[128,768]{1,0:T(8,128)(2,1)}, bf16[128,640]{1,0:T(8,128)(2,1)}) custom-call(s32[1]{0:T(128)} %bitcast.me_ref, s32[1,4]{1,0:T(1,128)S(1)} %copy-done.5, s32[1,4]{1,0:T(1,128)S(1)} %copy-done.6, f32[832,128]{1,0:T(8,128)S(1)} %shard_map.142.refs_0_, bf16[832,128]{1,0:T(8,128)(2,1)S(1)} %collective-permute-done.12.refs_1_, ...), custom_call_target="tpu_custom_call" | custom-call | flops 1250000000 | bytes 3750000 | tf_op jit(solution)/shard_map/pallas_call | solution.py:543
  72.5 1.7 %shard_map.149 = (f32[96,5760]{1,0:T(8,128)}, f32[96,320]{1,0:T(8,128)}, f32[640]{0:T(1024)}, f32[640]{0:T(1024)}) custom-call(bf16[96,2944]{1,0:T(8,128)(2,1)S(1)} %add_convert_fusion.1.low_ref, bf16[96,2944]{1,0:T(8,128)(2,1)S(1)} %collective-permute-done.16.low_met_ref, bf16[96,3200]{1,0:T(8,128)(2,1)S(1)} %add_convert_fusion.high_ref, ...), custom_call_target="tpu_custom_call" | custom-call | flops 750000000 | bytes 2250000 | tf_op jit(solution)/shard_map/pallas_call | solution.py:543
  (27 shorter events, 0.2 us)
Async XLA Ops:
  0.6 7.9 %copy-start = (bf16[96,5760]{1,0:T(8,128)(2,1)S(1)}, bf16[96,5760]{1,0:T(8,128)(2,1)}, u32[]{:S(2)}) copy-start(bf16[96,5760]{1,0:T(8,128)(2,1)} %refs_0_.1) | copy-start | bytes 3317764
  0.6 7.9 %copy-start.2 = (bf16[96,320]{1,0:T(8,128)(2,1)S(1)}, bf16[96,320]{1,0:T(8,128)(2,1)}, u32[]{:S(2)}) copy-start(bf16[96,320]{1,0:T(8,128)(2,1)} %refs_1_.1) | copy-start | bytes 184324
  0.7 7.9 %copy-start.3 = (f32[640]{0:T(1024)S(1)}, f32[640]{0:T(1024)}, u32[]{:S(2)}) copy-start(f32[640]{0:T(1024)} %refs_6_.1) | copy-start | bytes 7684
  0.7 7.9 %copy-start.4 = (f32[640]{0:T(1024)S(1)}, f32[640]{0:T(1024)}, u32[]{:S(2)}) copy-start(f32[640]{0:T(1024)} %refs_7_.1) | copy-start | bytes 7684
  2.9 5.6 %collective-permute-start.2 = (bf16[848,128]{1,0:T(8,128)(2,1)}, bf16[848,128]{1,0:T(8,128)(2,1)S(1)}, u32[]{:S(2)}, u32[]{:S(2)}) collective-permute-start(bf16[848,128]{1,0:T(8,128)(2,1)} %get-tuple-element.76.near_ref), channel_id=1, source_target_pairs={{0,1},{1,0},{2,3},{3,2},{4,5},{5,4},{6,7},{7,6},{8,9},{9,8},{10,11... | collective-permute-start | bytes 651272 | tf_op jit(solution)/shard_map/ppermute | solution.py:562
  3.4 16.6 %collective-permute-start = (bf16[1040,128]{1,0:T(8,128)(2,1)}, bf16[1040,128]{1,0:T(8,128)(2,1)S(1)}, u32[]{:S(2)}, u32[]{:S(2)}) collective-permute-start(bf16[1040,128]{1,0:T(8,128)(2,1)} %get-tuple-element.74), channel_id=1, source_target_pairs={{0,4},{1,5},{2,6},{3,7},{4,0},{5,1},{6,2},{7,3},{8,12},{9,13},{10,... | collective-permute-start | bytes 798728 | tf_op jit(solution)/shard_map/ppermute | solution.py:562
  7.0 11.3 %collective-permute-start.1 = (bf16[848,128]{1,0:T(8,128)(2,1)}, bf16[848,128]{1,0:T(8,128)(2,1)S(1)}, u32[]{:S(2)}, u32[]{:S(2)}) collective-permute-start(bf16[848,128]{1,0:T(8,128)(2,1)} %get-tuple-element.75), channel_id=1, source_target_pairs={{0,2},{1,3},{2,0},{3,1},{4,6},{5,7},{6,4},{7,5},{8,10},{9,11},{10,... | collective-permute-start | bytes 651272 | tf_op jit(solution)/shard_map/ppermute | solution.py:562
  8.6 0.9 %copy-start.1 = (bf16[848,128]{1,0:T(8,128)(2,1)S(1)}, bf16[848,128]{1,0:T(8,128)(2,1)}, u32[]{:S(2)}) copy-start(bf16[848,128]{1,0:T(8,128)(2,1)} %get-tuple-element.76.near_ref) | copy-start | bytes 651268
  18.3 2.9 %collective-permute-start.5 = (bf16[848,128]{1,0:T(8,128)(2,1)S(1)}, bf16[848,128]{1,0:T(8,128)(2,1)S(1)}, u32[]{:S(2)}, u32[]{:S(2)}) collective-permute-start(bf16[848,128]{1,0:T(8,128)(2,1)S(1)} %collective-permute-done.1.near_ref), channel_id=1, source_target_pairs={{0,1},{1,0},{2,3},{3,2},{4,5},{5,4},{6,7},{7,6},{8,9},{9,8},{10,11... | collective-permute-start | bytes 651272 | tf_op jit(solution)/shard_map/ppermute | solution.py:562
  19.9 5.0 %collective-permute-start.4 = (bf16[1040,128]{1,0:T(8,128)(2,1)S(1)}, bf16[1040,128]{1,0:T(8,128)(2,1)S(1)}, u32[]{:S(2)}, u32[]{:S(2)}) collective-permute-start(bf16[1040,128]{1,0:T(8,128)(2,1)S(1)} %collective-permute-done.near_ref), channel_id=1, source_target_pairs={{0,1},{1,0},{2,3},{3,2},{4,5},{5,4},{6,7},{7,6},{8,9},{9,8},{10,11... | collective-permute-start | bytes 798728 | tf_op jit(solution)/shard_map/ppermute | solution.py:562
  19.9 8.8 %collective-permute-start.3 = (bf16[1040,128]{1,0:T(8,128)(2,1)S(1)}, bf16[1040,128]{1,0:T(8,128)(2,1)S(1)}, u32[]{:S(2)}, u32[]{:S(2)}) collective-permute-start(bf16[1040,128]{1,0:T(8,128)(2,1)S(1)} %collective-permute-done.near_ref), channel_id=1, source_target_pairs={{0,2},{1,3},{2,0},{3,1},{4,6},{5,7},{6,4},{7,5},{8,10},{9,11},{10,... | collective-permute-start | bytes 798728 | tf_op jit(solution)/shard_map/ppermute | solution.py:562
  28.8 3.2 %collective-permute-start.6 = (bf16[1040,128]{1,0:T(8,128)(2,1)S(1)}, bf16[1040,128]{1,0:T(8,128)(2,1)S(1)}, u32[]{:S(2)}, u32[]{:S(2)}) collective-permute-start(bf16[1040,128]{1,0:T(8,128)(2,1)S(1)} %collective-permute-done.3.near_ref), channel_id=1, source_target_pairs={{0,1},{1,0},{2,3},{3,2},{4,5},{5,4},{6,7},{7,6},{8,9},{9,8},{10,11... | collective-permute-start | bytes 798728 | tf_op jit(solution)/shard_map/ppermute | solution.py:562
  28.8 1.8 %collective-permute-start.7 = (bf16[768,128]{1,0:T(8,128)(2,1)S(1)}, bf16[768,128]{1,0:T(8,128)(2,1)S(1)}, u32[]{:S(2)}, u32[]{:S(2)}) collective-permute-start(bf16[768,128]{1,0:T(8,128)(2,1)S(1)} %get-tuple-element.107), channel_id=1, source_target_pairs={{0,1},{1,0},{2,3},{3,2},{4,5},{5,4},{6,7},{7,6},{8,9},{9,8},{10,11... | collective-permute-start | bytes 589832 | tf_op jit(solution)/shard_map/ppermute | solution.py:562
  29.3 2.6 %collective-permute-start.8 = (bf16[768,128]{1,0:T(8,128)(2,1)S(1)}, bf16[768,128]{1,0:T(8,128)(2,1)S(1)}, u32[]{:S(2)}, u32[]{:S(2)}) collective-permute-start(bf16[768,128]{1,0:T(8,128)(2,1)S(1)} %get-tuple-element.109), channel_id=1, source_target_pairs={{0,1},{1,0},{2,3},{3,2},{4,5},{5,4},{6,7},{7,6},{8,9},{9,8},{10,11... | collective-permute-start | bytes 589832 | tf_op jit(solution)/shard_map/ppermute | solution.py:562
  29.3 2.6 %collective-permute-start.9 = (bf16[768,128]{1,0:T(8,128)(2,1)S(1)}, bf16[768,128]{1,0:T(8,128)(2,1)S(1)}, u32[]{:S(2)}, u32[]{:S(2)}) collective-permute-start(bf16[768,128]{1,0:T(8,128)(2,1)S(1)} %get-tuple-element.111), channel_id=1, source_target_pairs={{0,1},{1,0},{2,3},{3,2},{4,5},{5,4},{6,7},{7,6},{8,9},{9,8},{10,11... | collective-permute-start | bytes 589832 | tf_op jit(solution)/shard_map/ppermute | solution.py:562
  36.4 18.7 %collective-permute-start.11 = (bf16[96,3200]{1,0:T(8,128)(2,1)S(1)}, bf16[96,3200]{1,0:T(8,128)(2,1)S(1)}, u32[]{:S(2)}, u32[]{:S(2)}) collective-permute-start(bf16[96,3200]{1,0:T(8,128)(2,1)S(1)} %get-tuple-element.118), channel_id=1, source_target_pairs={{0,16},{8,24},{16,0},{24,8},{1,17},{9,25},{17,1},{25,9},{2,18},{10... | collective-permute-start | bytes 1843208 | tf_op jit(solution)/shard_map/ppermute | solution.py:562
  38.1 17.0 %collective-permute-start.10 = (bf16[96,2944]{1,0:T(8,128)(2,1)S(1)}, bf16[96,2944]{1,0:T(8,128)(2,1)S(1)}, u32[]{:S(2)}, u32[]{:S(2)}) collective-permute-start(bf16[96,2944]{1,0:T(8,128)(2,1)S(1)} %get-tuple-element.117), channel_id=1, source_target_pairs={{0,8},{8,0},{16,24},{24,16},{1,9},{9,1},{17,25},{25,17},{2,10},{10... | collective-permute-start | bytes 1695752 | tf_op jit(solution)/shard_map/ppermute | solution.py:562
  39.6 1.4 %collective-permute-start.13 = (bf16[768,128]{1,0:T(8,128)(2,1)S(1)}, bf16[768,128]{1,0:T(8,128)(2,1)S(1)}, u32[]{:S(2)}, u32[]{:S(2)}) collective-permute-start(bf16[768,128]{1,0:T(8,128)(2,1)S(1)} %get-tuple-element.123), channel_id=1, source_target_pairs={{0,1},{1,0},{2,3},{3,2},{4,5},{5,4},{6,7},{7,6},{8,9},{9,8},{10,11... | collective-permute-start | bytes 589832 | tf_op jit(solution)/shard_map/ppermute | solution.py:562
  41.1 14.0 %collective-permute-start.14 = (bf16[864,128]{1,0:T(8,128)(2,1)S(1)}, bf16[864,128]{1,0:T(8,128)(2,1)S(1)}, u32[]{:S(2)}, u32[]{:S(2)}) collective-permute-start(bf16[864,128]{1,0:T(8,128)(2,1)S(1)} %get-tuple-element.125), channel_id=1, source_target_pairs={{0,6},{1,7},{2,4},{3,5},{4,2},{5,3},{6,0},{7,1},{8,14},{9,15},{10,... | collective-permute-start | bytes 663560 | tf_op jit(solution)/shard_map/ppermute | solution.py:562
  44.6 10.4 %collective-permute-start.12 = (bf16[832,128]{1,0:T(8,128)(2,1)S(1)}, bf16[832,128]{1,0:T(8,128)(2,1)S(1)}, u32[]{:S(2)}, u32[]{:S(2)}) collective-permute-start(bf16[832,128]{1,0:T(8,128)(2,1)S(1)} %shard_map.143), channel_id=1, source_target_pairs={{0,2},{1,3},{2,0},{3,1},{4,6},{5,7},{6,4},{7,5},{8,10},{9,11},{10,... | collective-permute-start | bytes 638984 | tf_op jit(solution)/shard_map/ppermute | solution.py:562
  55.2 14.9 %copy-start.5 = (s32[1,4]{1,0:T(1,128)S(1)}, s32[1,4]{1,0:T(1,128)}, u32[]{:S(2)}) copy-start(s32[1,4]{1,0:T(1,128)} %heights_ref.3) | copy-start | bytes 52
  55.3 14.9 %copy-start.6 = (s32[1,4]{1,0:T(1,128)S(1)}, s32[1,4]{1,0:T(1,128)}, u32[]{:S(2)}) copy-start(s32[1,4]{1,0:T(1,128)} %widths_ref.3) | copy-start | bytes 52
  55.3 17.3 %collective-permute-start.17 = (bf16[96,3200]{1,0:T(8,128)(2,1)S(1)}, bf16[96,3200]{1,0:T(8,128)(2,1)S(1)}, u32[]{:S(2)}, u32[]{:S(2)}) collective-permute-start(bf16[96,3200]{1,0:T(8,128)(2,1)S(1)} %add_convert_fusion.high_ref), channel_id=1, source_target_pairs={{0,8},{8,0},{16,24},{24,16},{1,9},{9,1},{17,25},{25,17},{2,10},{10... | collective-permute-start | bytes 1843208 | tf_op jit(solution)/shard_map/ppermute | solution.py:562
  56.0 16.5 %collective-permute-start.16 = (bf16[96,2944]{1,0:T(8,128)(2,1)S(1)}, bf16[96,2944]{1,0:T(8,128)(2,1)S(1)}, u32[]{:S(2)}, u32[]{:S(2)}) collective-permute-start(bf16[96,2944]{1,0:T(8,128)(2,1)S(1)} %add_convert_fusion.1.low_ref), channel_id=1, source_target_pairs={{0,16},{8,24},{16,0},{24,8},{1,17},{9,25},{17,1},{25,9},{2,18},{10... | collective-permute-start | bytes 1695752 | tf_op jit(solution)/shard_map/ppermute | solution.py:562
  56.5 12.1 %collective-permute-start.15 = (bf16[832,128]{1,0:T(8,128)(2,1)S(1)}, bf16[832,128]{1,0:T(8,128)(2,1)S(1)}, u32[]{:S(2)}, u32[]{:S(2)}) collective-permute-start(bf16[832,128]{1,0:T(8,128)(2,1)S(1)} %shard_map.144), channel_id=1, source_target_pairs={{0,4},{1,5},{2,6},{3,7},{4,0},{5,1},{6,2},{7,3},{8,12},{9,13},{10,... | collective-permute-start | bytes 638984 | tf_op jit(solution)/shard_map/ppermute | solution.py:562
  58.8 4.0 %collective-permute-start.18 = (f32[8,640]{1,0:T(8,128)S(1)}, f32[8,640]{1,0:T(8,128)S(1)}, u32[]{:S(2)}, u32[]{:S(2)}) collective-permute-start(f32[8,640]{1,0:T(8,128)S(1)} %shard_map.148), channel_id=1, source_target_pairs={{0,2},{1,3},{2,0},{3,1},{4,6},{5,7},{6,4},{7,5},{8,10},{9,11},{10,... | collective-permute-start | bytes 61448 | tf_op jit(solution)/shard_map/ppermute | solution.py:562
  62.8 9.7 %collective-permute-start.21 = (f32[8,640]{1,0:T(8,128)S(1)}, f32[8,640]{1,0:T(8,128)S(1)}, u32[]{:S(2)}, u32[]{:S(2)}) collective-permute-start(f32[8,640]{1,0:T(8,128)S(1)} %add.11.refs_0_), channel_id=1, source_target_pairs={{0,24},{8,16},{16,8},{24,0},{1,25},{9,17},{17,9},{25,1},{2,26},{10... | collective-permute-start | bytes 61448 | tf_op jit(solution)/shard_map/ppermute | solution.py:562
  64.1 8.4 %collective-permute-start.20 = (f32[8,640]{1,0:T(8,128)S(1)}, f32[8,640]{1,0:T(8,128)S(1)}, u32[]{:S(2)}, u32[]{:S(2)}) collective-permute-start(f32[8,640]{1,0:T(8,128)S(1)} %add.11.refs_0_), channel_id=1, source_target_pairs={{0,16},{8,24},{16,0},{24,8},{1,17},{9,25},{17,1},{25,9},{2,18},{10... | collective-permute-start | bytes 61448 | tf_op jit(solution)/shard_map/ppermute | solution.py:562
  68.6 3.9 %collective-permute-start.19 = (f32[8,640]{1,0:T(8,128)S(1)}, f32[8,640]{1,0:T(8,128)S(1)}, u32[]{:S(2)}, u32[]{:S(2)}) collective-permute-start(f32[8,640]{1,0:T(8,128)S(1)} %add.11.refs_0_), channel_id=1, source_target_pairs={{0,8},{8,0},{16,24},{24,16},{1,9},{9,1},{17,25},{25,17},{2,10},{10... | collective-permute-start | bytes 61448 | tf_op jit(solution)/shard_map/ppermute | solution.py:562

commit v5 on v4

--- a/solution.py
+++ b/solution.py
@@ -709,6 +709,18 @@
 
     grads = [join(k) for k in range(last)]
     normed[-1][2], *grads = together(normed[-1][2], *grads)
+    part, terms = call(
+        join_last_kernel,
+        (shape((returned + padded + TERM_ROWS, LANES), bf16), shape((TERM_ROWS, LANES), bf16)),
+        [],
+        8,
+        0,
+        0.1,
+        ours[last][0],
+        met[last],
+        terms,
+    )
+    normed[last][2], part, terms = together(normed[last][2], part, terms)
     low, high = call(
         functools.partial(weight_grad_kernel, chips, low_taps, owned),
         (
@@ -722,17 +734,6 @@
         early,
         *normed[last][:2],
         *(result[i] for i in (2, 3) for result in normed),
-    )
-    part, terms = call(
-        join_last_kernel,
-        (shape((returned + padded + TERM_ROWS, LANES), bf16), shape((TERM_ROWS, LANES), bf16)),
-        [],
-        8,
-        0,
-        0.1,
-        ours[last][0],
-        met[last],
-        terms,
     )
     grads.append(part)
 

time: 74.4 us -> 73.6 us (0.989)
  waiting for transfers between devices: 25.3 us -> 23.4 us
  starting transfers between devices: 22.7 us -> 24 us
    ppermute x22, waiting for transfers between devices: 25.3 us -> 23.4 us  [exchange(): return lax.ppermute(value, axis, [(i, i ^ bit) for i in range(size)])]
    ppermute x22, starting transfers between devices: 22.7 us -> 24 us  [exchange(): return lax.ppermute(value, axis, [(i, i ^ bit) for i in range(size)])]
  transfers between devices with their start and end apart: 22 -> 22, of which waited for: 8 -> 8; matrix products, arithmetic and copies ran while one was open for 0% -> 0% of each run, Pallas kernels for 21% -> 26%
where the time goes in v5:
time: 73.6 us; the launch traced here: 73.5 us
  Pallas kernels  24 us (33%)
  starting transfers between devices  24 us (33%)
  waiting for transfers between devices  23.4 us (32%)
  local copies, waits for them, and re-layouts  0.96 us (1%)
  between operations  0.83 us (1%)
    ppermute x22, starting transfers between devices, exchange(): return lax.ppermute(value, axis, [(i, i ^ bit) for i in range(size)])  24 us
    pallas_call x14, Pallas kernels, call(): pl.pallas_call(kernel, out_shape=outs, in_specs=[smem] * scalars + [vmem]...  24 us
    ppermute x22, waiting for transfers between devices, exchange(): return lax.ppermute(value, axis, [(i, i ^ bit) for i in range(size)])  23.4 us
  transfers between devices with their start and end apart: 22, of which 8 were waited for; matrix products, arithmetic and copies ran while one was open for 0% of the time, Pallas kernels for 26%

profile of v5, /device:TPU:0, one launch (start us, length us, event | category | flops | bytes accessed | tf_op | source)
XLA Modules:
  0.0 73.5 jit_solution(11098261614751288642)
XLA Ops:
  0.7 2.2 %shard_map.136 = (bf16[848,128]{1,0:T(8,128)(2,1)}, bf16[848,128]{1,0:T(8,128)(2,1)}, bf16[1040,128]{1,0:T(8,128)(2,1)}) custom-call(s32[1]{0:T(128)} %bitcast.me_ref, s32[1,4]{1,0:T(1,128)} %heights_ref.3, s32[1,4]{1,0:T(1,128)} %widths_ref.3, s32[1,4]{1,0:T(1,128)} %times_ref.1, bf16[128,640]{1,0:T(8,128)(2,1)} %features_ref.1, bf16[128,768]{1,0:T(8,128)(2,1)} %cotan_ref.1), custom_call_target="tpu_custom_call" | custom-call | flops 2000000000 | bytes 6000000 | tf_op jit(solution)/shard_map/pallas_call | solution.py:543
  2.9 0.5 collective-permute-start.2
  3.4 3.6 %collective-permute-start = (bf16[1040,128]{1,0:T(8,128)(2,1)}, bf16[1040,128]{1,0:T(8,128)(2,1)S(1)}, u32[]{:S(2)}, u32[]{:S(2)}) collective-permute-start(bf16[1040,128]{1,0:T(8,128)(2,1)} %get-tuple-element.77), channel_id=1, source_target_pairs={{0,4},{1,5},{2,6},{3,7},{4,0},{5,1},{6,2},{7,3},{8,12},{9,13},{10,... | collective-permute-start | bytes 798728 | tf_op jit(solution)/shard_map/ppermute | solution.py:562
  7.0 1.6 %collective-permute-start.1 = (bf16[848,128]{1,0:T(8,128)(2,1)}, bf16[848,128]{1,0:T(8,128)(2,1)S(1)}, u32[]{:S(2)}, u32[]{:S(2)}) collective-permute-start(bf16[848,128]{1,0:T(8,128)(2,1)} %get-tuple-element.78), channel_id=1, source_target_pairs={{0,2},{1,3},{2,0},{3,1},{4,6},{5,7},{6,4},{7,5},{8,10},{9,11},{10,... | collective-permute-start | bytes 651272 | tf_op jit(solution)/shard_map/ppermute | solution.py:562
  8.6 0.9 %copy-done.1 = bf16[848,128]{1,0:T(8,128)(2,1)S(1)} copy-done((bf16[848,128]{1,0:T(8,128)(2,1)S(1)}, bf16[848,128]{1,0:T(8,128)(2,1)}, u32[]{:S(2)}) %copy-start.1) | copy-done | bytes 217112
  9.5 4.6 %shard_map.137 = (bf16[736,128]{1,0:T(8,128)(2,1)S(1)}, bf16[768,128]{1,0:T(8,128)(2,1)S(1)}, f32[8,640]{1,0:T(8,128)S(1)}, bf16[864,256]{1,0:T(8,128)(2,1)S(1)}...) custom-call(s32[1]{0:T(128)} %bitcast.me_ref, ...), custom_call_target="tpu_custom_call" | custom-call | flops 1000000000 | bytes 3000000 | tf_op jit(solution)/shard_map/pallas_call | solution.py:543
  14.1 4.2 %collective-permute-done.1.near_ref = bf16[848,128]{1,0:T(8,128)(2,1)S(1)} collective-permute-done((bf16[848,128]{1,0:T(8,128)(2,1)}, bf16[848,128]{1,0:T(8,128)(2,1)S(1)}, u32[]{:S(2)}, u32[]{:S(2)}) %collective-permute-start.1) | collective-permute-done | bytes 217120 | tf_op jit(solution)/shard_map/ppermute | solution.py:562
  18.3 1.6 %collective-permute-done.near_ref = bf16[1040,128]{1,0:T(8,128)(2,1)S(1)} collective-permute-done((bf16[1040,128]{1,0:T(8,128)(2,1)}, bf16[1040,128]{1,0:T(8,128)(2,1)S(1)}, u32[]{:S(2)}, u32[]{:S(2)}) %collective-permute-start) | collective-permute-done | bytes 266272 | tf_op jit(solution)/shard_map/ppermute | solution.py:562
  19.9 0.0 collective-permute-start.4
  19.9 1.2 %collective-permute-start.3 = (bf16[1040,128]{1,0:T(8,128)(2,1)S(1)}, bf16[1040,128]{1,0:T(8,128)(2,1)S(1)}, u32[]{:S(2)}, u32[]{:S(2)}) collective-permute-start(bf16[1040,128]{1,0:T(8,128)(2,1)S(1)} %collective-permute-done.near_ref), channel_id=1, source_target_pairs={{0,2},{1,3},{2,0},{3,1},{4,6},{5,7},{6,4},{7,5},{8,10},{9,11},{10,... | collective-permute-start | bytes 798728 | tf_op jit(solution)/shard_map/ppermute | solution.py:562
  21.2 3.7 %shard_map.138 = (bf16[736,128]{1,0:T(8,128)(2,1)S(1)}, bf16[768,128]{1,0:T(8,128)(2,1)S(1)}, f32[8,640]{1,0:T(8,128)S(1)}, bf16[864,256]{1,0:T(8,128)(2,1)S(1)}...) custom-call(s32[1]{0:T(128)} %bitcast.me_ref, ...), custom_call_target="tpu_custom_call" | custom-call | flops 1000000000 | bytes 3000000 | tf_op jit(solution)/shard_map/pallas_call | solution.py:543
  24.9 3.7 %shard_map.139 = (bf16[736,128]{1,0:T(8,128)(2,1)S(1)}, bf16[768,128]{1,0:T(8,128)(2,1)S(1)}, f32[8,640]{1,0:T(8,128)S(1)}, bf16[864,256]{1,0:T(8,128)(2,1)S(1)}...) custom-call(s32[1]{0:T(128)} %bitcast.me_ref, ...), custom_call_target="tpu_custom_call" | custom-call | flops 1000000000 | bytes 3000000 | tf_op jit(solution)/shard_map/pallas_call | solution.py:543
  28.5 0.2 collective-permute-done.3.near_ref
  28.8 0.0 collective-permute-start.6
  28.8 0.5 collective-permute-start.7
  29.3 0.0 collective-permute-start.8
  29.3 1.2 %shard_map.140.early_ref = f32[864,640]{1,0:T(8,128)S(1)} custom-call(bf16[864,256]{1,0:T(8,128)(2,1)S(1)} %get-tuple-element.93.refs_0_, bf16[864,256]{1,0:T(8,128)(2,1)S(1)} %get-tuple-element.94.refs_1_, bf16[864,256]{1,0:T(8,128)(2,1)S(1)} %get-tuple-element.95.refs_2_, bf16[256,640]{1,0:T(8,128)(2,1)S(1)} %get-tuple-element.96.refs_3_, ...), custom_call_target="tpu_custom_call" | custom-call | flops 500000000 | bytes 1500000 | tf_op jit(solution)/shard_map/pallas_call | solution.py:543
  30.5 0.6 collective-permute-start.9
  31.0 0.0 collective-permute-done.6.far_ref
  31.0 3.8 %shard_map.141 = (bf16[736,128]{1,0:T(8,128)(2,1)S(1)}, bf16[768,128]{1,0:T(8,128)(2,1)S(1)}, f32[8,640]{1,0:T(8,128)S(1)}, bf16[864,256]{1,0:T(8,128)(2,1)S(1)}...) custom-call(s32[1]{0:T(128)} %bitcast.me_ref, ...), custom_call_target="tpu_custom_call" | custom-call | flops 1000000000 | bytes 3000000 | tf_op jit(solution)/shard_map/pallas_call | solution.py:543
  34.9 0.1 collective-permute-start.10
  35.0 0.0 collective-permute-done.8.met_ref
  35.1 0.0 collective-permute-done.9.met_ref
  35.1 1.2 %collective-permute-done.10.met_ref = bf16[768,128]{1,0:T(8,128)(2,1)S(1)} collective-permute-done((bf16[768,128]{1,0:T(8,128)(2,1)S(1)}, bf16[768,128]{1,0:T(8,128)(2,1)S(1)}, u32[]{:S(2)}, u32[]{:S(2)}) %collective-permute-start.10) | collective-permute-done | bytes 196640 | tf_op jit(solution)/shard_map/ppermute | solution.py:562
  36.4 0.1 shard_map.145
  36.5 0.6 shard_map.146
  37.0 1.6 %collective-permute-start.12 = (bf16[96,3200]{1,0:T(8,128)(2,1)S(1)}, bf16[96,3200]{1,0:T(8,128)(2,1)S(1)}, u32[]{:S(2)}, u32[]{:S(2)}) collective-permute-start(bf16[96,3200]{1,0:T(8,128)(2,1)S(1)} %get-tuple-element.127), channel_id=1, source_target_pairs={{0,16},{8,24},{16,0},{24,8},{1,17},{9,25},{17,1},{25,9},{2,18},{10... | collective-permute-start | bytes 1843208 | tf_op jit(solution)/shard_map/ppermute | solution.py:562
  38.7 1.5 %collective-permute-start.11 = (bf16[96,2944]{1,0:T(8,128)(2,1)S(1)}, bf16[96,2944]{1,0:T(8,128)(2,1)S(1)}, u32[]{:S(2)}, u32[]{:S(2)}) collective-permute-start(bf16[96,2944]{1,0:T(8,128)(2,1)S(1)} %get-tuple-element.126), channel_id=1, source_target_pairs={{0,8},{8,0},{16,24},{24,16},{1,9},{9,1},{17,25},{25,17},{2,10},{10... | collective-permute-start | bytes 1695752 | tf_op jit(solution)/shard_map/ppermute | solution.py:562
  40.2 3.5 %collective-permute-start.14 = (bf16[864,128]{1,0:T(8,128)(2,1)S(1)}, bf16[864,128]{1,0:T(8,128)(2,1)S(1)}, u32[]{:S(2)}, u32[]{:S(2)}) collective-permute-start(bf16[864,128]{1,0:T(8,128)(2,1)S(1)} %get-tuple-element.131), channel_id=1, source_target_pairs={{0,6},{1,7},{2,4},{3,5},{4,2},{5,3},{6,0},{7,1},{8,14},{9,15},{10,... | collective-permute-start | bytes 663560 | tf_op jit(solution)/shard_map/ppermute | solution.py:562
  43.7 0.0 collective-permute-start.13
  43.7 9.9 %collective-permute-done.13.refs_1_ = bf16[832,128]{1,0:T(8,128)(2,1)S(1)} collective-permute-done((bf16[832,128]{1,0:T(8,128)(2,1)S(1)}, bf16[832,128]{1,0:T(8,128)(2,1)S(1)}, u32[]{:S(2)}, u32[]{:S(2)}) %collective-permute-start.13) | collective-permute-done | bytes 213024 | tf_op jit(solution)/shard_map/ppermute | solution.py:562
  53.5 0.0 collective-permute-done.14.refs_3_.met_ref
  53.6 0.2 add_convert_fusion.high_ref
  53.7 0.0 copy-start.5
  53.7 0.0 copy-start.6
  53.7 1.2 %collective-permute-start.17 = (bf16[96,3200]{1,0:T(8,128)(2,1)S(1)}, bf16[96,3200]{1,0:T(8,128)(2,1)S(1)}, u32[]{:S(2)}, u32[]{:S(2)}) collective-permute-start(bf16[96,3200]{1,0:T(8,128)(2,1)S(1)} %add_convert_fusion.high_ref), channel_id=1, source_target_pairs={{0,8},{8,0},{16,24},{24,16},{1,9},{9,1},{17,25},{25,17},{2,10},{10... | collective-permute-start | bytes 1843208 | tf_op jit(solution)/shard_map/ppermute | solution.py:562
  55.0 0.1 add_convert_fusion.1.low_ref
  55.1 1.4 %collective-permute-start.16 = (bf16[96,2944]{1,0:T(8,128)(2,1)S(1)}, bf16[96,2944]{1,0:T(8,128)(2,1)S(1)}, u32[]{:S(2)}, u32[]{:S(2)}) collective-permute-start(bf16[96,2944]{1,0:T(8,128)(2,1)S(1)} %add_convert_fusion.1.low_ref), channel_id=1, source_target_pairs={{0,16},{8,24},{16,0},{24,8},{1,17},{9,25},{17,1},{25,9},{2,18},{10... | collective-permute-start | bytes 1695752 | tf_op jit(solution)/shard_map/ppermute | solution.py:562
  56.5 2.7 %collective-permute-start.15 = (bf16[832,128]{1,0:T(8,128)(2,1)S(1)}, bf16[832,128]{1,0:T(8,128)(2,1)S(1)}, u32[]{:S(2)}, u32[]{:S(2)}) collective-permute-start(bf16[832,128]{1,0:T(8,128)(2,1)S(1)} %shard_map.144), channel_id=1, source_target_pairs={{0,4},{1,5},{2,6},{3,7},{4,0},{5,1},{6,2},{7,3},{8,12},{9,13},{10,... | collective-permute-start | bytes 638984 | tf_op jit(solution)/shard_map/ppermute | solution.py:562
  59.3 1.4 %collective-permute-start.18 = (f32[8,640]{1,0:T(8,128)S(1)}, f32[8,640]{1,0:T(8,128)S(1)}, u32[]{:S(2)}, u32[]{:S(2)}) collective-permute-start(f32[8,640]{1,0:T(8,128)S(1)} %shard_map.148), channel_id=1, source_target_pairs={{0,2},{1,3},{2,0},{3,1},{4,6},{5,7},{6,4},{7,5},{8,10},{9,11},{10,... | collective-permute-start | bytes 61448 | tf_op jit(solution)/shard_map/ppermute | solution.py:562
  60.7 2.5 %collective-permute-done.18 = f32[8,640]{1,0:T(8,128)S(1)} collective-permute-done((f32[8,640]{1,0:T(8,128)S(1)}, f32[8,640]{1,0:T(8,128)S(1)}, u32[]{:S(2)}, u32[]{:S(2)}) %collective-permute-start.18) | collective-permute-done | bytes 20512 | tf_op jit(solution)/shard_map/ppermute | solution.py:562
  63.2 0.6 collective-permute-start.21
  63.8 1.4 %collective-permute-start.20 = (f32[8,640]{1,0:T(8,128)S(1)}, f32[8,640]{1,0:T(8,128)S(1)}, u32[]{:S(2)}, u32[]{:S(2)}) collective-permute-start(f32[8,640]{1,0:T(8,128)S(1)} %add.11.refs_0_), channel_id=1, source_target_pairs={{0,16},{8,24},{16,0},{24,8},{1,17},{9,25},{17,1},{25,9},{2,18},{10... | collective-permute-start | bytes 61448 | tf_op jit(solution)/shard_map/ppermute | solution.py:562
  65.2 2.8 %collective-permute-done.15.refs_2_ = bf16[832,128]{1,0:T(8,128)(2,1)S(1)} collective-permute-done((bf16[832,128]{1,0:T(8,128)(2,1)S(1)}, bf16[832,128]{1,0:T(8,128)(2,1)S(1)}, u32[]{:S(2)}, u32[]{:S(2)}) %collective-permute-start.15) | collective-permute-done | bytes 213024 | tf_op jit(solution)/shard_map/ppermute | solution.py:562
  68.0 0.6 collective-permute-start.19
  68.6 2.3 %shard_map.147 = (bf16[128,768]{1,0:T(8,128)(2,1)}, bf16[128,640]{1,0:T(8,128)(2,1)}) custom-call(s32[1]{0:T(128)} %bitcast.me_ref, s32[1,4]{1,0:T(1,128)S(1)} %copy-done.5, s32[1,4]{1,0:T(1,128)S(1)} %copy-done.6, f32[832,128]{1,0:T(8,128)S(1)} %shard_map.142.refs_0_, bf16[832,128]{1,0:T(8,128)(2,1)S(1)} %collective-permute-done.13.refs_1_, ...), custom_call_target="tpu_custom_call" | custom-call | flops 1250000000 | bytes 3750000 | tf_op jit(solution)/shard_map/pallas_call | solution.py:543
  71.0 0.8 %collective-permute-done.19.refs_1_ = f32[8,640]{1,0:T(8,128)S(1)} collective-permute-done((f32[8,640]{1,0:T(8,128)S(1)}, f32[8,640]{1,0:T(8,128)S(1)}, u32[]{:S(2)}, u32[]{:S(2)}) %collective-permute-start.19) | collective-permute-done | bytes 20512 | tf_op jit(solution)/shard_map/ppermute | solution.py:562
  71.8 1.7 %shard_map.149 = (f32[96,5760]{1,0:T(8,128)}, f32[96,320]{1,0:T(8,128)}, f32[640]{0:T(1024)}, f32[640]{0:T(1024)}) custom-call(bf16[96,2944]{1,0:T(8,128)(2,1)S(1)} %add_convert_fusion.1.low_ref, bf16[96,2944]{1,0:T(8,128)(2,1)S(1)} %collective-permute-done.16.low_met_ref, bf16[96,3200]{1,0:T(8,128)(2,1)S(1)} %add_convert_fusion.high_ref, ...), custom_call_target="tpu_custom_call" | custom-call | flops 750000000 | bytes 2250000 | tf_op jit(solution)/shard_map/pallas_call | solution.py:543
  (27 shorter events, 0.2 us)
Async XLA Ops:
  0.6 7.9 %copy-start = (bf16[96,5760]{1,0:T(8,128)(2,1)S(1)}, bf16[96,5760]{1,0:T(8,128)(2,1)}, u32[]{:S(2)}) copy-start(bf16[96,5760]{1,0:T(8,128)(2,1)} %refs_0_.1) | copy-start | bytes 3317764
  0.6 7.9 %copy-start.2 = (bf16[96,320]{1,0:T(8,128)(2,1)S(1)}, bf16[96,320]{1,0:T(8,128)(2,1)}, u32[]{:S(2)}) copy-start(bf16[96,320]{1,0:T(8,128)(2,1)} %refs_1_.1) | copy-start | bytes 184324
  0.7 7.9 %copy-start.3 = (f32[640]{0:T(1024)S(1)}, f32[640]{0:T(1024)}, u32[]{:S(2)}) copy-start(f32[640]{0:T(1024)} %refs_6_.1) | copy-start | bytes 7684
  0.7 7.9 %copy-start.4 = (f32[640]{0:T(1024)S(1)}, f32[640]{0:T(1024)}, u32[]{:S(2)}) copy-start(f32[640]{0:T(1024)} %refs_7_.1) | copy-start | bytes 7684
  2.9 5.6 %collective-permute-start.2 = (bf16[848,128]{1,0:T(8,128)(2,1)}, bf16[848,128]{1,0:T(8,128)(2,1)S(1)}, u32[]{:S(2)}, u32[]{:S(2)}) collective-permute-start(bf16[848,128]{1,0:T(8,128)(2,1)} %get-tuple-element.79.near_ref), channel_id=1, source_target_pairs={{0,1},{1,0},{2,3},{3,2},{4,5},{5,4},{6,7},{7,6},{8,9},{9,8},{10,11... | collective-permute-start | bytes 651272 | tf_op jit(solution)/shard_map/ppermute | solution.py:562
  3.4 16.6 %collective-permute-start = (bf16[1040,128]{1,0:T(8,128)(2,1)}, bf16[1040,128]{1,0:T(8,128)(2,1)S(1)}, u32[]{:S(2)}, u32[]{:S(2)}) collective-permute-start(bf16[1040,128]{1,0:T(8,128)(2,1)} %get-tuple-element.77), channel_id=1, source_target_pairs={{0,4},{1,5},{2,6},{3,7},{4,0},{5,1},{6,2},{7,3},{8,12},{9,13},{10,... | collective-permute-start | bytes 798728 | tf_op jit(solution)/shard_map/ppermute | solution.py:562
  7.0 11.3 %collective-permute-start.1 = (bf16[848,128]{1,0:T(8,128)(2,1)}, bf16[848,128]{1,0:T(8,128)(2,1)S(1)}, u32[]{:S(2)}, u32[]{:S(2)}) collective-permute-start(bf16[848,128]{1,0:T(8,128)(2,1)} %get-tuple-element.78), channel_id=1, source_target_pairs={{0,2},{1,3},{2,0},{3,1},{4,6},{5,7},{6,4},{7,5},{8,10},{9,11},{10,... | collective-permute-start | bytes 651272 | tf_op jit(solution)/shard_map/ppermute | solution.py:562
  8.6 0.9 %copy-start.1 = (bf16[848,128]{1,0:T(8,128)(2,1)S(1)}, bf16[848,128]{1,0:T(8,128)(2,1)}, u32[]{:S(2)}) copy-start(bf16[848,128]{1,0:T(8,128)(2,1)} %get-tuple-element.79.near_ref) | copy-start | bytes 651268
  18.3 2.9 %collective-permute-start.5 = (bf16[848,128]{1,0:T(8,128)(2,1)S(1)}, bf16[848,128]{1,0:T(8,128)(2,1)S(1)}, u32[]{:S(2)}, u32[]{:S(2)}) collective-permute-start(bf16[848,128]{1,0:T(8,128)(2,1)S(1)} %collective-permute-done.1.near_ref), channel_id=1, source_target_pairs={{0,1},{1,0},{2,3},{3,2},{4,5},{5,4},{6,7},{7,6},{8,9},{9,8},{10,11... | collective-permute-start | bytes 651272 | tf_op jit(solution)/shard_map/ppermute | solution.py:562
  19.9 4.9 %collective-permute-start.4 = (bf16[1040,128]{1,0:T(8,128)(2,1)S(1)}, bf16[1040,128]{1,0:T(8,128)(2,1)S(1)}, u32[]{:S(2)}, u32[]{:S(2)}) collective-permute-start(bf16[1040,128]{1,0:T(8,128)(2,1)S(1)} %collective-permute-done.near_ref), channel_id=1, source_target_pairs={{0,1},{1,0},{2,3},{3,2},{4,5},{5,4},{6,7},{7,6},{8,9},{9,8},{10,11... | collective-permute-start | bytes 798728 | tf_op jit(solution)/shard_map/ppermute | solution.py:562
  19.9 8.8 %collective-permute-start.3 = (bf16[1040,128]{1,0:T(8,128)(2,1)S(1)}, bf16[1040,128]{1,0:T(8,128)(2,1)S(1)}, u32[]{:S(2)}, u32[]{:S(2)}) collective-permute-start(bf16[1040,128]{1,0:T(8,128)(2,1)S(1)} %collective-permute-done.near_ref), channel_id=1, source_target_pairs={{0,2},{1,3},{2,0},{3,1},{4,6},{5,7},{6,4},{7,5},{8,10},{9,11},{10,... | collective-permute-start | bytes 798728 | tf_op jit(solution)/shard_map/ppermute | solution.py:562
  28.8 2.3 %collective-permute-start.6 = (bf16[1040,128]{1,0:T(8,128)(2,1)S(1)}, bf16[1040,128]{1,0:T(8,128)(2,1)S(1)}, u32[]{:S(2)}, u32[]{:S(2)}) collective-permute-start(bf16[1040,128]{1,0:T(8,128)(2,1)S(1)} %collective-permute-done.3.near_ref), channel_id=1, source_target_pairs={{0,1},{1,0},{2,3},{3,2},{4,5},{5,4},{6,7},{7,6},{8,9},{9,8},{10,11... | collective-permute-start | bytes 798728 | tf_op jit(solution)/shard_map/ppermute | solution.py:562
  28.8 6.2 %collective-permute-start.7 = (bf16[768,128]{1,0:T(8,128)(2,1)S(1)}, bf16[768,128]{1,0:T(8,128)(2,1)S(1)}, u32[]{:S(2)}, u32[]{:S(2)}) collective-permute-start(bf16[768,128]{1,0:T(8,128)(2,1)S(1)} %get-tuple-element.110), channel_id=1, source_target_pairs={{0,1},{1,0},{2,3},{3,2},{4,5},{5,4},{6,7},{7,6},{8,9},{9,8},{10,11... | collective-permute-start | bytes 589832 | tf_op jit(solution)/shard_map/ppermute | solution.py:562
  29.3 5.8 %collective-permute-start.8 = (bf16[768,128]{1,0:T(8,128)(2,1)S(1)}, bf16[768,128]{1,0:T(8,128)(2,1)S(1)}, u32[]{:S(2)}, u32[]{:S(2)}) collective-permute-start(bf16[768,128]{1,0:T(8,128)(2,1)S(1)} %get-tuple-element.112), channel_id=1, source_target_pairs={{0,1},{1,0},{2,3},{3,2},{4,5},{5,4},{6,7},{7,6},{8,9},{9,8},{10,11... | collective-permute-start | bytes 589832 | tf_op jit(solution)/shard_map/ppermute | solution.py:562
  30.5 4.6 %collective-permute-start.9 = (bf16[768,128]{1,0:T(8,128)(2,1)S(1)}, bf16[768,128]{1,0:T(8,128)(2,1)S(1)}, u32[]{:S(2)}, u32[]{:S(2)}) collective-permute-start(bf16[768,128]{1,0:T(8,128)(2,1)S(1)} %get-tuple-element.114), channel_id=1, source_target_pairs={{0,1},{1,0},{2,3},{3,2},{4,5},{5,4},{6,7},{7,6},{8,9},{9,8},{10,11... | collective-permute-start | bytes 589832 | tf_op jit(solution)/shard_map/ppermute | solution.py:562
  34.9 1.5 %collective-permute-start.10 = (bf16[768,128]{1,0:T(8,128)(2,1)S(1)}, bf16[768,128]{1,0:T(8,128)(2,1)S(1)}, u32[]{:S(2)}, u32[]{:S(2)}) collective-permute-start(bf16[768,128]{1,0:T(8,128)(2,1)S(1)} %get-tuple-element.117), channel_id=1, source_target_pairs={{0,1},{1,0},{2,3},{3,2},{4,5},{5,4},{6,7},{7,6},{8,9},{9,8},{10,11... | collective-permute-start | bytes 589832 | tf_op jit(solution)/shard_map/ppermute | solution.py:562
  37.0 16.5 %collective-permute-start.12 = (bf16[96,3200]{1,0:T(8,128)(2,1)S(1)}, bf16[96,3200]{1,0:T(8,128)(2,1)S(1)}, u32[]{:S(2)}, u32[]{:S(2)}) collective-permute-start(bf16[96,3200]{1,0:T(8,128)(2,1)S(1)} %get-tuple-element.127), channel_id=1, source_target_pairs={{0,16},{8,24},{16,0},{24,8},{1,17},{9,25},{17,1},{25,9},{2,18},{10... | collective-permute-start | bytes 1843208 | tf_op jit(solution)/shard_map/ppermute | solution.py:562
  38.7 14.9 %collective-permute-start.11 = (bf16[96,2944]{1,0:T(8,128)(2,1)S(1)}, bf16[96,2944]{1,0:T(8,128)(2,1)S(1)}, u32[]{:S(2)}, u32[]{:S(2)}) collective-permute-start(bf16[96,2944]{1,0:T(8,128)(2,1)S(1)} %get-tuple-element.126), channel_id=1, source_target_pairs={{0,8},{8,0},{16,24},{24,16},{1,9},{9,1},{17,25},{25,17},{2,10},{10... | collective-permute-start | bytes 1695752 | tf_op jit(solution)/shard_map/ppermute | solution.py:562
  40.2 13.4 %collective-permute-start.14 = (bf16[864,128]{1,0:T(8,128)(2,1)S(1)}, bf16[864,128]{1,0:T(8,128)(2,1)S(1)}, u32[]{:S(2)}, u32[]{:S(2)}) collective-permute-start(bf16[864,128]{1,0:T(8,128)(2,1)S(1)} %get-tuple-element.131), channel_id=1, source_target_pairs={{0,6},{1,7},{2,4},{3,5},{4,2},{5,3},{6,0},{7,1},{8,14},{9,15},{10,... | collective-permute-start | bytes 663560 | tf_op jit(solution)/shard_map/ppermute | solution.py:562
  43.7 9.9 %collective-permute-start.13 = (bf16[832,128]{1,0:T(8,128)(2,1)S(1)}, bf16[832,128]{1,0:T(8,128)(2,1)S(1)}, u32[]{:S(2)}, u32[]{:S(2)}) collective-permute-start(bf16[832,128]{1,0:T(8,128)(2,1)S(1)} %shard_map.143), channel_id=1, source_target_pairs={{0,2},{1,3},{2,0},{3,1},{4,6},{5,7},{6,4},{7,5},{8,10},{9,11},{10,... | collective-permute-start | bytes 638984 | tf_op jit(solution)/shard_map/ppermute | solution.py:562
  53.7 14.9 %copy-start.5 = (s32[1,4]{1,0:T(1,128)S(1)}, s32[1,4]{1,0:T(1,128)}, u32[]{:S(2)}) copy-start(s32[1,4]{1,0:T(1,128)} %heights_ref.3) | copy-start | bytes 52
  53.7 14.9 %copy-start.6 = (s32[1,4]{1,0:T(1,128)S(1)}, s32[1,4]{1,0:T(1,128)}, u32[]{:S(2)}) copy-start(s32[1,4]{1,0:T(1,128)} %widths_ref.3) | copy-start | bytes 52
  53.7 18.1 %collective-permute-start.17 = (bf16[96,3200]{1,0:T(8,128)(2,1)S(1)}, bf16[96,3200]{1,0:T(8,128)(2,1)S(1)}, u32[]{:S(2)}, u32[]{:S(2)}) collective-permute-start(bf16[96,3200]{1,0:T(8,128)(2,1)S(1)} %add_convert_fusion.high_ref), channel_id=1, source_target_pairs={{0,8},{8,0},{16,24},{24,16},{1,9},{9,1},{17,25},{25,17},{2,10},{10... | collective-permute-start | bytes 1843208 | tf_op jit(solution)/shard_map/ppermute | solution.py:562
  55.1 16.7 %collective-permute-start.16 = (bf16[96,2944]{1,0:T(8,128)(2,1)S(1)}, bf16[96,2944]{1,0:T(8,128)(2,1)S(1)}, u32[]{:S(2)}, u32[]{:S(2)}) collective-permute-start(bf16[96,2944]{1,0:T(8,128)(2,1)S(1)} %add_convert_fusion.1.low_ref), channel_id=1, source_target_pairs={{0,16},{8,24},{16,0},{24,8},{1,17},{9,25},{17,1},{25,9},{2,18},{10... | collective-permute-start | bytes 1695752 | tf_op jit(solution)/shard_map/ppermute | solution.py:562
  56.5 11.5 %collective-permute-start.15 = (bf16[832,128]{1,0:T(8,128)(2,1)S(1)}, bf16[832,128]{1,0:T(8,128)(2,1)S(1)}, u32[]{:S(2)}, u32[]{:S(2)}) collective-permute-start(bf16[832,128]{1,0:T(8,128)(2,1)S(1)} %shard_map.144), channel_id=1, source_target_pairs={{0,4},{1,5},{2,6},{3,7},{4,0},{5,1},{6,2},{7,3},{8,12},{9,13},{10,... | collective-permute-start | bytes 638984 | tf_op jit(solution)/shard_map/ppermute | solution.py:562
  59.3 3.9 %collective-permute-start.18 = (f32[8,640]{1,0:T(8,128)S(1)}, f32[8,640]{1,0:T(8,128)S(1)}, u32[]{:S(2)}, u32[]{:S(2)}) collective-permute-start(f32[8,640]{1,0:T(8,128)S(1)} %shard_map.148), channel_id=1, source_target_pairs={{0,2},{1,3},{2,0},{3,1},{4,6},{5,7},{6,4},{7,5},{8,10},{9,11},{10,... | collective-permute-start | bytes 61448 | tf_op jit(solution)/shard_map/ppermute | solution.py:562
  63.2 7.8 %collective-permute-start.21 = (f32[8,640]{1,0:T(8,128)S(1)}, f32[8,640]{1,0:T(8,128)S(1)}, u32[]{:S(2)}, u32[]{:S(2)}) collective-permute-start(f32[8,640]{1,0:T(8,128)S(1)} %add.11.refs_0_), channel_id=1, source_target_pairs={{0,24},{8,16},{16,8},{24,0},{1,25},{9,17},{17,9},{25,1},{2,26},{10... | collective-permute-start | bytes 61448 | tf_op jit(solution)/shard_map/ppermute | solution.py:562
  63.8 7.2 %collective-permute-start.20 = (f32[8,640]{1,0:T(8,128)S(1)}, f32[8,640]{1,0:T(8,128)S(1)}, u32[]{:S(2)}, u32[]{:S(2)}) collective-permute-start(f32[8,640]{1,0:T(8,128)S(1)} %add.11.refs_0_), channel_id=1, source_target_pairs={{0,16},{8,24},{16,0},{24,8},{1,17},{9,25},{17,1},{25,9},{2,18},{10... | collective-permute-start | bytes 61448 | tf_op jit(solution)/shard_map/ppermute | solution.py:562
  68.0 3.8 %collective-permute-start.19 = (f32[8,640]{1,0:T(8,128)S(1)}, f32[8,640]{1,0:T(8,128)S(1)}, u32[]{:S(2)}, u32[]{:S(2)}) collective-permute-start(f32[8,640]{1,0:T(8,128)S(1)} %add.11.refs_0_), channel_id=1, source_target_pairs={{0,8},{8,0},{16,24},{24,16},{1,9},{9,1},{17,25},{25,17},{2,10},{10... | collective-permute-start | bytes 61448 | tf_op jit(solution)/shard_map/ppermute | solution.py:562
